TPU v7x, 32 devices: a whole 2x2x4 slice. The times are simulated.
32 devices in a mesh: batch: 16 (over z, y, core), seq: 2 (over x).
Axes of the slice: x: 2, y: 2, z: 4, core: 2. Of those that a mesh axis runs over, the one named last changes fastest.
Arguments:
- hidden_in: bfloat16 [32, 256, 512], P('batch', 'seq'), may hold values from -6 to 6
- memory: bfloat16 [32, 512, 512], P('batch', 'seq'), may hold values from -6 to 6
- target_lengths: int32 [32], P('batch'), may hold values from 76 to 230, as said below
- source_mask: int32 [32, 512], P('batch'), may hold values 0 or 1
- grad_out: bfloat16 [32, 256, 512], P('batch', 'seq'), may hold values from -6 to 6
- attn_qkv: bfloat16 [512, 1536], P(('batch', 'seq')), may hold values from -0.25 to 0.25
- attn_out: bfloat16 [512, 512], P(('batch', 'seq')), may hold values from -1 to 1
- cross_q: bfloat16 [512, 512], P(('batch', 'seq')), may hold values from -0.25 to 0.25
- cross_kv: bfloat16 [512, 1024], P(('batch', 'seq')), may hold values from -0.25 to 0.25
- cross_out: bfloat16 [512, 512], P(('batch', 'seq')), may hold values from -1 to 1
- ffn_up: bfloat16 [512, 2048], P(('batch', 'seq')), may hold values from -0.25 to 0.25
- ffn_down: bfloat16 [2048, 512], P(('batch', 'seq')), may hold values from -0.125 to 0.125
- gains: bfloat16 [512, 3], P(('batch', 'seq')), may hold values from 0.5 to 1.5
- biases: bfloat16 [512, 10], P(('batch', 'seq')), may hold values from -1.796875 to 1.796875
- ffn_bias: bfloat16 [2048], P(('batch', 'seq')), may hold values from -1.796875 to 1.796875
Outputs:
- output: bfloat16 [32, 256, 512], P('batch', 'seq')
- grad_hidden_in: float32 [32, 256, 512], P('batch', 'seq')
- grad_memory: float32 [32, 512, 512], P('batch', 'seq')
- grad_attn_qkv: float32 [512, 1536], P(('batch', 'seq'))
- grad_attn_out: float32 [512, 512], P(('batch', 'seq'))
- grad_cross_q: float32 [512, 512], P(('batch', 'seq'))
- grad_cross_kv: float32 [512, 1024], P(('batch', 'seq'))
- grad_cross_out: float32 [512, 512], P(('batch', 'seq'))
- grad_ffn_up: float32 [512, 2048], P(('batch', 'seq'))
- grad_ffn_down: float32 [2048, 512], P(('batch', 'seq'))
- grad_gains: float32 [512, 3], P(('batch', 'seq'))
- grad_biases: float32 [512, 10], P(('batch', 'seq'))
- grad_ffn_bias: float32 [2048], P(('batch', 'seq'))
Inputs may be any that keep to these rules, and one draw needn't show every extreme that they name: `target_lengths`: in each aligned block of 2 examples (one index of batch) some example has a target length above 128.
All inputs are finite; a program needn't handle non-finite values. No bound on the sum of `source_mask` on one device may be relied on, other than what follows from the above.
Results may differ from a plain program's by a relative error of at most 0.015.
Values may be sent and summed in bfloat16 or wider, within the bound.
No kernel may reach another device: no remote copies, remote signals or barrier semaphores. Data moves between devices by JAX's collectives and lax.ppermute only.
A program may use at most 128 MiB of HBM per device.

v0:
```python
import jax
import jax.numpy as jnp
from jax import lax
from jax.sharding import PartitionSpec as P

HEADS = 8
HEAD_DIM = 64


EPSILON = 1e-05
NEGATIVE = -1000000000.0


def layer_norm(values, gain, shift):
    centred = values - jnp.mean(values, axis=-1, keepdims=True)
    variance = jnp.mean(centred * centred, axis=-1, keepdims=True)
    return centred * lax.rsqrt(variance + EPSILON) * gain + shift


def dense(left, weight):
    return jnp.einsum("erd,df->erf", left, weight, preferred_element_type=jnp.float32)


def weight_grad(left, grad_rows):
    return jnp.einsum("erd,erf->df", left, grad_rows, preferred_element_type=jnp.float32)


def back_dense(grad_rows, weight):
    return jnp.einsum("erf,df->erd", grad_rows, weight, preferred_element_type=jnp.float32)


def column_sum(grad_rows):
    return jnp.sum(grad_rows.astype(jnp.float32), axis=(0, 1))


def split_heads(values):
    return values.reshape(values.shape[0], values.shape[1], HEADS, HEAD_DIM)


def attn_scores(queries, key_rows, visible):
    scores = jnp.einsum(
        "eqhc,ekhc->ehqk",
        split_heads(queries),
        split_heads(key_rows),
        preferred_element_type=jnp.float32,
    ) * HEAD_DIM ** (-0.5)
    return jnp.where(visible, scores, NEGATIVE)


def attend_forward(queries, key_rows, values, visible):
    scores = attn_scores(queries, key_rows, visible)
    row_max = jnp.max(scores, axis=-1, keepdims=True)
    exponent = jnp.exp(scores - row_max)
    row_total = jnp.sum(exponent, axis=-1, keepdims=True)
    attn_weights = (exponent / row_total).astype(jnp.bfloat16)
    mixed = jnp.einsum(
        "ehqk,ekhc->eqhc", attn_weights, split_heads(values), preferred_element_type=jnp.float32
    )
    return (mixed.reshape(queries.shape).astype(jnp.bfloat16), row_max + jnp.log(row_total))


def attend_backward(queries, key_rows, values, visible, log_total, grad_mixed):
    scores = attn_scores(queries, key_rows, visible)
    attn_weights = jnp.exp(scores - log_total)
    grad_heads = split_heads(grad_mixed)
    grad_weights = jnp.einsum(
        "eqhc,ekhc->ehqk", grad_heads, split_heads(values), preferred_element_type=jnp.float32
    )
    grad_values = jnp.einsum(
        "ehqk,eqhc->ekhc",
        attn_weights.astype(jnp.bfloat16),
        grad_heads,
        preferred_element_type=jnp.float32,
    )
    grad_scores = attn_weights * (
        grad_weights - jnp.sum(attn_weights * grad_weights, axis=-1, keepdims=True)
    )
    grad_low = grad_scores.astype(jnp.bfloat16)
    score_scale = HEAD_DIM ** (-0.5)
    grad_queries = (
        jnp.einsum(
            "ehqk,ekhc->eqhc", grad_low, split_heads(key_rows), preferred_element_type=jnp.float32
        )
        * score_scale
    )
    grad_keys = (
        jnp.einsum(
            "ehqk,eqhc->ekhc", grad_low, split_heads(queries), preferred_element_type=jnp.float32
        )
        * score_scale
    )
    return (
        grad_queries.reshape(queries.shape),
        grad_keys.reshape(key_rows.shape),
        grad_values.reshape(values.shape),
    )


def prepare(gathered):
    return gathered[:7] + (
        gathered[7].astype(jnp.float32),
        gathered[8].astype(jnp.float32),
        gathered[9].astype(jnp.float32),
    )


def per_device(
    hidden_in,
    memory,
    target_lengths,
    source_mask,
    grad_out,
    attn_qkv,
    attn_out,
    cross_q,
    cross_kv,
    cross_out,
    ffn_up,
    ffn_down,
    gains,
    biases,
    ffn_bias,
):
    gathered = (
        lax.all_gather(attn_qkv, ("batch", "seq"), axis=0, tiled=True),
        lax.all_gather(attn_out, ("batch", "seq"), axis=0, tiled=True),
        lax.all_gather(cross_q, ("batch", "seq"), axis=0, tiled=True),
        lax.all_gather(cross_kv, ("batch", "seq"), axis=0, tiled=True),
        lax.all_gather(cross_out, ("batch", "seq"), axis=0, tiled=True),
        lax.all_gather(ffn_up, ("batch", "seq"), axis=0, tiled=True),
        lax.all_gather(ffn_down, ("batch", "seq"), axis=0, tiled=True),
        lax.all_gather(gains, ("batch", "seq"), axis=0, tiled=True),
        lax.all_gather(biases, ("batch", "seq"), axis=0, tiled=True),
        lax.all_gather(ffn_bias, ("batch", "seq"), axis=0, tiled=True),
    )
    w_qkv, w_out, w_cq, w_ckv, w_co, w_up, w_down, gain_cols, bias_cols, bias_up = prepare(gathered)
    model_width = hidden_in.shape[2]
    seq_count = lax.axis_size("seq")
    seq_index = lax.axis_index("seq")
    tgt_rows = hidden_in.shape[1]
    query_pos = seq_index * tgt_rows + jnp.arange(tgt_rows)
    key_pos = jnp.arange(tgt_rows * seq_count)
    src_len = source_mask.shape[1]
    self_ok = (key_pos[None, None, None, :] <= query_pos[None, None, :, None]) & (
        key_pos[None, None, None, :] < target_lengths[:, None, None, None]
    )
    cross_ok = ((source_mask > 0) | (jnp.arange(src_len) == 0)[None, :])[:, None, None, :]
    hidden_float = hidden_in.astype(jnp.float32)
    normed1 = layer_norm(hidden_float, gain_cols[:, 0], bias_cols[:, 0]).astype(jnp.bfloat16)
    joined_proj = dense(normed1, w_qkv)
    queries = (joined_proj[..., :model_width] + bias_cols[:, 1]).astype(jnp.bfloat16)
    key_rows = joined_proj[..., model_width : 2 * model_width].astype(jnp.bfloat16)
    values = (joined_proj[..., 2 * model_width :] + bias_cols[:, 2]).astype(jnp.bfloat16)
    keys_all, values_all = (
        lax.all_gather(key_rows, "seq", axis=1, tiled=True),
        lax.all_gather(values, "seq", axis=1, tiled=True),
    )
    mixed1, log_total1 = attend_forward(queries, keys_all, values_all, self_ok)
    after_self = hidden_float + (dense(mixed1, w_out) + bias_cols[:, 3])
    normed2 = layer_norm(after_self, gain_cols[:, 1], bias_cols[:, 4]).astype(jnp.bfloat16)
    cross_queries = (dense(normed2, w_cq) + bias_cols[:, 5]).astype(jnp.bfloat16)
    memory_all = lax.all_gather(memory, "seq", axis=1, tiled=True)
    cross_proj = dense(memory_all, w_ckv)
    cross_keys_all = cross_proj[..., :model_width].astype(jnp.bfloat16)
    cross_values_all = (cross_proj[..., model_width:] + bias_cols[:, 6]).astype(jnp.bfloat16)
    mixed2, log_total2 = attend_forward(cross_queries, cross_keys_all, cross_values_all, cross_ok)
    after_cross = after_self + (dense(mixed2, w_co) + bias_cols[:, 7])
    normed3 = layer_norm(after_cross, gain_cols[:, 2], bias_cols[:, 8]).astype(jnp.bfloat16)
    hidden = dense(normed3, w_up) + bias_up
    active = jax.nn.gelu(hidden).astype(jnp.bfloat16)
    output = (after_cross + (dense(active, w_down) + bias_cols[:, 9])).astype(jnp.bfloat16)
    regathered = (
        lax.all_gather(attn_qkv, ("batch", "seq"), axis=0, tiled=True),
        lax.all_gather(attn_out, ("batch", "seq"), axis=0, tiled=True),
        lax.all_gather(cross_q, ("batch", "seq"), axis=0, tiled=True),
        lax.all_gather(cross_kv, ("batch", "seq"), axis=0, tiled=True),
        lax.all_gather(cross_out, ("batch", "seq"), axis=0, tiled=True),
        lax.all_gather(ffn_up, ("batch", "seq"), axis=0, tiled=True),
        lax.all_gather(ffn_down, ("batch", "seq"), axis=0, tiled=True),
        lax.all_gather(gains, ("batch", "seq"), axis=0, tiled=True),
        lax.all_gather(biases, ("batch", "seq"), axis=0, tiled=True),
        lax.all_gather(ffn_bias, ("batch", "seq"), axis=0, tiled=True),
    )
    w_qkv, w_out, w_cq, w_ckv, w_co, w_up, w_down, gain_cols, bias_cols, bias_up = prepare(
        regathered
    )
    d_down = weight_grad(active, grad_out)
    d_bias9 = column_sum(grad_out)
    grad_active = back_dense(grad_out, w_down)
    _, gelu_back = jax.vjp(jax.nn.gelu, hidden)
    grad_hidden = gelu_back(grad_active)[0].astype(jnp.bfloat16)
    d_up = weight_grad(normed3, grad_hidden)
    d_bias_up = column_sum(grad_hidden)
    _, norm3_back = jax.vjp(layer_norm, after_cross, gain_cols[:, 2], bias_cols[:, 8])
    part3, d_gain3, d_shift3 = norm3_back(back_dense(grad_hidden, w_up))
    grad_after_cross = grad_out.astype(jnp.float32) + part3
    grad_y2 = grad_after_cross.astype(jnp.bfloat16)
    d_co = weight_grad(mixed2, grad_y2)
    d_bias7 = column_sum(grad_y2)
    grad_mixed2 = back_dense(grad_y2, w_co).astype(jnp.bfloat16)
    grad_cq_f, grad_ck_all, grad_cv_all = attend_backward(
        cross_queries, cross_keys_all, cross_values_all, cross_ok, log_total2, grad_mixed2
    )
    grad_cq_rows = grad_cq_f.astype(jnp.bfloat16)
    grad_ck_sum, grad_cv_sum = (
        lax.psum_scatter(
            grad_ck_all.astype(jnp.bfloat16), "seq", scatter_dimension=1, tiled=True
        ).astype(jnp.float32),
        lax.psum_scatter(
            grad_cv_all.astype(jnp.bfloat16), "seq", scatter_dimension=1, tiled=True
        ).astype(jnp.float32),
    )
    grad_ck = grad_ck_sum.astype(jnp.bfloat16)
    grad_cv = grad_cv_sum.astype(jnp.bfloat16)
    d_ckv = jnp.concatenate([weight_grad(memory, grad_ck), weight_grad(memory, grad_cv)], axis=1)
    d_bias6 = column_sum(grad_cv)
    grad_memory = back_dense(grad_ck, w_ckv[:, :model_width]) + back_dense(
        grad_cv, w_ckv[:, model_width:]
    )
    d_cq = weight_grad(normed2, grad_cq_rows)
    d_bias5 = column_sum(grad_cq_rows)
    _, norm2_back = jax.vjp(layer_norm, after_self, gain_cols[:, 1], bias_cols[:, 4])
    part2, d_gain2, d_shift2 = norm2_back(back_dense(grad_cq_rows, w_cq))
    grad_after_self = grad_after_cross + part2
    grad_y1 = grad_after_self.astype(jnp.bfloat16)
    d_out = weight_grad(mixed1, grad_y1)
    d_bias3 = column_sum(grad_y1)
    grad_mixed1 = back_dense(grad_y1, w_out).astype(jnp.bfloat16)
    grad_q_f, grad_k_all, grad_v_all = attend_backward(
        queries, keys_all, values_all, self_ok, log_total1, grad_mixed1
    )
    grad_q = grad_q_f.astype(jnp.bfloat16)
    grad_k_sum, grad_v_sum = (
        lax.psum_scatter(
            grad_k_all.astype(jnp.bfloat16), "seq", scatter_dimension=1, tiled=True
        ).astype(jnp.float32),
        lax.psum_scatter(
            grad_v_all.astype(jnp.bfloat16), "seq", scatter_dimension=1, tiled=True
        ).astype(jnp.float32),
    )
    grad_k = grad_k_sum.astype(jnp.bfloat16)
    grad_v = grad_v_sum.astype(jnp.bfloat16)
    d_qkv = jnp.concatenate(
        [weight_grad(normed1, grad_q), weight_grad(normed1, grad_k), weight_grad(normed1, grad_v)],
        axis=1,
    )
    d_bias1 = column_sum(grad_q)
    d_bias2 = column_sum(grad_v)
    grad_normed1 = (
        back_dense(grad_q, w_qkv[:, :model_width])
        + back_dense(grad_k, w_qkv[:, model_width : 2 * model_width])
        + back_dense(grad_v, w_qkv[:, 2 * model_width :])
    )
    _, norm1_back = jax.vjp(layer_norm, hidden_float, gain_cols[:, 0], bias_cols[:, 0])
    part1, d_gain1, d_shift1 = norm1_back(grad_normed1)
    grad_input = grad_after_self + part1
    d_gains = jnp.stack([d_gain1, d_gain2, d_gain3], axis=1)
    d_biases = jnp.stack(
        [
            d_shift1,
            d_bias1,
            d_bias2,
            d_bias3,
            d_shift2,
            d_bias5,
            d_bias6,
            d_bias7,
            d_shift3,
            d_bias9,
        ],
        axis=1,
    )
    g_qkv, g_out, g_cq, g_ckv, g_co, g_up, g_down, g_gains, g_biases, g_bias_up = (
        lax.psum_scatter(d_qkv, ("batch", "seq"), scatter_dimension=0, tiled=True),
        lax.psum_scatter(d_out, ("batch", "seq"), scatter_dimension=0, tiled=True),
        lax.psum_scatter(d_cq, ("batch", "seq"), scatter_dimension=0, tiled=True),
        lax.psum_scatter(d_ckv, ("batch", "seq"), scatter_dimension=0, tiled=True),
        lax.psum_scatter(d_co, ("batch", "seq"), scatter_dimension=0, tiled=True),
        lax.psum_scatter(d_up, ("batch", "seq"), scatter_dimension=0, tiled=True),
        lax.psum_scatter(d_down, ("batch", "seq"), scatter_dimension=0, tiled=True),
        lax.psum_scatter(d_gains, ("batch", "seq"), scatter_dimension=0, tiled=True),
        lax.psum_scatter(d_biases, ("batch", "seq"), scatter_dimension=0, tiled=True),
        lax.psum_scatter(d_bias_up, ("batch", "seq"), scatter_dimension=0, tiled=True),
    )
    return (
        output,
        grad_input,
        grad_memory,
        g_qkv,
        g_out,
        g_cq,
        g_ckv,
        g_co,
        g_up,
        g_down,
        g_gains,
        g_biases,
        g_bias_up,
    )


def solution(mesh):
    return jax.shard_map(
        per_device,
        mesh=mesh,
        in_specs=(
            P("batch", "seq", None),
            P("batch", "seq", None),
            P("batch"),
            P("batch", None),
            P("batch", "seq", None),
            P(("batch", "seq"), None),
            P(("batch", "seq"), None),
            P(("batch", "seq"), None),
            P(("batch", "seq"), None),
            P(("batch", "seq"), None),
            P(("batch", "seq"), None),
            P(("batch", "seq"), None),
            P(("batch", "seq"), None),
            P(("batch", "seq"), None),
            P(("batch", "seq")),
        ),
        out_specs=(
            P("batch", "seq", None),
            P("batch", "seq", None),
            P("batch", "seq", None),
            P(("batch", "seq"), None),
            P(("batch", "seq"), None),
            P(("batch", "seq"), None),
            P(("batch", "seq"), None),
            P(("batch", "seq"), None),
            P(("batch", "seq"), None),
            P(("batch", "seq"), None),
            P(("batch", "seq"), None),
            P(("batch", "seq"), None),
            P(("batch", "seq")),
        ),
        check_vma=False,
    )
```

profile of v0, /device:TPU:0, one launch (start us, length us, event | category | flops | bytes accessed | tf_op | source)
XLA Modules:
  0.0 1754.2 jit_solution(1642458181159627239)
XLA Ops:
  10.7 71.1 %all_gather.48 = bf16[512,10]{1,0:T(8,128)(2,1)S(1)} all-gather(bf16[16,10]{1,0:T(8,128)(2,1)} %param.28), channel_id=1, replica_groups=mesh['batch'=16,'seq'=2] {'batch','seq'}, dimensions={0}, use_global_device_ids=true | all-gather | bytes 10560 | tf_op jit(solution)/shard_map/all_gather | solution.py:133
  83.2 63.4 %all-gather = bf16[32,16,3]{1,2,0:T(4,128)(2,1)S(1)} all-gather(bf16[1,16,3]{1,2,0:T(4,128)(2,1)S(1)} %bitcast.259), channel_id=1, replica_groups=mesh['batch'=16,'seq'=2] {'batch','seq'}, dimensions={0}, use_global_device_ids=true | all-gather | bytes 3168 | tf_op jit(solution)/shard_map/all_gather | solution.py:132
  147.5 74.0 %all_gather.52 = bf16[512,512]{1,0:T(8,128)(2,1)} all-gather(bf16[16,512]{1,0:T(8,128)(2,1)S(1)} %copy-done.48), channel_id=1, replica_groups=mesh['batch'=16,'seq'=2] {'batch','seq'}, dimensions={0}, use_global_device_ids=true | all-gather | bytes 540672 | tf_op jit(solution)/shard_map/all_gather | solution.py:126
  221.5 71.9 %all_gather.55 = bf16[512,512]{1,0:T(8,128)(2,1)} all-gather(bf16[16,512]{1,0:T(8,128)(2,1)S(1)} %copy-done.49), channel_id=1, replica_groups=mesh['batch'=16,'seq'=2] {'batch','seq'}, dimensions={0}, use_global_device_ids=true | all-gather | bytes 540672 | tf_op jit(solution)/shard_map/all_gather | solution.py:127
  293.5 73.6 %all_gather.56 = bf16[512,512]{1,0:T(8,128)(2,1)} all-gather(bf16[16,512]{1,0:T(8,128)(2,1)S(1)} %copy-done.50), channel_id=1, replica_groups=mesh['batch'=16,'seq'=2] {'batch','seq'}, dimensions={0}, use_global_device_ids=true | all-gather | bytes 540672 | tf_op jit(solution)/shard_map/all_gather | solution.py:129
  367.2 36.9 %all-reduce = bf16[2048]{0:T(1024)(128)(2,1)S(1)} all-reduce(bf16[2048]{0:T(1024)(128)(2,1)S(1)} %dynamic-update-slice), channel_id=1, replica_groups=mesh['batch'=16,'seq'=2] {'batch','seq'}, use_global_device_ids=true, to_apply=%add | all-reduce | flops 2048 | bytes 8192
  404.3 2.8 fusion.47
  412.4 7.9 all_gather.50
  421.5 7.2 all_gather.51
  439.7 3.7 convolution_add_fusion
  443.4 4.3 convert_reduce_fusion
  453.5 4.2 multiply_reduce_fusion
  478.7 4.5 fusion.27
  492.3 13.9 reduce-scatter.42.cloned.1.call-done
  523.7 5.1 reduce-scatter.28.cloned.1.call-done
  531.0 3.5 pad_maximum_fusion
  534.5 3.6 copy.147
  539.8 11.7 reduce-scatter.26.cloned.1.call-done
  554.5 2.9 copy.149
  558.7 2.8 convolution_bitcast_fusion.1
  562.4 4.5 convolution_bitcast_fusion
  566.9 39.5 %all-reduce.1 = f32[2048]{0:T(1024)S(1)} all-reduce(f32[2048]{0:T(1024)S(1)} %get-tuple-element.117), channel_id=15, replica_groups=mesh['batch'=16,'seq'=2] {'batch','seq'}, use_global_device_ids=true, to_apply=%region_45.46.clone | all-reduce | flops 2048 | bytes 16384
  607.0 3.8 fusion.41
  611.9 75.2 %reduce-scatter.48.cloned.1.call-done = f32[16,3]{1,0:T(8,128)} async-done(((f32[512,3]{1,0:T(8,128)}), f32[16,3]{1,0:T(8,128)}) %reduce-scatter.48.cloned.1.call-update) | async-done | bytes 208
  690.4 131.2 %reduce-scatter.30.cloned.1.call-done = f32[16,512]{1,0:T(8,128)} async-done(((f32[512,512]{1,0:T(8,128)}), f32[16,512]{1,0:T(8,128)}) %reduce-scatter.30.cloned.1.call-update) | async-done | bytes 32784 | tf_op jit(solution)/shard_map/reduce_scatter | solution.py:275
  821.6 133.7 %reduce-scatter.32.cloned.1.call-done = f32[16,512]{1,0:T(8,128)} async-done(((f32[512,512]{1,0:T(8,128)}), f32[16,512]{1,0:T(8,128)}) %reduce-scatter.32.cloned.1.call-update) | async-done | bytes 32784 | tf_op jit(solution)/shard_map/reduce_scatter | solution.py:276
  955.3 134.2 %reduce-scatter.34.cloned.1.call-done = f32[16,512]{1,0:T(8,128)} async-done(((f32[512,512]{1,0:T(8,128)}), f32[16,512]{1,0:T(8,128)}) %reduce-scatter.34.cloned.1.call-update) | async-done | bytes 32784 | tf_op jit(solution)/shard_map/reduce_scatter | solution.py:278
  1089.5 132.0 %reduce-scatter.50.cloned.1.call-done = f32[16,10]{1,0:T(8,128)} async-done(((f32[512,10]{1,0:T(8,128)}), f32[16,10]{1,0:T(8,128)}) %reduce-scatter.50.cloned.1.call-update) | async-done | bytes 656
  1221.5 104.2 %reduce-scatter.44.cloned.1.call-done = f32[16,1536]{1,0:T(8,128)} async-done(((f32[512,1536]{1,0:T(8,128)}), f32[16,1536]{1,0:T(8,128)}) %reduce-scatter.44.cloned.1.call-update) | async-done | bytes 98320
  1325.7 139.5 %reduce-scatter.46.cloned.1.call-done = f32[16,1024]{1,0:T(8,128)} async-done(((f32[512,1024]{1,0:T(8,128)}), f32[16,1024]{1,0:T(8,128)}) %reduce-scatter.46.cloned.1.call-update) | async-done | bytes 65552
  1465.2 140.7 %reduce-scatter.36.cloned.1.call-done = f32[16,2048]{1,0:T(8,128)} async-done(((f32[512,2048]{1,0:T(8,128)}), f32[16,2048]{1,0:T(8,128)}) %reduce-scatter.36.cloned.1.call-update) | async-done | bytes 131088 | tf_op jit(solution)/shard_map/reduce_scatter | solution.py:279
  1605.9 141.4 %reduce-scatter.38.cloned.1.call-done = f32[64,512]{1,0:T(8,128)} async-done(((f32[2048,512]{1,0:T(8,128)}), f32[64,512]{1,0:T(8,128)}) %reduce-scatter.38.cloned.1.call-update) | async-done | bytes 131088 | tf_op jit(solution)/shard_map/reduce_scatter | solution.py:280
  (257 shorter events, 90.0 us)
Async XLA Ops:
  7.2 76.1 %copy-start.52 = (bf16[16,3]{0,1:T(4,128)(2,1)S(1)}, bf16[16,3]{0,1:T(4,128)(2,1)}, u32[]{:S(2)}) copy-start(bf16[16,3]{0,1:T(4,128)(2,1)} %param.27) | copy-start | bytes 292
  7.2 139.8 %copy-start.2 = (bf16[2,128,512]{2,1,0:T(8,128)(2,1)S(1)}, bf16[2,128,512]{2,1,0:T(8,128)(2,1)}, u32[]{:S(2)}) copy-start(bf16[2,128,512]{2,1,0:T(8,128)(2,1)} %param.15) | copy-start | bytes 786436
  7.2 397.1 %all-gather.9.cloned.1.call-start = ((), (), s32[]{:S(2)}) async-start(), calls=%async_computation.14 | async-start | bytes 1572864 | tf_op jit(solution)/shard_map/all_gather | solution.py:162
  7.9 139.4 %copy-start.53 = (s32[2]{0:T(128)S(1)}, s32[2]{0:T(128)}, u32[]{:S(2)}) copy-start(s32[2]{0:T(128)} %param.17) | copy-start | bytes 28
  7.9 139.6 %copy-start.48 = (bf16[16,512]{1,0:T(8,128)(2,1)S(1)}, bf16[16,512]{1,0:T(8,128)(2,1)}, u32[]{:S(2)}) copy-start(bf16[16,512]{1,0:T(8,128)(2,1)} %param.21) | copy-start | bytes 49156
  7.9 396.3 %all-gather.11.cloned.1.call-start = ((), (), s32[]{:S(2)}) async-start(), calls=%async_computation.15 | async-start | bytes 1081344 | tf_op jit(solution)/shard_map/all_gather | solution.py:128
  8.7 401.5 %all-gather.7.cloned.1.call-start = ((), (), s32[]{:S(2)}) async-start(), calls=%async_computation.13 | async-start | bytes 1622016 | tf_op jit(solution)/shard_map/all_gather | solution.py:125
  9.4 430.3 %all-gather.13.cloned.1.call-start = ((), (), s32[]{:S(2)}) async-start(), calls=%async_computation.16 | async-start | bytes 2162688 | tf_op jit(solution)/shard_map/all_gather | solution.py:130
  10.0 433.4 %all-gather.15.cloned.1.call-start = ((), (), s32[]{:S(2)}) async-start(), calls=%async_computation.17 | async-start | bytes 2162688 | tf_op jit(solution)/shard_map/all_gather | solution.py:131
  10.6 478.7 %reduce-scatter.40.cloned.1.call-start = ((), (), s32[]{:S(2)}) async-start(), calls=%async_computation.25 | async-start | bytes 786432
  81.8 139.8 %copy-start.49 = (bf16[16,512]{1,0:T(8,128)(2,1)S(1)}, bf16[16,512]{1,0:T(8,128)(2,1)}, u32[]{:S(2)}) copy-start(bf16[16,512]{1,0:T(8,128)(2,1)} %param.22) | copy-start | bytes 49156
  81.8 211.6 %copy-start.50 = (bf16[16,512]{1,0:T(8,128)(2,1)S(1)}, bf16[16,512]{1,0:T(8,128)(2,1)}, u32[]{:S(2)}) copy-start(bf16[16,512]{1,0:T(8,128)(2,1)} %param.24) | copy-start | bytes 49156
  81.8 285.2 %copy-start.54 = (bf16[64]{0:T(256)(128)(2,1)S(1)}, bf16[64]{0:T(256)(128)(2,1)}, u32[]{:S(2)}) copy-start(bf16[64]{0:T(256)(128)(2,1)} %param.29) | copy-start | bytes 388
  81.8 322.4 %copy-start.51 = (s32[2,512]{1,0:T(2,128)S(1)}, s32[2,512]{1,0:T(2,128)}, u32[]{:S(2)}) copy-start(s32[2,512]{1,0:T(2,128)} %param.18) | copy-start | bytes 12292
  421.5 8.1 copy-start.24
  474.0 32.3 %reduce-scatter.42.cloned.1.call-start = ((), (), s32[]{:S(2)}) async-start(), calls=%async_computation.26 | async-start | bytes 786432
  478.6 4.6 copy-start.4
  478.6 50.2 %reduce-scatter.28.cloned.1.call-start = ((), (), s32[]{:S(2)}) async-start(), calls=%async_computation.19 | async-start | bytes 1572864 | tf_op jit(solution)/shard_map/reduce_scatter | solution.py:209
  483.2 68.4 %reduce-scatter.26.cloned.1.call-start = ((), (), s32[]{:S(2)}) async-start(), calls=%async_computation.18 | async-start | bytes 1572864 | tf_op jit(solution)/shard_map/reduce_scatter | solution.py:206
  485.6 201.5 %reduce-scatter.48.cloned.1.call-start = ((), (), s32[]{:S(2)}) async-start(), calls=%async_computation.29 | async-start | bytes 270336
  487.8 22.2 %copy-start.26 = (bf16[2,8,64,128]{3,2,1,0:T(8,128)(2,1)}, bf16[2,8,64,128]{3,2,1,0:T(8,128)(2,1)S(1)}, u32[]{:S(2)}) copy-start(bf16[2,8,64,128]{3,2,1,0:T(8,128)(2,1)S(1)} %get-tuple-element.114) | copy-start | bytes 786436
  492.3 17.6 %copy-start.28 = (bf16[2,128,512]{1,2,0:T(8,128)(2,1)}, bf16[2,128,512]{1,2,0:T(8,128)(2,1)S(1)}, u32[]{:S(2)}) copy-start(bf16[2,128,512]{1,2,0:T(8,128)(2,1)S(1)} %copy.144) | copy-start | bytes 786436
  514.8 306.7 %reduce-scatter.30.cloned.1.call-start = ((), (), s32[]{:S(2)}) async-start(), calls=%async_computation.20 | async-start | bytes 1081344 | tf_op jit(solution)/shard_map/reduce_scatter | solution.py:275
  517.2 438.1 %reduce-scatter.32.cloned.1.call-start = ((), (), s32[]{:S(2)}) async-start(), calls=%async_computation.21 | async-start | bytes 1081344 | tf_op jit(solution)/shard_map/reduce_scatter | solution.py:276
  518.7 570.8 %reduce-scatter.34.cloned.1.call-start = ((), (), s32[]{:S(2)}) async-start(), calls=%async_computation.22 | async-start | bytes 1081344 | tf_op jit(solution)/shard_map/reduce_scatter | solution.py:278
  520.1 701.4 %reduce-scatter.50.cloned.1.call-start = ((), (), s32[]{:S(2)}) async-start(), calls=%async_computation.30 | async-start | bytes 270336
  531.0 794.8 %reduce-scatter.44.cloned.1.call-start = ((), (), s32[]{:S(2)}) async-start(), calls=%async_computation.27 | async-start | bytes 3244032
  538.2 927.0 %reduce-scatter.46.cloned.1.call-start = ((), (), s32[]{:S(2)}) async-start(), calls=%async_computation.28 | async-start | bytes 2162688
  557.5 1048.5 %reduce-scatter.36.cloned.1.call-start = ((), (), s32[]{:S(2)}) async-start(), calls=%async_computation.23 | async-start | bytes 4325376 | tf_op jit(solution)/shard_map/reduce_scatter | solution.py:279
  561.5 1185.9 %reduce-scatter.38.cloned.1.call-start = ((), (), s32[]{:S(2)}) async-start(), calls=%async_computation.24 | async-start | bytes 4325376 | tf_op jit(solution)/shard_map/reduce_scatter | solution.py:280
  610.8 77.6 %copy-start.23 = (bf16[512,1024]{1,0:T(8,128)(2,1)S(1)}, bf16[512,1024]{1,0:T(8,128)(2,1)}, u32[]{:S(2)}) copy-start(bf16[512,1024]{1,0:T(8,128)(2,1)} %all-gather.11.cloned.1.call-done) | copy-start | bytes 3145732
  610.8 77.6 %copy-start.39 = (bf16[2,256,512]{1,2,0:T(8,128)(2,1)S(1)}, bf16[2,256,512]{1,2,0:T(8,128)(2,1)}, u32[]{:S(2)}) copy-start(bf16[2,256,512]{1,2,0:T(8,128)(2,1)} %reduce-scatter.26.cloned.1.call-done) | copy-start | bytes 1572868
  (41 other events, 70.3 us)
Sparse Core Ops, SparseCore 0:
  9.6 24.6 all-gather.8
  37.1 53.8 all-gather.10
  93.9 54.1 all-gather.6
  150.9 55.9 all-gather.12
  209.8 56.9 all-gather.14
  474.1 15.2 reduce-scatter.39
  491.7 14.5 reduce-scatter.41
  508.5 20.2 reduce-scatter.27
  531.2 20.3 reduce-scatter.25
  553.6 133.4 reduce-scatter.47
  690.0 131.5 reduce-scatter.29
  824.3 130.9 reduce-scatter.31
  958.2 131.2 reduce-scatter.33
  1092.2 129.3 reduce-scatter.49
  1228.2 97.4 reduce-scatter.43
  1328.5 136.6 reduce-scatter.45
  1467.9 137.9 reduce-scatter.35
  1608.6 138.6 reduce-scatter.37
where the time goes:
time: 1760 us; the launch traced here: 1750 us
  waiting for transfers between devices  1170 us (66%)
  blocking collectives  446 us (25%)
  matrix products  69.3 us (4%)
  local copies, waits for them, and re-layouts  42.4 us (2%)
    unnamed x24, waiting for transfers between devices  469 us
    reduce_scatter x1, waiting for transfers between devices, per_device(): lax.psum_scatter(d_down, ('batch', 'seq'), scatter_dimension=0, tiled=True)  141 us
    reduce_scatter x1, waiting for transfers between devices, per_device(): lax.psum_scatter(d_up, ('batch', 'seq'), scatter_dimension=0, tiled=True)  141 us
    reduce_scatter x1, waiting for transfers between devices, per_device(): lax.psum_scatter(d_co, ('batch', 'seq'), scatter_dimension=0, tiled=True)  134 us
    reduce_scatter x1, waiting for transfers between devices, per_device(): lax.psum_scatter(d_cq, ('batch', 'seq'), scatter_dimension=0, tiled=True)  134 us
    reduce_scatter x1, waiting for transfers between devices, per_device(): lax.psum_scatter(d_out, ('batch', 'seq'), scatter_dimension=0, tiled=True)  131 us
    unnamed x2, blocking collectives  76.4 us
    all_gather x1, blocking collectives, per_device(): lax.all_gather(attn_out, ('batch', 'seq'), axis=0, tiled=True)  74 us
  transfers between devices with their start and end apart: 18, of which 13 were waited for; matrix products, arithmetic and copies ran while one was open for 5% of the time, Pallas kernels for 0%

commit v1 on v0

v1 whole, which is shorter than its diff:
```python
import functools

import jax
import jax.numpy as jnp
from jax import lax
from jax.experimental import pallas as pl
from jax.experimental.pallas import tpu as pltpu
from jax.sharding import PartitionSpec as P

D = 512
FF = 2048
HEADS = 8
HEAD_DIM = 64
EPSILON = 1e-05
NEGATIVE = -1000000000.0
SCALE = HEAD_DIM ** (-0.5)
BLOCKS = 32
WIDE = 4096
BF = jnp.bfloat16
F32 = jnp.float32
BOTH = ("batch", "seq")

QKV, OUT, CQ, CKV, CO = (0, 1536), (1536, 2048), (2048, 2560), (2560, 3584), (3584, 4096)


def dot(a, b):
    return lax.dot_general(a, b, (((1,), (0,)), ((), ())), preferred_element_type=F32)


def dot_nt(a, b):
    return lax.dot_general(a, b, (((1,), (1,)), ((), ())), preferred_element_type=F32)


def dot_tn(a, b):
    return lax.dot_general(a, b, (((0,), (0,)), ((), ())), preferred_element_type=F32)


def norm(values):
    centred = values - jnp.mean(values, axis=-1, keepdims=True)
    rate = lax.rsqrt(jnp.mean(centred * centred, axis=-1, keepdims=True) + EPSILON)
    return centred * rate, rate


def norm_back(values, gain, grad):
    unit, rate = norm(values)
    scaled = grad * gain
    part = rate * (
        scaled
        - jnp.mean(scaled, axis=-1, keepdims=True)
        - unit * jnp.mean(scaled * unit, axis=-1, keepdims=True)
    )
    return part, row_sum(grad * unit), row_sum(grad)


def row_sum(values):
    return jnp.sum(values.astype(F32), axis=0, keepdims=True)


def lane_masks(dtype):
    lane = lax.broadcasted_iota(jnp.int32, (1, 128), 1)
    return [(lane // HEAD_DIM == j).astype(dtype) for j in range(2)]


def scores_t(keys, queries, visible):
    return jnp.where(visible, dot_nt(keys, queries) * SCALE, NEGATIVE)


def attend(q_ref, k_ref, v_ref, visible, mixed_ref, log_ref):
    masks = lane_masks(BF)
    for pair in range(HEADS // 2):
        cols = slice(128 * pair, 128 * pair + 128)
        queries, keys, values = q_ref[:, cols], k_ref[:, cols], v_ref[:, cols]
        total = None
        for j in range(2):
            scores = scores_t(keys, queries * masks[j], visible)
            top = jnp.max(scores, axis=0, keepdims=True)
            exponent = jnp.exp(scores - top)
            row_total = jnp.sum(exponent, axis=0, keepdims=True)
            probs = (exponent * (1.0 / row_total)).astype(BF)
            log_ref[2 * pair + j : 2 * pair + j + 1, :] = top + jnp.log(row_total)
            part = dot_tn(probs, values * masks[j])
            total = part if total is None else total + part
        mixed_ref[:, cols] = total.astype(BF)


def attend_back(q_ref, k_ref, v_ref, visible, log_ref, grad_ref, dq_ref, dk_ref, dv_ref):
    masks = lane_masks(BF)
    for pair in range(HEADS // 2):
        cols = slice(128 * pair, 128 * pair + 128)
        queries, keys, values, grads = q_ref[:, cols], k_ref[:, cols], v_ref[:, cols], grad_ref[:, cols]
        dq = dk = dv = None
        for j in range(2):
            own_q, own_k, own_g = queries * masks[j], keys * masks[j], grads * masks[j]
            scores = scores_t(keys, own_q, visible)
            probs = jnp.exp(scores - log_ref[2 * pair + j : 2 * pair + j + 1, :])
            grad_probs = dot_nt(values, own_g)
            part_v = dot(probs.astype(BF), own_g)
            inner = jnp.sum(probs * grad_probs, axis=0, keepdims=True)
            low = (probs * (grad_probs - inner)).astype(BF)
            part_k = dot(low, own_q)
            part_q = dot_tn(low, own_k)
            dq = part_q if dq is None else dq + part_q
            dk = part_k if dk is None else dk + part_k
            dv = part_v if dv is None else dv + part_v
        dq_ref[:, cols] = (dq * SCALE).astype(BF)
        dk_ref[:, cols] = (dk * SCALE).astype(BF)
        dv_ref[:, cols] = dv.astype(BF)


def copies_in(order, pieces, pairs, sems):
    started, slot = [], 0
    first = 0
    for piece in pieces:
        for k in range(piece.shape[0]):
            for source, target in pairs(piece, k, order[first + k]):
                copy = pltpu.make_async_copy(source, target, sems.at[slot])
                copy.start()
                started.append(copy)
                slot += 1
        first += piece.shape[0]
    return started


def copies_out(order, outs, pairs, sems):
    return copies_in(order, outs, lambda out, k, index: [(b, a) for a, b in pairs(out, k, index)], sems)


def wait_all(started):
    for copy in started:
        copy.wait()


def rows16(index):
    return pl.ds(pl.multiple_of(index * 16, 16), 16)


def halves(ref, place, rows):
    own = pl.ds(pl.multiple_of(place * rows, rows), rows)
    other = pl.ds(pl.multiple_of((1 - place) * rows, rows), rows)
    return ref.at[own], ref.at[other]


def self_visible(length, rows):
    key = lax.broadcasted_iota(jnp.int32, (rows, rows), 0)
    query = lax.broadcasted_iota(jnp.int32, (rows, rows), 1)
    return (key <= query) & (key < length)


def forward_kernel(
    n_pieces, order, info, *refs
):
    pieces = refs[:n_pieces]
    (h_own, h_new, m_own, m_new, mask) = refs[n_pieces : n_pieces + 5]
    (
        x0, mem, normed1, q, k, v, mixed1, log1, x1, normed2, cq, ck, cv, mixed2, log2, x2, normed3, vecs, ffb,
        weights, small, sems, sems2,
    ) = refs[n_pieces + 5 :]
    place, length = info[0], info[1]
    started = copies_in(
        order,
        pieces,
        lambda piece, b, index: [(piece.at[b, :, 0:WIDE], weights.at[rows16(index)])],
        sems,
    )
    started += copies_in(
        order, pieces, lambda piece, b, index: [(piece.at[b, :, WIDE : WIDE + 128], small.at[index])], sems2
    )
    rows = h_own.shape[0]
    own, new = halves(x0, place, rows)
    own[...], new[...] = h_own[...], h_new[...]
    own, new = halves(mem, place, m_own.shape[0])
    own[...], new[...] = m_own[...], m_new[...]
    hidden = x0[...].astype(F32)
    unit1, _ = norm(hidden)
    wait_all(started)

    lane = lax.broadcasted_iota(jnp.int32, (16, 128), 1)
    for tile in range(D // 128):
        row = jnp.zeros((16, 128), F32)
        for i in range(8):
            row = jnp.where(lane // 16 == i, small[8 * tile + i].astype(F32), row)
        vecs[:, 128 * tile : 128 * tile + 128] = row
    ffb[...] = jnp.zeros_like(ffb)
    for tile in range(FF // 128):
        row = jnp.where(lane < 64, small[2 * tile].astype(F32), small[2 * tile + 1].astype(F32))
        ffb[tile // 4 : tile // 4 + 1, 128 * (tile % 4) : 128 * (tile % 4) + 128] = row[13:14, :]

    def bias(j):
        return vecs[j : j + 1, :]

    normed1[...] = (unit1 * bias(10) + bias(0)).astype(BF)
    q[...] = (dot(normed1[...], weights[:, 0:512]) + bias(1)).astype(BF)
    k[...] = dot(normed1[...], weights[:, 512:1024]).astype(BF)
    v[...] = (dot(normed1[...], weights[:, 1024:1536]) + bias(2)).astype(BF)
    ck[...] = dot(mem[...], weights[:, 2560:3072]).astype(BF)
    cv[...] = (dot(mem[...], weights[:, 3072:3584]) + bias(6)).astype(BF)
    attend(q, k, v, self_visible(length, 2 * rows), mixed1, log1)
    after_self = hidden + (dot(mixed1[...], weights[:, OUT[0] : OUT[1]]) + bias(3))
    x1[...] = after_self
    normed2[...] = (norm(after_self)[0] * bias(11) + bias(4)).astype(BF)
    cq[...] = (dot(normed2[...], weights[:, CQ[0] : CQ[1]]) + bias(5)).astype(BF)
    attend(cq, ck, cv, mask[...] > 0, mixed2, log2)
    after_cross = after_self + (dot(mixed2[...], weights[:, CO[0] : CO[1]]) + bias(7))
    x2[...] = after_cross
    normed3[...] = (norm(after_cross)[0] * bias(12) + bias(8)).astype(BF)


def ffn_kernel(n_pieces, n_outs, order, info, *refs):
    pieces = refs[:n_pieces]
    (x2, normed3, g_own, g_new, vecs, ffb) = refs[n_pieces : n_pieces + 6]
    rest = refs[n_pieces + 6 :]
    (out_keep, out_send, grad_x2, small, ffg) = rest[:5]
    outs = rest[5 : 5 + n_outs]
    (up, down, d_up, d_down, grad_out, sems) = rest[5 + n_outs :]
    place = info[0]

    def down_rows(index):
        return pl.ds(pl.multiple_of(index * 4, 4), 4)

    wait = copies_in(
        order,
        pieces,
        lambda piece, b, index: [
            (piece.at[b, 0:4], up.at[:, rows16(index)]),
            (piece.at[b, 4:8], down.at[down_rows(index)]),
        ],
        sems,
    )
    rows = g_own.shape[0]
    own, new = halves(grad_out, place, rows)
    own[...], new[...] = g_own[...], g_new[...]
    wait_all(wait)
    grads = grad_out[...]
    normed = normed3[...]
    normed_t = normed.T
    result = None
    grad_normed = None
    c0 = (2.0 / jnp.pi) ** 0.5
    ffg[...] = jnp.zeros_like(ffg)
    for group in range(FF // 512):
        w_up = up[group]
        w_down = down[32 * group : 32 * group + 32].reshape(512, D)
        hidden = dot(normed, w_up) + ffb[group : group + 1, :]
        square = hidden * hidden
        tanh = jnp.tanh(c0 * (hidden + 0.044715 * (square * hidden)))
        half = 0.5 * (1.0 + tanh)
        active = (hidden * half).astype(BF)
        slope = half + hidden * (0.5 * c0) * (1.0 - tanh * tanh) * (1.0 + (3 * 0.044715) * square)
        part = dot(active, w_down)
        result = part if result is None else result + part
        grad_hidden = (slope * dot_nt(grads, w_down)).astype(BF)
        d_down[32 * group : 32 * group + 32] = dot_tn(active, grads).astype(BF).reshape(32, 16, D)
        d_up[group] = dot(normed_t, grad_hidden).astype(BF)
        ffg[group : group + 1, :] = row_sum(grad_hidden)
        part = dot_nt(grad_hidden, w_up)
        grad_normed = part if grad_normed is None else grad_normed + part
    done = copies_out(
        order,
        outs,
        lambda out, b, index: [
            (out.at[b, 0:4], d_up.at[:, rows16(index)]),
            (out.at[b, 4:8], d_down.at[down_rows(index)]),
        ],
        sems,
    )
    after_cross = x2[...]
    grad_out[...] = (after_cross + (result + vecs[9:10, :])).astype(BF)
    own, new = halves(grad_out, place, rows)
    out_keep[...], out_send[...] = own[...], new[...]
    part, d_gain, d_shift = norm_back(after_cross, vecs[12:13, :], grad_normed)
    grad_x2[...] = grads.astype(F32) + part
    small[...] = jnp.zeros_like(small)
    small[12:13, :] = d_gain
    small[8:9, :] = d_shift
    small[9:10, :] = row_sum(grads)
    wait_all(done)


def cross_back_kernel(n_pieces, n_outs, order, info, *refs):
    pieces = refs[:n_pieces]
    (x1, normed2, mem, cq, ck, cv, mixed2, log2, mask, grad_x2, vecs, small_in) = refs[n_pieces : n_pieces + 12]
    rest = refs[n_pieces + 12 :]
    (grad_x1, mem_keep, mem_send, small) = rest[:4]
    outs = rest[4 : 4 + n_outs]
    (weights, d_weights, grad_mixed, dq, dk, dv, grad_mem, sems) = rest[4 + n_outs :]
    place = info[0]
    wait = copies_in(
        order, pieces, lambda piece, b, index: [(piece.at[b, :, 2048:4096], weights.at[rows16(index)])], sems
    )
    small[...] = small_in[...]
    grad_y = grad_x2[...].astype(BF)
    d_weights[:, 1536:2048] = dot_tn(mixed2[...], grad_y).astype(BF)
    small[7:8, :] = row_sum(grad_y)
    wait_all(wait)
    grad_mixed[...] = dot_nt(grad_y, weights[:, 1536:2048]).astype(BF)
    attend_back(cq, ck, cv, mask[...] > 0, log2, grad_mixed, dq, dk, dv)
    memory = mem[...]
    memory_t = memory.T
    d_weights[:, 512:1024] = dot(memory_t, dk[...]).astype(BF)
    d_weights[:, 1024:1536] = dot(memory_t, dv[...]).astype(BF)
    d_weights[:, 0:512] = dot_tn(normed2[...], dq[...]).astype(BF)
    done = copies_out(
        order, outs, lambda out, b, index: [(out.at[b], d_weights.at[rows16(index)])], sems
    )
    small[6:7, :] = row_sum(dv[...])
    small[5:6, :] = row_sum(dq[...])
    grad_mem[...] = dot_nt(dk[...], weights[:, 512:1024]) + dot_nt(dv[...], weights[:, 1024:1536])
    own, new = halves(grad_mem, place, mem_keep.shape[0])
    mem_keep[...] = own[...]
    mem_send[...] = new[...].astype(BF)
    part, d_gain, d_shift = norm_back(x1[...], vecs[11:12, :], dot_nt(dq[...], weights[:, 0:512]))
    small[11:12, :] = d_gain
    small[4:5, :] = d_shift
    grad_x1[...] = grad_x2[...] + part
    wait_all(done)


def self_back_kernel(n_pieces, n_outs, order, info, *refs):
    pieces = refs[:n_pieces]
    (x0, normed1, q, k, v, mixed1, log1, grad_x1, vecs, small_in, ffg) = refs[n_pieces : n_pieces + 11]
    rest = refs[n_pieces + 11 :]
    (in_keep, in_send) = rest[:2]
    outs = rest[2 : 2 + n_outs]
    (weights, d_weights, d_small, small, grad_mixed, dq, dk, dv, grad_in, sems) = rest[2 + n_outs :]
    place, length = info[0], info[1]
    wait = copies_in(
        order, pieces, lambda piece, b, index: [(piece.at[b, :, 0:2048], weights.at[rows16(index)])], sems
    )
    small[...] = small_in[...]
    grad_y = grad_x1[...].astype(BF)
    d_weights[:, 1536:2048] = dot_tn(mixed1[...], grad_y).astype(BF)
    small[3:4, :] = row_sum(grad_y)
    wait_all(wait)
    grad_mixed[...] = dot_nt(grad_y, weights[:, 1536:2048]).astype(BF)
    rows = q.shape[0]
    attend_back(q, k, v, self_visible(length, rows), log1, grad_mixed, dq, dk, dv)
    normed_t = normed1[...].T
    for i, part in enumerate((dq, dk, dv)):
        d_weights[:, 512 * i : 512 * i + 512] = dot(normed_t, part[...]).astype(BF)
    small[1:2, :] = row_sum(dq[...])
    small[2:3, :] = row_sum(dv[...])
    grad_normed = (
        dot_nt(dq[...], weights[:, 0:512])
        + dot_nt(dk[...], weights[:, 512:1024])
        + dot_nt(dv[...], weights[:, 1024:1536])
    )
    part, d_gain, d_shift = norm_back(x0[...].astype(F32), vecs[10:11, :], grad_normed)
    small[10:11, :] = d_gain
    small[0:1, :] = d_shift
    for index in range(BLOCKS):
        tile = 128 * (index // 8)
        d_small[index] = small[:, tile : tile + 128].astype(BF)
        group, tile = index // 8, 128 * ((index // 2) % 4)
        d_small[index, 13:14, :] = ffg[group : group + 1, tile : tile + 128].astype(BF)
    done = copies_out(
        order,
        outs,
        lambda out, b, index: [
            (out.at[b, :, 0:2048], d_weights.at[rows16(index)]),
            (out.at[b, :, 2048:2176], d_small.at[index]),
        ],
        sems,
    )
    grad_in[...] = grad_x1[...] + part
    own, new = halves(grad_in, place, rows // 2)
    in_keep[...] = own[...]
    in_send[...] = new[...].astype(BF)
    wait_all(done)


VMEM = pl.BlockSpec(memory_space=pltpu.VMEM)
SMEM = pl.BlockSpec(memory_space=pltpu.SMEM)
ANY = pl.BlockSpec(memory_space=pl.ANY)


def shape(dims, dtype):
    return jax.ShapeDtypeStruct(dims, dtype)


def call(kernel, name, order, info, pieces, arrays, out_shapes, block_outs, scratch, flops):
    outs = [shape(*s) for s in out_shapes] + [shape(*s) for s in block_outs]
    moved = sum(a.size * a.dtype.itemsize for a in list(pieces) + list(arrays))
    return pl.pallas_call(
        kernel,
        name=name,
        out_shape=outs,
        in_specs=[SMEM, SMEM] + [ANY] * len(pieces) + [VMEM] * len(arrays),
        out_specs=[VMEM] * len(out_shapes) + [ANY] * len(block_outs),
        scratch_shapes=scratch,
        compiler_params=pltpu.CompilerParams(vmem_limit_bytes=50 * 1024 * 1024),
        cost_estimate=pl.CostEstimate(flops=flops, bytes_accessed=moved, transcendentals=0),
    )(order, info, *pieces, *arrays)


def flat_index(z, y, c, x):
    return ((z * 2 + y) * 2 + c) * 2 + x


def pairs_of(move):
    pairs = []
    for z in range(4):
        for y in range(2):
            for c in range(2):
                for x in range(2):
                    pairs.append((flat_index(z, y, c, x), flat_index(*move(z, y, c, x))))
    return pairs


CORE = pairs_of(lambda z, y, c, x: (z, y, 1 - c, x))
HOP_Z1 = pairs_of(lambda z, y, c, x: (z ^ 1 if c == 0 else z ^ 2, y, c, x))
HOP_Z2 = pairs_of(lambda z, y, c, x: (z ^ 2 if c == 0 else z ^ 1, y, c, x))
HOP_P1 = pairs_of(lambda z, y, c, x: (z, y, c, 1 - x) if c == 0 else (z, 1 - y, c, x))
HOP_P2 = pairs_of(lambda z, y, c, x: (z, y, c, 1 - x) if c == 1 else (z, 1 - y, c, x))
HOPS = (HOP_Z1, HOP_Z2, HOP_P1, HOP_P2)
FLIPS = ((8, 16, 1, 4), (16, 8, 4, 1))


def permute(value, pairs):
    return lax.ppermute(value, BOTH, pairs)


def join(*parts):
    return jnp.concatenate(parts, axis=0)


def block_order():
    me = lax.axis_index(BOTH)
    core = (me // 2) % 2
    k = jnp.arange(16, dtype=jnp.int32)
    planes = []
    for flips in FLIPS:
        planes.append(sum(((k >> b) & 1) * flip for b, flip in enumerate(flips)))
    own = jnp.where(core == 0, planes[0], planes[1])
    other = jnp.where(core == 0, planes[1], planes[0])
    return jnp.concatenate([me ^ own, (me ^ 2) ^ other]).astype(jnp.int32)


def gather(own):
    r1 = permute(own, HOPS[0])
    c2 = join(own, r1)
    r2 = permute(c2, HOPS[1])
    c4 = join(c2, r2)
    r3 = permute(c4, HOPS[2])
    c8 = join(c4, r3)
    r4 = permute(c8, HOPS[3])
    s8 = permute(c8, CORE)
    s4 = permute(r4, CORE)
    return [c8, r4, s8, s4]


def add(a, b):
    return (a.astype(F32) + b.astype(F32)).astype(BF)


def scatter(own, other):
    got = permute(other, CORE)
    for hop, count in ((3, 8), (2, 4), (1, 2)):
        send = add(own[count:], got[count:])
        keep = add(own[:count], got[:count])
        own, got = keep, permute(send, HOPS[hop])
    send = add(own[1:], got[1:])
    keep = own[0].astype(F32) + got[0].astype(F32)
    return keep + permute(send, HOPS[0])[0].astype(F32)


def small_rows(biases, gains, ffn_bias):
    count = biases.shape[0]
    columns = jnp.concatenate([biases, gains], axis=2).transpose(0, 2, 1)
    rows = jnp.tile(columns, (1, 1, 8))
    units = jnp.tile(ffn_bias.reshape(count, 1, 64), (1, 1, 2))
    return jnp.concatenate([rows, units, jnp.zeros((count, 2, 128), BF)], axis=1)


def pack_attention(qkv, out, cq, ckv, co, small):
    return jnp.concatenate([qkv, out, cq, ckv, co, small], axis=2)


def pack_ffn(up, down):
    count = up.shape[0]
    up = up.reshape(count, 16, 4, 512).transpose(0, 2, 1, 3)
    return jnp.concatenate([up, down.reshape(count, 4, 16, 512)], axis=1)


def per_device(n_devices, hidden_in, memory, lengths, source_mask, grad_out, *params):
    (w_qkv, w_out, w_cq, w_ckv, w_co, w_up, w_down, gains, biases, ffn_bias) = params
    permuted = n_devices == BLOCKS
    if not permuted:
        params = [lax.all_gather(p, BOTH, axis=0, tiled=True) for p in params]
        (w_qkv, w_out, w_cq, w_ckv, w_co, w_up, w_down, gains, biases, ffn_bias) = params
    count = w_qkv.shape[0] // 16
    cut = lambda w: w.reshape(count, -1, w.shape[1])
    attention = pack_attention(
        *(cut(w) for w in (w_qkv, w_out, w_cq, w_ckv, w_co)), small_rows(cut(biases), cut(gains), ffn_bias)
    )
    ffn = pack_ffn(cut(w_up), cut(w_down))

    place = lax.axis_index("seq")
    swap = lambda v: lax.ppermute(v, "seq", [(0, 1), (1, 0)])
    pick = lambda v, i: lax.dynamic_index_in_dim(v, i, 0, keepdims=False)
    rows, sources = hidden_in.shape[1], memory.shape[1]
    sent = jnp.concatenate([pick(hidden_in, 1 - place), pick(memory, 1 - place)], axis=0)
    new = swap(sent)
    h_own, m_own, g_own = (pick(v, place) for v in (hidden_in, memory, grad_out))
    h_new, m_new = new[:rows], new[rows:]
    g_new = swap(pick(grad_out, 1 - place))
    source = pick(source_mask, place)
    visible = ((source > 0) | (jnp.arange(source.shape[0]) == 0)).astype(F32)[:, None]
    info = jnp.stack([place, pick(lengths, place)]).astype(jnp.int32)

    if permuted:
        order = block_order()
        a_pieces, f_pieces = gather(attention), gather(ffn)
        halves_of = (16, 16)
    else:
        order = jnp.arange(BLOCKS, dtype=jnp.int32)
        a_pieces, f_pieces = [attention], [ffn]
        halves_of = (32,)

    tgt, src = 2 * rows, 2 * sources
    wide = (tgt, D)
    vec = ((16, D), F32)
    units = ((8, 512), F32)
    dma = pltpu.SemaphoreType.DMA
    mm = 2 * D * D
    (
        x0, mem, normed1, q, k, v, mixed1, log1, x1, normed2, cq, ck, cv, mixed2, log2, x2, normed3, vecs, ffb,
    ) = call(
        functools.partial(forward_kernel, len(a_pieces)), "forward", order, info, a_pieces,
        [h_own, h_new, m_own, m_new, visible],
        [
            (wide, BF), ((src, D), BF), (wide, BF), (wide, BF), (wide, BF), (wide, BF), (wide, BF),
            ((HEADS, tgt), F32), (wide, F32), (wide, BF), (wide, BF), ((src, D), BF), ((src, D), BF), (wide, BF),
            ((HEADS, tgt), F32), (wide, F32), (wide, BF), vec, units,
        ],
        [],
        [pltpu.VMEM((D, WIDE), BF), pltpu.VMEM((BLOCKS, 16, 128), BF), dma((BLOCKS,)), dma((BLOCKS,))],
        mm * (6 * tgt + 2 * src) * 2,
    )
    out_keep, out_send, grad_x2, small, ffg, *d_ffn = call(
        functools.partial(ffn_kernel, len(f_pieces), len(halves_of)), "ffn", order, info, f_pieces,
        [x2, normed3, g_own, g_new, vecs, ffb],
        [((rows, D), BF), ((rows, D), BF), (wide, F32), vec, units],
        [((n, 8, 16, 512), BF) for n in halves_of],
        [
            pltpu.VMEM((4, D, 512), BF), pltpu.VMEM((128, 16, D), BF), pltpu.VMEM((4, D, 512), BF),
            pltpu.VMEM((128, 16, D), BF), pltpu.VMEM(wide, BF), dma((2 * BLOCKS,)),
        ],
        mm * 24 * tgt,
    )
    grad_x1, mem_keep, mem_send, small, *d_cross = call(
        functools.partial(cross_back_kernel, len(a_pieces), len(halves_of)), "cross_back", order, info, a_pieces,
        [x1, normed2, mem, cq, ck, cv, mixed2, log2, visible, grad_x2, vecs, small],
        [(wide, F32), ((sources, D), F32), ((sources, D), BF), vec],
        [((n, 16, 2048), BF) for n in halves_of],
        [
            pltpu.VMEM((D, 2048), BF), pltpu.VMEM((D, 2048), BF), pltpu.VMEM(wide, BF), pltpu.VMEM(wide, BF),
            pltpu.VMEM((src, D), BF), pltpu.VMEM((src, D), BF), pltpu.VMEM((src, D), F32), dma((BLOCKS,)),
        ],
        mm * (8 * tgt + 4 * src),
    )
    in_keep, in_send, *d_self = call(
        functools.partial(self_back_kernel, len(a_pieces), len(halves_of)), "self_back", order, info, a_pieces,
        [x0, normed1, q, k, v, mixed1, log1, grad_x1, vecs, small, ffg],
        [((rows, D), F32), ((rows, D), BF)],
        [((n, 16, 2176), BF) for n in halves_of],
        [
            pltpu.VMEM((D, 2048), BF), pltpu.VMEM((D, 2048), BF), pltpu.VMEM((BLOCKS, 16, 128), BF),
            pltpu.VMEM((16, D), F32), pltpu.VMEM(wide, BF), pltpu.VMEM(wide, BF), pltpu.VMEM(wide, BF),
            pltpu.VMEM(wide, BF), pltpu.VMEM(wide, F32), dma((2 * BLOCKS,)),
        ],
        mm * 12 * tgt,
    )

    def both(keep, sent):
        got = swap(sent).astype(keep.dtype)
        return jnp.where(place == 0, jnp.stack([keep, got]), jnp.stack([got, keep]))

    outputs = (both(out_keep, out_send), both(in_keep, in_send), both(mem_keep, mem_send))

    if permuted:
        g_ffn, g_cross, g_self = scatter(*d_ffn), scatter(*d_cross), scatter(*d_self)
        me = lax.axis_index(BOTH)
        g_small = g_self[:, 2048:]
        columns = lax.dynamic_slice(g_small, (0, (me % 8) * 16), (13, 16)).T
        g_unit = lax.dynamic_slice(g_small, (13, (me % 2) * 64), (1, 64)).reshape(64)
        g_up = g_ffn[:4].transpose(1, 0, 2).reshape(16, FF)
        g_down = g_ffn[4:].reshape(64, D)
        rest = (
            g_self[:, :1536], g_self[:, 1536:2048], g_cross[:, :512], g_cross[:, 512:1536], g_cross[:, 1536:],
            g_up, g_down, columns[:, 10:], columns[:, :10], g_unit,
        )
    else:
        d_ffn, d_cross, d_self = (d[0].astype(F32) for d in (d_ffn, d_cross, d_self))
        d_small = d_self[:, :, 2048:]
        columns = jnp.concatenate([d_small[i, :13, 16 * (i % 8) : 16 * (i % 8) + 16].T for i in range(BLOCKS)])
        d_unit = jnp.concatenate([d_small[i, 13, 64 * (i % 2) : 64 * (i % 2) + 64] for i in range(BLOCKS)])
        d_self = d_self[:, :, :2048].reshape(D, 2048)
        d_cross = d_cross.reshape(D, 2048)
        d_up = d_ffn[:, :4].transpose(0, 2, 1, 3).reshape(D, FF)
        d_down = d_ffn[:, 4:].reshape(FF, D)
        rest = tuple(
            lax.psum_scatter(d, BOTH, scatter_dimension=0, tiled=True)
            for d in (
                d_self[:, :1536], d_self[:, 1536:], d_cross[:, :512], d_cross[:, 512:1536], d_cross[:, 1536:],
                d_up, d_down, columns[:, 10:], columns[:, :10], d_unit,
            )
        )
    return outputs + rest


def solution(mesh):
    rows = P(BOTH, None)
    part = P("batch", "seq", None)
    return jax.shard_map(
        functools.partial(per_device, mesh.devices.size),
        mesh=mesh,
        in_specs=(part, part, P("batch"), P("batch", None), part) + (rows,) * 9 + (P(BOTH),),
        out_specs=(part, part, part) + (rows,) * 9 + (P(BOTH),),
        check_vma=False,
    )
```

time: 1760 us -> 203 us (0.12)
  waiting for transfers between devices: 1170 us -> 86.3 us
  blocking collectives: 446 us -> 0 us
  matrix products: 69.3 us -> 0 us
  Pallas kernels: 0 us -> 39.2 us
  starting transfers between devices: 0.99 us -> 39 us
    reduce_scatter x7 -> x0, waiting for transfers between devices: 698 us -> none  [the longest x1 141 us: per_device(): lax.psum_scatter(d_down, ('batch', 'seq'), scatter_dimension=0, tiled=True)]
    unnamed x24 -> x0, waiting for transfers between devices: 469 us -> none
    all_gather x7 -> x0, blocking collectives: 369 us -> none  [the longest x1 74 us: per_device(): lax.all_gather(attn_out, ('batch', 'seq'), axis=0, tiled=True)]
    ppermute x0 -> x32, waiting for transfers between devices: none -> 86.3 us  [the longest x27 81.3 us: permute(): return lax.ppermute(value, BOTH, pairs)]
    unnamed x2 -> x0, blocking collectives: 76.4 us -> none
    dot_general x39 -> x0, matrix products: 69.3 us -> none  [the longest x10 17.4 us: weight_grad(): jnp.einsum('erd,erf->df', left, grad_rows, preferred_element_type=jnp.flo...]
    pallas_call x0 -> x4, Pallas kernels: none -> 39.2 us  [call(): pl.pallas_call(kernel, name=name, out_shape=outs, in_specs=[SMEM, SMEM] +...]
    ppermute x0 -> x32, starting transfers between devices: none -> 39 us  [the longest x27 34.5 us: permute(): return lax.ppermute(value, BOTH, pairs)]
  transfers between devices with their start and end apart: 18 -> 32, of which waited for: 13 -> 16; matrix products, arithmetic and copies ran while one was open for 5% -> 11% of each run, Pallas kernels for 0% -> 9%
where the time goes in v1:
time: 203 us; the launch traced here: 202 us
  waiting for transfers between devices  86.3 us (43%)
  Pallas kernels  39.2 us (19%)
  starting transfers between devices  39 us (19%)
  local copies, waits for them, and re-layouts  25.6 us (13%)
  other arithmetic  10.5 us (5%)
    ppermute x27, waiting for transfers between devices, permute(): return lax.ppermute(value, BOTH, pairs)  81.3 us
    pallas_call x4, Pallas kernels, call(): pl.pallas_call(kernel, name=name, out_shape=outs, in_specs=[SMEM, SMEM] +...  39.2 us
    ppermute x27, starting transfers between devices, permute(): return lax.ppermute(value, BOTH, pairs)  34.5 us
    unnamed x56, local copies, waits for them, and re-layouts  10.9 us
    ppermute x5, waiting for transfers between devices, per_device(): swap = lambda v: lax.ppermute(v, 'seq', [(0, 1), (1, 0)])  5.04 us
    ppermute x5, starting transfers between devices, per_device(): swap = lambda v: lax.ppermute(v, 'seq', [(0, 1), (1, 0)])  4.45 us
  transfers between devices with their start and end apart: 32, of which 16 were waited for; matrix products, arithmetic and copies ran while one was open for 11% of the time, Pallas kernels for 9%

profile of v1, /device:TPU:0, one launch (start us, length us, event | category | flops | bytes accessed | tf_op | source)
XLA Modules:
  0.0 201.7 jit_solution(12289393039971726576)
XLA Ops:
  7.1 3.0 %collective-permute-start.6 = (bf16[1,16,4224]{2,1,0:T(8,128)(2,1)S(1)}, bf16[1,16,4224]{2,1,0:T(8,128)(2,1)S(1)}, u32[]{:S(2)}, u32[]{:S(2)}) collective-permute-start(bf16[1,16,4224]{2,1,0:T(8,128)(2,1)S(1)} %constant_dynamic-update-slice_fusion), channel_id=1, source_target_pairs={{0,8},{1,9},{2,18},{3,19},{4,12},{5,13},{6,22},{7,23},{8,0},{9,1},... | collective-permute-start | bytes 405512 | tf_op jit(solution)/shard_map/ppermute | solution.py:419
  10.1 4.1 %collective-permute-done.6 = bf16[1,16,4224]{2,1,0:T(8,128)(2,1)S(1)} collective-permute-done((bf16[1,16,4224]{2,1,0:T(8,128)(2,1)S(1)}, bf16[1,16,4224]{2,1,0:T(8,128)(2,1)S(1)}, u32[]{:S(2)}, u32[]{:S(2)}) %collective-permute-start.6) | collective-permute-done | bytes 135200 | tf_op jit(solution)/shard_map/ppermute | solution.py:419
  14.2 2.3 %collective-permute-start.7 = (bf16[2,16,4224]{2,1,0:T(8,128)(2,1)S(1)}, bf16[2,16,4224]{2,1,0:T(8,128)(2,1)S(1)}, u32[]{:S(2)}, u32[]{:S(2)}) collective-permute-start(bf16[2,16,4224]{2,1,0:T(8,128)(2,1)S(1)} %pad_maximum_fusion.5), channel_id=1, source_target_pairs={{0,16},{1,17},{2,10},{3,11},{4,20},{5,21},{6,14},{7,15},{8,24},{9,... | collective-permute-start | bytes 811016 | tf_op jit(solution)/shard_map/ppermute | solution.py:419
  17.5 2.6 %collective-permute-start = (bf16[1,8,16,512]{3,2,1,0:T(8,128)(2,1)S(1)}, bf16[1,8,16,512]{3,2,1,0:T(8,128)(2,1)S(1)}, u32[]{:S(2)}, u32[]{:S(2)}) collective-permute-start(bf16[1,8,16,512]{3,2,1,0:T(8,128)(2,1)S(1)} %pad_maximum_fusion.7), channel_id=1, source_target_pairs={{0,8},{1,9},{2,18},{3,19},{4,12},{5,13},{6,22},{7,23},{8,0},{9,1},... | collective-permute-start | bytes 393224 | tf_op jit(solution)/shard_map/ppermute | solution.py:419
  20.1 7.1 %collective-permute-done.7 = bf16[2,16,4224]{2,1,0:T(8,128)(2,1)S(1)} collective-permute-done((bf16[2,16,4224]{2,1,0:T(8,128)(2,1)S(1)}, bf16[2,16,4224]{2,1,0:T(8,128)(2,1)S(1)}, u32[]{:S(2)}, u32[]{:S(2)}) %collective-permute-start.7) | collective-permute-done | bytes 270368 | tf_op jit(solution)/shard_map/ppermute | solution.py:419
  27.3 2.1 %collective-permute-start.8 = (bf16[4,16,4224]{2,1,0:T(8,128)(2,1)S(1)}, bf16[4,16,4224]{2,1,0:T(8,128)(2,1)S(1)}, u32[]{:S(2)}, u32[]{:S(2)}) collective-permute-start(bf16[4,16,4224]{2,1,0:T(8,128)(2,1)S(1)} %pad_maximum_fusion.2), channel_id=1, source_target_pairs={{0,1},{1,0},{2,6},{3,7},{4,5},{5,4},{6,2},{7,3},{8,9},{9,8},{10,14... | collective-permute-start | bytes 1622024 | tf_op jit(solution)/shard_map/ppermute | solution.py:419
  29.5 10.1 %collective-permute-done.1 = bf16[2,8,16,512]{3,2,1,0:T(8,128)(2,1)S(1)} collective-permute-done((bf16[2,8,16,512]{3,2,1,0:T(8,128)(2,1)S(1)}, bf16[2,8,16,512]{3,2,1,0:T(8,128)(2,1)S(1)}, u32[]{:S(2)}, u32[]{:S(2)}) %collective-permute-start.1) | collective-permute-done | bytes 262176 | tf_op jit(solution)/shard_map/ppermute | solution.py:419
  39.9 2.1 %collective-permute-start.9 = (bf16[8,16,4224]{2,1,0:T(8,128)(2,1)S(1)}, bf16[8,16,4224]{2,1,0:T(8,128)(2,1)S(1)}, u32[]{:S(2)}, u32[]{:S(2)}) collective-permute-start(bf16[8,16,4224]{2,1,0:T(8,128)(2,1)S(1)} %pad_maximum_fusion.refs_0_), channel_id=1, source_target_pairs={{0,4},{1,5},{2,3},{3,2},{4,0},{5,1},{6,7},{7,6},{8,12},{9,13},{10,... | collective-permute-start | bytes 3244040 | tf_op jit(solution)/shard_map/ppermute | solution.py:419
  42.0 12.6 %collective-permute-done.2 = bf16[4,8,16,512]{3,2,1,0:T(8,128)(2,1)S(1)} collective-permute-done((bf16[4,8,16,512]{3,2,1,0:T(8,128)(2,1)S(1)}, bf16[4,8,16,512]{3,2,1,0:T(8,128)(2,1)S(1)}, u32[]{:S(2)}, u32[]{:S(2)}) %collective-permute-start.2) | collective-permute-done | bytes 524320 | tf_op jit(solution)/shard_map/ppermute | solution.py:419
  56.8 1.6 dynamic-slice_bitcast_fusion.4
  61.6 8.1 %collective-permute-done.3.refs_1_ = bf16[8,8,16,512]{3,2,1,0:T(8,128)(2,1)} collective-permute-done((bf16[8,8,16,512]{3,2,1,0:T(8,128)(2,1)S(1)}, bf16[8,8,16,512]{3,2,1,0:T(8,128)(2,1)}, u32[]{:S(2)}, u32[]{:S(2)}) %collective-permute-start.3) | collective-permute-done | bytes 1048608 | tf_op jit(solution)/shard_map/ppermute | solution.py:419
  77.3 10.5 %forward.1 = (bf16[256,512]{1,0:T(8,128)(2,1)S(1)}, bf16[512,512]{1,0:T(8,128)(2,1)}, bf16[256,512]{1,0:T(8,128)(2,1)S(1)}, bf16[256,512]{1,0:T(8,128)(2,1)S(1)}...) custom-call(s32[32]{0:T(128)S(1)} %pad_add_fusion.order, ...), custom_call_target="tpu_custom_call" | custom-call | flops 2684354560 | bytes 5113856 | tf_op jit(solution)/shard_map/forward/pallas_call | solution.py:383
  90.3 10.4 %ffn.1 = (bf16[128,512]{1,0:T(8,128)(2,1)S(1)}, bf16[128,512]{1,0:T(8,128)(2,1)S(1)}, f32[256,512]{1,0:T(8,128)S(1)}, f32[16,512]{1,0:T(8,128)S(1)}, f32[8,512]{...) custom-call(s32[32]{0:T(128)S(1)} %pad_add_fusion.order, s32[2]{0:T(128)S(1)} %pad_add_fusion.1.info, ...), custom_call_target="tpu_custom_call" | custom-call | flops 3221225472 | bytes 5292032 | tf_op jit(solution)/shard_map/ffn/pallas_call | solution.py:383
  102.2 10.1 %cross_back.1 = (f32[256,512]{1,0:T(8,128)S(1)}, f32[256,512]{1,0:T(8,128)S(1)}, bf16[256,512]{1,0:T(8,128)(2,1)S(1)}, f32[16,512]{1,0:T(8,128)S(1)}, bf16[16,16...) custom-call(s32[32]{0:T(128)S(1)} %pad_add_fusion.order, s32[2]{0:T(128)S(1)} %pad_add_fusion.1.info, ...), custom_call_target="tpu_custom_call" | custom-call | flops 2147483648 | bytes 7809024 | tf_op jit(solution)/shard_map/cross_back/pallas_call | solution.py:383
  115.6 8.2 %self_back.1 = (f32[128,512]{1,0:T(8,128)S(1)}, bf16[128,512]{1,0:T(8,128)(2,1)S(1)}, bf16[16,16,2176]{2,1,0:T(8,128)(2,1)}, bf16[16,16,2176]{2,1,0:T(8,128)(2,1)}) custom-call(s32[32]{0:T(128)S(1)} %pad_add_fusion.order, s32[2]{0:T(128)S(1)} %pad_add_fusion.1.info, bf16[8,16,4224]{2,1,0:T(8,128)(2,1)S(1)} %copy-done.1, bf16[8,16,4224]{2,1,0:T(8,128)(2,1)} %copy-done.17, ...), custom_call_target="tpu_custom_call" | custom-call | flops 1610612736 | bytes 6512640 | tf_op jit(solution)/shard_map/self_back/pallas_call | solution.py:383
  123.8 1.8 collective-permute-start.15
  128.0 2.2 %collective-permute-done.15 = bf16[128,512]{1,0:T(8,128)(2,1)S(1)} collective-permute-done((bf16[128,512]{1,0:T(8,128)(2,1)S(1)}, bf16[128,512]{1,0:T(8,128)(2,1)S(1)}, u32[]{:S(2)}, u32[]{:S(2)}) %collective-permute-start.15) | collective-permute-done | bytes 131104 | tf_op jit(solution)/shard_map/ppermute | solution.py:498
  133.1 2.8 %collective-permute-done.16 = bf16[256,512]{1,0:T(8,128)(2,1)S(1)} collective-permute-done((bf16[256,512]{1,0:T(8,128)(2,1)S(1)}, bf16[256,512]{1,0:T(8,128)(2,1)S(1)}, u32[]{:S(2)}, u32[]{:S(2)}) %collective-permute-start.16) | collective-permute-done | bytes 262176 | tf_op jit(solution)/shard_map/ppermute | solution.py:498
  135.9 3.5 %collective-permute-done.23 = bf16[8,16,2048]{2,1,0:T(8,128)(2,1)S(1)} collective-permute-done((bf16[8,16,2048]{2,1,0:T(8,128)(2,1)S(1)}, bf16[8,16,2048]{2,1,0:T(8,128)(2,1)S(1)}, u32[]{:S(2)}, u32[]{:S(2)}) %collective-permute-start.23) | collective-permute-done | bytes 524320 | tf_op jit(solution)/shard_map/ppermute | solution.py:419
  139.6 1.8 collective-permute-start.24
  143.8 4.2 %collective-permute-done.24 = bf16[4,16,2048]{2,1,0:T(8,128)(2,1)S(1)} collective-permute-done((bf16[4,16,2048]{2,1,0:T(8,128)(2,1)S(1)}, bf16[4,16,2048]{2,1,0:T(8,128)(2,1)S(1)}, u32[]{:S(2)}, u32[]{:S(2)}) %collective-permute-start.24) | collective-permute-done | bytes 262176 | tf_op jit(solution)/shard_map/ppermute | solution.py:419
  149.3 2.3 %collective-permute-done.18 = bf16[8,16,2176]{2,1,0:T(8,128)(2,1)S(1)} collective-permute-done((bf16[8,16,2176]{2,1,0:T(8,128)(2,1)S(1)}, bf16[8,16,2176]{2,1,0:T(8,128)(2,1)S(1)}, u32[]{:S(2)}, u32[]{:S(2)}) %collective-permute-start.18) | collective-permute-done | bytes 557088 | tf_op jit(solution)/shard_map/ppermute | solution.py:419
  151.8 1.8 collective-permute-start.19
  153.6 1.8 collective-permute-done.25
  158.1 1.9 collective-permute-done.19
  162.9 8.6 %collective-permute-done.28 = bf16[8,8,16,512]{3,2,1,0:T(8,128)(2,1)S(1)} collective-permute-done((bf16[8,8,16,512]{3,2,1,0:T(8,128)(2,1)S(1)}, bf16[8,8,16,512]{3,2,1,0:T(8,128)(2,1)S(1)}, u32[]{:S(2)}, u32[]{:S(2)}) %collective-permute-start.28) | collective-permute-done | bytes 1048608 | tf_op jit(solution)/shard_map/ppermute | solution.py:419
  171.9 1.9 collective-permute-start.29
  173.8 2.1 %collective-permute-start.21 = (bf16[1,16,2176]{2,1,0:T(8,128)(2,1)S(1)}, bf16[1,16,2176]{2,1,0:T(8,128)(2,1)S(1)}, u32[]{:S(2)}, u32[]{:S(2)}) collective-permute-start(bf16[1,16,2176]{2,1,0:T(8,128)(2,1)S(1)} %add_convert_fusion.19), channel_id=1, source_target_pairs={{0,8},{1,9},{2,18},{3,19},{4,12},{5,13},{6,22},{7,23},{8,0},{9,1},... | collective-permute-start | bytes 208904 | tf_op jit(solution)/shard_map/ppermute | solution.py:419
  175.8 5.3 %collective-permute-done.29 = bf16[4,8,16,512]{3,2,1,0:T(8,128)(2,1)S(1)} collective-permute-done((bf16[4,8,16,512]{3,2,1,0:T(8,128)(2,1)S(1)}, bf16[4,8,16,512]{3,2,1,0:T(8,128)(2,1)S(1)}, u32[]{:S(2)}, u32[]{:S(2)}) %collective-permute-start.29) | collective-permute-done | bytes 524320 | tf_op jit(solution)/shard_map/ppermute | solution.py:419
  181.3 4.0 %collective-permute-start.30 = (bf16[2,8,16,512]{3,2,1,0:T(8,128)(2,1)S(1)}, bf16[2,8,16,512]{3,2,1,0:T(8,128)(2,1)S(1)}, u32[]{:S(2)}, u32[]{:S(2)}) collective-permute-start(bf16[2,8,16,512]{3,2,1,0:T(8,128)(2,1)S(1)} %get-tuple-element.135), channel_id=1, source_target_pairs={{0,16},{1,17},{2,10},{3,11},{4,20},{5,21},{6,14},{7,15},{8,24},{9,... | collective-permute-start | bytes 786440 | tf_op jit(solution)/shard_map/ppermute | solution.py:419
  185.3 9.9 %collective-permute-done.30 = bf16[2,8,16,512]{3,2,1,0:T(8,128)(2,1)S(1)} collective-permute-done((bf16[2,8,16,512]{3,2,1,0:T(8,128)(2,1)S(1)}, bf16[2,8,16,512]{3,2,1,0:T(8,128)(2,1)S(1)}, u32[]{:S(2)}, u32[]{:S(2)}) %collective-permute-start.30) | collective-permute-done | bytes 262176 | tf_op jit(solution)/shard_map/ppermute | solution.py:419
  198.6 1.8 collective-permute-done.31
  (154 shorter events, 48.1 us)
Async XLA Ops:
  7.1 7.1 %collective-permute-start.6 = (bf16[1,16,4224]{2,1,0:T(8,128)(2,1)S(1)}, bf16[1,16,4224]{2,1,0:T(8,128)(2,1)S(1)}, u32[]{:S(2)}, u32[]{:S(2)}) collective-permute-start(bf16[1,16,4224]{2,1,0:T(8,128)(2,1)S(1)} %constant_dynamic-update-slice_fusion), channel_id=1, source_target_pairs={{0,8},{1,9},{2,18},{3,19},{4,12},{5,13},{6,22},{7,23},{8,0},{9,1},... | collective-permute-start | bytes 405512 | tf_op jit(solution)/shard_map/ppermute | solution.py:419
  14.2 13.0 %collective-permute-start.7 = (bf16[2,16,4224]{2,1,0:T(8,128)(2,1)S(1)}, bf16[2,16,4224]{2,1,0:T(8,128)(2,1)S(1)}, u32[]{:S(2)}, u32[]{:S(2)}) collective-permute-start(bf16[2,16,4224]{2,1,0:T(8,128)(2,1)S(1)} %pad_maximum_fusion.5), channel_id=1, source_target_pairs={{0,16},{1,17},{2,10},{3,11},{4,20},{5,21},{6,14},{7,15},{8,24},{9,... | collective-permute-start | bytes 811016 | tf_op jit(solution)/shard_map/ppermute | solution.py:419
  17.5 11.9 %collective-permute-start = (bf16[1,8,16,512]{3,2,1,0:T(8,128)(2,1)S(1)}, bf16[1,8,16,512]{3,2,1,0:T(8,128)(2,1)S(1)}, u32[]{:S(2)}, u32[]{:S(2)}) collective-permute-start(bf16[1,8,16,512]{3,2,1,0:T(8,128)(2,1)S(1)} %pad_maximum_fusion.7), channel_id=1, source_target_pairs={{0,8},{1,9},{2,18},{3,19},{4,12},{5,13},{6,22},{7,23},{8,0},{9,1},... | collective-permute-start | bytes 393224 | tf_op jit(solution)/shard_map/ppermute | solution.py:419
  27.3 12.4 %collective-permute-start.8 = (bf16[4,16,4224]{2,1,0:T(8,128)(2,1)S(1)}, bf16[4,16,4224]{2,1,0:T(8,128)(2,1)S(1)}, u32[]{:S(2)}, u32[]{:S(2)}) collective-permute-start(bf16[4,16,4224]{2,1,0:T(8,128)(2,1)S(1)} %pad_maximum_fusion.2), channel_id=1, source_target_pairs={{0,1},{1,0},{2,6},{3,7},{4,5},{5,4},{6,2},{7,3},{8,9},{9,8},{10,14... | collective-permute-start | bytes 1622024 | tf_op jit(solution)/shard_map/ppermute | solution.py:419
  29.4 10.1 %collective-permute-start.1 = (bf16[2,8,16,512]{3,2,1,0:T(8,128)(2,1)S(1)}, bf16[2,8,16,512]{3,2,1,0:T(8,128)(2,1)S(1)}, u32[]{:S(2)}, u32[]{:S(2)}) collective-permute-start(bf16[2,8,16,512]{3,2,1,0:T(8,128)(2,1)S(1)} %pad_maximum_fusion.6), channel_id=1, source_target_pairs={{0,16},{1,17},{2,10},{3,11},{4,20},{5,21},{6,14},{7,15},{8,24},{9,... | collective-permute-start | bytes 786440 | tf_op jit(solution)/shard_map/ppermute | solution.py:419
  39.6 14.9 %collective-permute-start.2 = (bf16[4,8,16,512]{3,2,1,0:T(8,128)(2,1)S(1)}, bf16[4,8,16,512]{3,2,1,0:T(8,128)(2,1)S(1)}, u32[]{:S(2)}, u32[]{:S(2)}) collective-permute-start(bf16[4,8,16,512]{3,2,1,0:T(8,128)(2,1)S(1)} %pad_maximum_fusion.3), channel_id=1, source_target_pairs={{0,1},{1,0},{2,6},{3,7},{4,5},{5,4},{6,2},{7,3},{8,9},{9,8},{10,14... | collective-permute-start | bytes 1572872 | tf_op jit(solution)/shard_map/ppermute | solution.py:419
  39.9 16.4 %collective-permute-start.9 = (bf16[8,16,4224]{2,1,0:T(8,128)(2,1)S(1)}, bf16[8,16,4224]{2,1,0:T(8,128)(2,1)S(1)}, u32[]{:S(2)}, u32[]{:S(2)}) collective-permute-start(bf16[8,16,4224]{2,1,0:T(8,128)(2,1)S(1)} %pad_maximum_fusion.refs_0_), channel_id=1, source_target_pairs={{0,4},{1,5},{2,3},{3,2},{4,0},{5,1},{6,7},{7,6},{8,12},{9,13},{10,... | collective-permute-start | bytes 3244040 | tf_op jit(solution)/shard_map/ppermute | solution.py:419
  54.7 15.0 %collective-permute-start.3 = (bf16[8,8,16,512]{3,2,1,0:T(8,128)(2,1)S(1)}, bf16[8,8,16,512]{3,2,1,0:T(8,128)(2,1)}, u32[]{:S(2)}, u32[]{:S(2)}) collective-permute-start(bf16[8,8,16,512]{3,2,1,0:T(8,128)(2,1)S(1)} %pad_maximum_fusion.1.refs_0_), channel_id=1, source_target_pairs={{0,4},{1,5},{2,3},{3,2},{4,0},{5,1},{6,7},{7,6},{8,12},{9,13},{10,... | collective-permute-start | bytes 3145736 | tf_op jit(solution)/shard_map/ppermute | solution.py:419
  56.3 20.1 %collective-permute-start.10 = (bf16[8,16,4224]{2,1,0:T(8,128)(2,1)S(1)}, bf16[8,16,4224]{2,1,0:T(8,128)(2,1)}, u32[]{:S(2)}, u32[]{:S(2)}) collective-permute-start(bf16[8,16,4224]{2,1,0:T(8,128)(2,1)S(1)} %pad_maximum_fusion.refs_0_), channel_id=1, source_target_pairs={{0,2},{1,3},{2,0},{3,1},{4,6},{5,7},{6,4},{7,5},{8,10},{9,11},{10,... | collective-permute-start | bytes 3244040 | tf_op jit(solution)/shard_map/ppermute | solution.py:419
  56.3 20.1 %collective-permute-start.11 = (bf16[8,16,4224]{2,1,0:T(8,128)(2,1)S(1)}, bf16[8,16,4224]{2,1,0:T(8,128)(2,1)}, u32[]{:S(2)}, u32[]{:S(2)}) collective-permute-start(bf16[8,16,4224]{2,1,0:T(8,128)(2,1)S(1)} %collective-permute-done.9.refs_1_), channel_id=1, source_target_pairs={{0,2},{1,3},{2,0},{3,1},{4,6},{5,7},{6,4},{7,5},{8,10},{9,11},{10,... | collective-permute-start | bytes 3244040 | tf_op jit(solution)/shard_map/ppermute | solution.py:419
  60.3 12.9 %collective-permute-start.12 = (bf16[384,512]{1,0:T(8,128)(2,1)}, bf16[384,512]{1,0:T(8,128)(2,1)}, u32[]{:S(2)}, u32[]{:S(2)}) collective-permute-start(bf16[384,512]{1,0:T(8,128)(2,1)} %pad_maximum_fusion.4), channel_id=1, source_target_pairs={{0,1},{1,0},{2,3},{3,2},{4,5},{5,4},{6,7},{7,6},{8,9},{9,8},{10,11... | collective-permute-start | bytes 1179656 | tf_op jit(solution)/shard_map/ppermute | solution.py:498
  61.5 27.7 %collective-permute-start.4 = (bf16[8,8,16,512]{3,2,1,0:T(8,128)(2,1)S(1)}, bf16[8,8,16,512]{3,2,1,0:T(8,128)(2,1)}, u32[]{:S(2)}, u32[]{:S(2)}) collective-permute-start(bf16[8,8,16,512]{3,2,1,0:T(8,128)(2,1)S(1)} %pad_maximum_fusion.1.refs_0_), channel_id=1, source_target_pairs={{0,2},{1,3},{2,0},{3,1},{4,6},{5,7},{6,4},{7,5},{8,10},{9,11},{10,... | collective-permute-start | bytes 3145736 | tf_op jit(solution)/shard_map/ppermute | solution.py:419
  69.6 19.6 %collective-permute-start.5 = (bf16[8,8,16,512]{3,2,1,0:T(8,128)(2,1)}, bf16[8,8,16,512]{3,2,1,0:T(8,128)(2,1)}, u32[]{:S(2)}, u32[]{:S(2)}) collective-permute-start(bf16[8,8,16,512]{3,2,1,0:T(8,128)(2,1)} %collective-permute-done.3.refs_1_), channel_id=1, source_target_pairs={{0,2},{1,3},{2,0},{3,1},{4,6},{5,7},{6,4},{7,5},{8,10},{9,11},{10,... | collective-permute-start | bytes 3145736 | tf_op jit(solution)/shard_map/ppermute | solution.py:419
  73.1 16.1 %collective-permute-start.13 = (bf16[128,512]{1,0:T(8,128)(2,1)S(1)}, bf16[128,512]{1,0:T(8,128)(2,1)S(1)}, u32[]{:S(2)}, u32[]{:S(2)}) collective-permute-start(bf16[128,512]{1,0:T(8,128)(2,1)S(1)} %get-tuple-element.146), channel_id=1, source_target_pairs={{0,1},{1,0},{2,3},{3,2},{4,5},{5,4},{6,7},{7,6},{8,9},{9,8},{10,11... | collective-permute-start | bytes 393224 | tf_op jit(solution)/shard_map/ppermute | solution.py:498
  113.0 12.9 %collective-permute-start.22 = (bf16[16,16,2048]{2,1,0:T(8,128)(2,1)}, bf16[16,16,2048]{2,1,0:T(8,128)(2,1)}, u32[]{:S(2)}, u32[]{:S(2)}) collective-permute-start(bf16[16,16,2048]{2,1,0:T(8,128)(2,1)} %get-tuple-element.82), channel_id=1, source_target_pairs={{0,2},{1,3},{2,0},{3,1},{4,6},{5,7},{6,4},{7,5},{8,10},{9,11},{10,... | collective-permute-start | bytes 3145736 | tf_op jit(solution)/shard_map/ppermute | solution.py:419
  114.3 17.2 %collective-permute-start.14 = (bf16[128,512]{1,0:T(8,128)(2,1)}, bf16[128,512]{1,0:T(8,128)(2,1)S(1)}, u32[]{:S(2)}, u32[]{:S(2)}) collective-permute-start(bf16[128,512]{1,0:T(8,128)(2,1)} %copy-done.15), channel_id=1, source_target_pairs={{0,1},{1,0},{2,3},{3,2},{4,5},{5,4},{6,7},{7,6},{8,9},{9,8},{10,11... | collective-permute-start | bytes 393224 | tf_op jit(solution)/shard_map/ppermute | solution.py:498
  123.8 6.5 %collective-permute-start.15 = (bf16[128,512]{1,0:T(8,128)(2,1)S(1)}, bf16[128,512]{1,0:T(8,128)(2,1)S(1)}, u32[]{:S(2)}, u32[]{:S(2)}) collective-permute-start(bf16[128,512]{1,0:T(8,128)(2,1)S(1)} %get-tuple-element.76), channel_id=1, source_target_pairs={{0,1},{1,0},{2,3},{3,2},{4,5},{5,4},{6,7},{7,6},{8,9},{9,8},{10,11... | collective-permute-start | bytes 393224 | tf_op jit(solution)/shard_map/ppermute | solution.py:498
  125.6 10.3 %collective-permute-start.16 = (bf16[256,512]{1,0:T(8,128)(2,1)S(1)}, bf16[256,512]{1,0:T(8,128)(2,1)S(1)}, u32[]{:S(2)}, u32[]{:S(2)}) collective-permute-start(bf16[256,512]{1,0:T(8,128)(2,1)S(1)} %copy-done.14), channel_id=1, source_target_pairs={{0,1},{1,0},{2,3},{3,2},{4,5},{5,4},{6,7},{7,6},{8,9},{9,8},{10,11... | collective-permute-start | bytes 786440 | tf_op jit(solution)/shard_map/ppermute | solution.py:498
  125.9 15.5 %collective-permute-start.17 = (bf16[16,16,2176]{2,1,0:T(8,128)(2,1)}, bf16[16,16,2176]{2,1,0:T(8,128)(2,1)S(1)}, u32[]{:S(2)}, u32[]{:S(2)}) collective-permute-start(bf16[16,16,2176]{2,1,0:T(8,128)(2,1)} %get-tuple-element.80), channel_id=1, source_target_pairs={{0,2},{1,3},{2,0},{3,1},{4,6},{5,7},{6,4},{7,5},{8,10},{9,11},{10,... | collective-permute-start | bytes 3342344 | tf_op jit(solution)/shard_map/ppermute | solution.py:419
  125.9 29.7 %collective-permute-start.27 = (bf16[16,8,16,512]{3,2,1,0:T(8,128)(2,1)S(1)}, bf16[16,8,16,512]{3,2,1,0:T(8,128)(2,1)S(1)}, u32[]{:S(2)}, u32[]{:S(2)}) collective-permute-start(bf16[16,8,16,512]{3,2,1,0:T(8,128)(2,1)S(1)} %copy-done.23), channel_id=1, source_target_pairs={{0,2},{1,3},{2,0},{3,1},{4,6},{5,7},{6,4},{7,5},{8,10},{9,11},{10,... | collective-permute-start | bytes 6291464 | tf_op jit(solution)/shard_map/ppermute | solution.py:419
  130.3 9.2 %collective-permute-start.23 = (bf16[8,16,2048]{2,1,0:T(8,128)(2,1)S(1)}, bf16[8,16,2048]{2,1,0:T(8,128)(2,1)S(1)}, u32[]{:S(2)}, u32[]{:S(2)}) collective-permute-start(bf16[8,16,2048]{2,1,0:T(8,128)(2,1)S(1)} %get-tuple-element.131), channel_id=1, source_target_pairs={{0,4},{1,5},{2,3},{3,2},{4,0},{5,1},{6,7},{7,6},{8,12},{9,13},{10,... | collective-permute-start | bytes 1572872 | tf_op jit(solution)/shard_map/ppermute | solution.py:419
  139.6 8.4 %collective-permute-start.24 = (bf16[4,16,2048]{2,1,0:T(8,128)(2,1)S(1)}, bf16[4,16,2048]{2,1,0:T(8,128)(2,1)S(1)}, u32[]{:S(2)}, u32[]{:S(2)}) collective-permute-start(bf16[4,16,2048]{2,1,0:T(8,128)(2,1)S(1)} %get-tuple-element.137), channel_id=1, source_target_pairs={{0,1},{1,0},{2,6},{3,7},{4,5},{5,4},{6,2},{7,3},{8,9},{9,8},{10,14... | collective-permute-start | bytes 786440 | tf_op jit(solution)/shard_map/ppermute | solution.py:419
  141.6 10.0 %collective-permute-start.18 = (bf16[8,16,2176]{2,1,0:T(8,128)(2,1)S(1)}, bf16[8,16,2176]{2,1,0:T(8,128)(2,1)S(1)}, u32[]{:S(2)}, u32[]{:S(2)}) collective-permute-start(bf16[8,16,2176]{2,1,0:T(8,128)(2,1)S(1)} %get-tuple-element.127), channel_id=1, source_target_pairs={{0,4},{1,5},{2,3},{3,2},{4,0},{5,1},{6,7},{7,6},{8,12},{9,13},{10,... | collective-permute-start | bytes 1671176 | tf_op jit(solution)/shard_map/ppermute | solution.py:419
  148.0 7.3 %collective-permute-start.25 = (bf16[2,16,2048]{2,1,0:T(8,128)(2,1)S(1)}, bf16[2,16,2048]{2,1,0:T(8,128)(2,1)S(1)}, u32[]{:S(2)}, u32[]{:S(2)}) collective-permute-start(bf16[2,16,2048]{2,1,0:T(8,128)(2,1)S(1)} %get-tuple-element.141), channel_id=1, source_target_pairs={{0,16},{1,17},{2,10},{3,11},{4,20},{5,21},{6,14},{7,15},{8,24},{9,... | collective-permute-start | bytes 393224 | tf_op jit(solution)/shard_map/ppermute | solution.py:419
  151.8 8.3 %collective-permute-start.19 = (bf16[4,16,2176]{2,1,0:T(8,128)(2,1)S(1)}, bf16[4,16,2176]{2,1,0:T(8,128)(2,1)S(1)}, u32[]{:S(2)}, u32[]{:S(2)}) collective-permute-start(bf16[4,16,2176]{2,1,0:T(8,128)(2,1)S(1)} %get-tuple-element.133), channel_id=1, source_target_pairs={{0,1},{1,0},{2,6},{3,7},{4,5},{5,4},{6,2},{7,3},{8,9},{9,8},{10,14... | collective-permute-start | bytes 835592 | tf_op jit(solution)/shard_map/ppermute | solution.py:419
  155.4 6.2 %collective-permute-start.26 = (bf16[1,16,2048]{2,1,0:T(8,128)(2,1)S(1)}, bf16[1,16,2048]{2,1,0:T(8,128)(2,1)S(1)}, u32[]{:S(2)}, u32[]{:S(2)}) collective-permute-start(bf16[1,16,2048]{2,1,0:T(8,128)(2,1)S(1)} %add_convert_fusion.20), channel_id=1, source_target_pairs={{0,8},{1,9},{2,18},{3,19},{4,12},{5,13},{6,22},{7,23},{8,0},{9,1},... | collective-permute-start | bytes 196616 | tf_op jit(solution)/shard_map/ppermute | solution.py:419
  156.6 14.9 %collective-permute-start.28 = (bf16[8,8,16,512]{3,2,1,0:T(8,128)(2,1)S(1)}, bf16[8,8,16,512]{3,2,1,0:T(8,128)(2,1)S(1)}, u32[]{:S(2)}, u32[]{:S(2)}) collective-permute-start(bf16[8,8,16,512]{3,2,1,0:T(8,128)(2,1)S(1)} %get-tuple-element.125), channel_id=1, source_target_pairs={{0,4},{1,5},{2,3},{3,2},{4,0},{5,1},{6,7},{7,6},{8,12},{9,13},{10,... | collective-permute-start | bytes 3145736 | tf_op jit(solution)/shard_map/ppermute | solution.py:419
  160.1 13.7 %collective-permute-start.20 = (bf16[2,16,2176]{2,1,0:T(8,128)(2,1)S(1)}, bf16[2,16,2176]{2,1,0:T(8,128)(2,1)S(1)}, u32[]{:S(2)}, u32[]{:S(2)}) collective-permute-start(bf16[2,16,2176]{2,1,0:T(8,128)(2,1)S(1)} %get-tuple-element.139), channel_id=1, source_target_pairs={{0,16},{1,17},{2,10},{3,11},{4,20},{5,21},{6,14},{7,15},{8,24},{9,... | collective-permute-start | bytes 417800 | tf_op jit(solution)/shard_map/ppermute | solution.py:419
  171.9 9.2 %collective-permute-start.29 = (bf16[4,8,16,512]{3,2,1,0:T(8,128)(2,1)S(1)}, bf16[4,8,16,512]{3,2,1,0:T(8,128)(2,1)S(1)}, u32[]{:S(2)}, u32[]{:S(2)}) collective-permute-start(bf16[4,8,16,512]{3,2,1,0:T(8,128)(2,1)S(1)} %get-tuple-element.129), channel_id=1, source_target_pairs={{0,1},{1,0},{2,6},{3,7},{4,5},{5,4},{6,2},{7,3},{8,9},{9,8},{10,14... | collective-permute-start | bytes 1572872 | tf_op jit(solution)/shard_map/ppermute | solution.py:419
  173.8 11.5 %collective-permute-start.21 = (bf16[1,16,2176]{2,1,0:T(8,128)(2,1)S(1)}, bf16[1,16,2176]{2,1,0:T(8,128)(2,1)S(1)}, u32[]{:S(2)}, u32[]{:S(2)}) collective-permute-start(bf16[1,16,2176]{2,1,0:T(8,128)(2,1)S(1)} %add_convert_fusion.19), channel_id=1, source_target_pairs={{0,8},{1,9},{2,18},{3,19},{4,12},{5,13},{6,22},{7,23},{8,0},{9,1},... | collective-permute-start | bytes 208904 | tf_op jit(solution)/shard_map/ppermute | solution.py:419
  181.3 13.9 %collective-permute-start.30 = (bf16[2,8,16,512]{3,2,1,0:T(8,128)(2,1)S(1)}, bf16[2,8,16,512]{3,2,1,0:T(8,128)(2,1)S(1)}, u32[]{:S(2)}, u32[]{:S(2)}) collective-permute-start(bf16[2,8,16,512]{3,2,1,0:T(8,128)(2,1)S(1)} %get-tuple-element.135), channel_id=1, source_target_pairs={{0,16},{1,17},{2,10},{3,11},{4,20},{5,21},{6,14},{7,15},{8,24},{9,... | collective-permute-start | bytes 786440 | tf_op jit(solution)/shard_map/ppermute | solution.py:419
  195.3 5.0 %collective-permute-start.31 = (bf16[1,8,16,512]{3,2,1,0:T(8,128)(2,1)S(1)}, bf16[1,8,16,512]{3,2,1,0:T(8,128)(2,1)S(1)}, u32[]{:S(2)}, u32[]{:S(2)}) collective-permute-start(bf16[1,8,16,512]{3,2,1,0:T(8,128)(2,1)S(1)} %add_convert_fusion.16), channel_id=1, source_target_pairs={{0,8},{1,9},{2,18},{3,19},{4,12},{5,13},{6,22},{7,23},{8,0},{9,1},... | collective-permute-start | bytes 393224 | tf_op jit(solution)/shard_map/ppermute | solution.py:419
  (25 other events, 187.4 us)

commit v2 on v1

v2 whole, which is shorter than its diff:
```python
import functools

import jax
import jax.numpy as jnp
from jax import lax
from jax.experimental import pallas as pl
from jax.experimental.pallas import tpu as pltpu
from jax.sharding import PartitionSpec as P

D = 512
FF = 2048
HEADS = 8
HEAD_DIM = 64
EPSILON = 1e-05
NEGATIVE = -1000000000.0
SCALE = HEAD_DIM ** (-0.5)
BLOCKS = 32
WIDE = 4096
BF = jnp.bfloat16
F32 = jnp.float32
BOTH = ("batch", "seq")

QKV, OUT, CQ, CKV, CO = (0, 1536), (1536, 2048), (2048, 2560), (2560, 3584), (3584, 4096)


def dot(a, b):
    return lax.dot_general(a, b, (((1,), (0,)), ((), ())), preferred_element_type=F32)


def dot_nt(a, b):
    return lax.dot_general(a, b, (((1,), (1,)), ((), ())), preferred_element_type=F32)


def dot_tn(a, b):
    return lax.dot_general(a, b, (((0,), (0,)), ((), ())), preferred_element_type=F32)


def norm(values):
    centred = values - jnp.mean(values, axis=-1, keepdims=True)
    rate = lax.rsqrt(jnp.mean(centred * centred, axis=-1, keepdims=True) + EPSILON)
    return centred * rate, rate


def norm_back(values, gain, grad):
    unit, rate = norm(values)
    scaled = grad * gain
    part = rate * (
        scaled
        - jnp.mean(scaled, axis=-1, keepdims=True)
        - unit * jnp.mean(scaled * unit, axis=-1, keepdims=True)
    )
    return part, row_sum(grad * unit), row_sum(grad)


def row_sum(values):
    return jnp.sum(values.astype(F32), axis=0, keepdims=True)


def lane_masks(dtype):
    lane = lax.broadcasted_iota(jnp.int32, (1, 128), 1)
    return [(lane // HEAD_DIM == j).astype(dtype) for j in range(2)]


def scores_t(keys, queries, visible):
    return jnp.where(visible, dot_nt(keys, queries) * SCALE, NEGATIVE)


def attend(q_ref, k_ref, v_ref, visible, mixed_ref, log_ref):
    masks = lane_masks(BF)
    for pair in range(HEADS // 2):
        cols = slice(128 * pair, 128 * pair + 128)
        queries, keys, values = q_ref[:, cols], k_ref[:, cols], v_ref[:, cols]
        total = None
        for j in range(2):
            scores = scores_t(keys, queries * masks[j], visible)
            top = jnp.max(scores, axis=0, keepdims=True)
            exponent = jnp.exp(scores - top)
            row_total = jnp.sum(exponent, axis=0, keepdims=True)
            probs = (exponent * (1.0 / row_total)).astype(BF)
            log_ref[2 * pair + j : 2 * pair + j + 1, :] = top + jnp.log(row_total)
            part = dot_tn(probs, values * masks[j])
            total = part if total is None else total + part
        mixed_ref[:, cols] = total.astype(BF)


def attend_back(q_ref, k_ref, v_ref, visible, log_ref, grad_ref, dq_ref, dk_ref, dv_ref):
    masks = lane_masks(BF)
    for pair in range(HEADS // 2):
        cols = slice(128 * pair, 128 * pair + 128)
        queries, keys, values, grads = q_ref[:, cols], k_ref[:, cols], v_ref[:, cols], grad_ref[:, cols]
        dq = dk = dv = None
        for j in range(2):
            own_q, own_k, own_g = queries * masks[j], keys * masks[j], grads * masks[j]
            scores = scores_t(keys, own_q, visible)
            probs = jnp.exp(scores - log_ref[2 * pair + j : 2 * pair + j + 1, :])
            grad_probs = dot_nt(values, own_g)
            part_v = dot(probs.astype(BF), own_g)
            inner = jnp.sum(probs * grad_probs, axis=0, keepdims=True)
            low = (probs * (grad_probs - inner)).astype(BF)
            part_k = dot(low, own_q)
            part_q = dot_tn(low, own_k)
            dq = part_q if dq is None else dq + part_q
            dk = part_k if dk is None else dk + part_k
            dv = part_v if dv is None else dv + part_v
        dq_ref[:, cols] = (dq * SCALE).astype(BF)
        dk_ref[:, cols] = (dk * SCALE).astype(BF)
        dv_ref[:, cols] = dv.astype(BF)


def place_blocks(order, base, pieces, put):
    for i, piece in enumerate(pieces):
        if piece is None:
            continue
        count = piece.shape[0]

        @pl.loop(0, count)
        def _(b, piece=piece, first=base + i * count):
            put(piece, b, order[first + b])


def rows16(index):
    return pl.ds(pl.multiple_of(index * 16, 16), 16)


def halves(ref, place, rows):
    own = pl.ds(pl.multiple_of(place * rows, rows), rows)
    other = pl.ds(pl.multiple_of((1 - place) * rows, rows), rows)
    return ref.at[own], ref.at[other]


def self_visible(length, rows):
    key = lax.broadcasted_iota(jnp.int32, (rows, rows), 0)
    query = lax.broadcasted_iota(jnp.int32, (rows, rows), 1)
    return (key <= query) & (key < length)


def cross_visible(mask):
    row = jnp.broadcast_to(mask[...].astype(F32), (8, mask.shape[1]))
    column = row.T[:, 0:1]
    return (column > 0) | (lax.broadcasted_iota(jnp.int32, column.shape, 0) == 0)


def pack_kernel(
    me, all_lengths, all_units, gains, biases, qkv, out, cq, ckv, co, up, down, hidden, memory, grads, masks,
    order, info, attention, w_up, w_down, sent, kept, mask, token, rows, gain_rows, bias_rows, lengths, units, sems,
):
    index = me[0]
    core = (index // 2) % 2
    place = index % 2
    far = 1 - place
    moves = [(gains, gain_rows), (biases, bias_rows), (masks.at[pl.ds(place, 1)], mask), (up, w_up), (down, w_down)]
    moves += [(all_lengths, lengths), (all_units, units)]
    first = 0
    for part in (hidden, memory, grads):
        last = first + part.shape[1]
        moves.append((part.at[far], sent.at[first:last]))
        moves.append((part.at[place], kept.at[first:last]))
        first = last
    first = 0
    for part in (qkv, out, cq, ckv, co):
        width = part.shape[1]
        moves.append((part, attention.at[0, :, first : first + width]))
        first += width
    moves = [pltpu.make_async_copy(a, b, sems.at[i]) for i, (a, b) in enumerate(moves)]
    for move in moves:
        move.start()
    info[0] = place
    for kind, both in enumerate(FLIPS):
        for k in range(16):
            plane = [sum(((k >> b) & 1) * flip for b, flip in enumerate(flips)) for flips in both]
            order[BLOCKS * kind + k] = index ^ jnp.where(core == 0, plane[0], plane[1])
            order[BLOCKS * kind + 16 + k] = index ^ jnp.where(core == 0, plane[1] | 2, plane[0] | 2)
    token[...] = jnp.zeros_like(token)
    rows[...] = jnp.zeros_like(rows)
    lane = lax.broadcasted_iota(jnp.int32, (16, 128), 1)
    spread = (lane % 16 == lax.broadcasted_iota(jnp.int32, (16, 128), 0)).astype(BF)
    unit_lane = lax.broadcasted_iota(jnp.int32, (64, 128), 1)
    unit_spread = (unit_lane % 64 == lax.broadcasted_iota(jnp.int32, (64, 128), 0)).astype(BF)
    for move in moves:
        move.wait()
    info[1] = lengths[place]
    rows[13:14, :] = dot(jnp.broadcast_to(units[...], (16, 64)), unit_spread)[0:1, :]
    rows[0:10, :] = dot_tn(bias_rows[...], spread)
    rows[10:13, :] = dot(gain_rows[...], spread)
    attention[0, :, WIDE : WIDE + 128] = rows[...].astype(BF)


def join_kernel(have, got, extra, joined):
    count = have.shape[0]
    joined[0:count] = have[...]
    joined[count:] = got[...]


def pass_kernel(value, out):
    out[...] = value[...]


def add_kernel(own, got, send, keep):
    count = send.shape[0]
    send[...] = (own[count:].astype(F32) + got[count:].astype(F32)).astype(send.dtype)
    keep[...] = (own[:count].astype(F32) + got[:count].astype(F32)).astype(keep.dtype)


def last_kernel(own, got, out):
    out[...] = own[0] + got[0].astype(F32)


def last_cross_kernel(own, got, d_cq, d_ckv, d_co, d_out):
    total = own[0] + got[0].astype(F32)
    d_cq[...] = total[:, 0:512]
    d_ckv[...] = total[:, 512:1536]
    d_co[...] = total[:, 1536:2048]
    d_out[...] = total[:, 2048:2560]


def last_self_kernel(me, own, got, d_qkv, d_gains, d_biases, d_units):
    total = own[0] + got[0].astype(F32)
    d_qkv[...] = total[:, 0:1536]
    small = total[:, 1536:1664]
    index = me[0]
    vectors = pltpu.roll(small, (128 - 16 * (index % 8)) % 128, 1)[:, 0:16]
    d_gains[...] = vectors[10:13, :]
    d_biases[...] = vectors.T[:, 0:10]
    d_units[...] = pltpu.roll(small, (128 - 64 * (index % 2)) % 128, 1)[13:14, 0:64]


def halves_kernel(info, kept, got, out):
    place = info[0]
    out[place] = kept[...]
    out[1 - place] = got[...].astype(out.dtype)


def self_forward_kernel(
    base, order, info, p0, p1, p2, p3, kept, new, weights, vecs, ffb, x0, normed1, q, k, v, mixed1, log1, x1, normed2,
    small,
):
    place, length = info[0], info[1]

    def put(piece, b, index):
        weights[rows16(index), :] = piece[b, :, 0:2048]
        small[index] = piece[b, :, WIDE : WIDE + 128]

    place_blocks(order, base, (p0, p1, p2, p3), put)
    rows = x0.shape[0] // 2
    own, other = halves(x0, place, rows)
    own[...], other[...] = kept[0:rows], new[0:rows]
    hidden = x0[...].astype(F32)
    lane = lax.broadcasted_iota(jnp.int32, (16, 128), 1)
    for tile in range(D // 128):
        row = jnp.zeros((16, 128), F32)
        for i in range(8):
            row = jnp.where(lane // 16 == i, small[8 * tile + i].astype(F32), row)
        vecs[:, 128 * tile : 128 * tile + 128] = row
    ffb[...] = jnp.zeros_like(ffb)
    for tile in range(FF // 128):
        row = jnp.where(lane < 64, small[2 * tile].astype(F32), small[2 * tile + 1].astype(F32))
        ffb[tile // 4 : tile // 4 + 1, 128 * (tile % 4) : 128 * (tile % 4) + 128] = row[13:14, :]

    def bias(j):
        return vecs[j : j + 1, :]

    normed1[...] = (norm(hidden)[0] * bias(10) + bias(0)).astype(BF)
    q[...] = (dot(normed1[...], weights[:, 0:512]) + bias(1)).astype(BF)
    k[...] = dot(normed1[...], weights[:, 512:1024]).astype(BF)
    v[...] = (dot(normed1[...], weights[:, 1024:1536]) + bias(2)).astype(BF)
    attend(q, k, v, self_visible(length, 2 * rows), mixed1, log1)
    after_self = hidden + (dot(mixed1[...], weights[:, 1536:2048]) + bias(3))
    x1[...] = after_self
    normed2[...] = (norm(after_self)[0] * bias(11) + bias(4)).astype(BF)


def cross_forward_kernel(
    base, order, info, p0, p1, p2, p3, kept, new, mask, vecs, x1, normed2,
    weights, mem, cq, ck, cv, mixed2, log2, x2, normed3,
):
    place = info[0]

    def put(piece, b, index):
        weights[rows16(index), :] = piece[b, :, 2048:4096]

    place_blocks(order, base, (p0, p1, p2, p3), put)
    sources = mem.shape[0] // 2
    first = x1.shape[0] // 2
    own, other = halves(mem, place, sources)
    own[...], other[...] = kept[first : first + sources], new[first : first + sources]

    def bias(j):
        return vecs[j : j + 1, :]

    ck[...] = dot(mem[...], weights[:, 512:1024]).astype(BF)
    cv[...] = (dot(mem[...], weights[:, 1024:1536]) + bias(6)).astype(BF)
    cq[...] = (dot(normed2[...], weights[:, 0:512]) + bias(5)).astype(BF)
    attend(cq, ck, cv, cross_visible(mask), mixed2, log2)
    after_cross = x1[...] + (dot(mixed2[...], weights[:, 1536:2048]) + bias(7))
    x2[...] = after_cross
    normed3[...] = (norm(after_cross)[0] * bias(12) + bias(8)).astype(BF)


def four_rows(index):
    return pl.ds(pl.multiple_of(index * 4, 4), 4)


def ffn_kernel(
    bases, order, info, u0, u1, u2, u3, w0, w1, w2, w3, x2, normed3, kept, new, vecs, ffb,
    out_keep, out_send, up, grad_hidden, grad_out, own_out, other_out,
    down, d_down, result,
):
    place = info[0]

    def put_up(piece, b, index):
        up[rows16(index), :] = piece[b]

    def put_down(piece, b, index):
        down[four_rows(index)] = piece[b]

    place_blocks(order, bases[0], (u0, u1, u2, u3), put_up)
    place_blocks(order, bases[1], (w0, w1, w2, w3), put_down)
    rows = out_keep.shape[0]
    first = kept.shape[0] - rows
    own, other = halves(grad_out, place, rows)
    own[...], other[...] = kept[first:], new[first:]
    grads = grad_out[...]
    normed = normed3[...]
    total = None
    c0 = (2.0 / jnp.pi) ** 0.5
    for group in range(FF // 512):
        w_down = down[32 * group : 32 * group + 32].reshape(512, D)
        hidden = dot(normed, up[:, 512 * group : 512 * group + 512]) + ffb[group : group + 1, :]
        square = hidden * hidden
        tanh = jnp.tanh(c0 * (hidden + 0.044715 * (square * hidden)))
        half = 0.5 * (1.0 + tanh)
        active = (hidden * half).astype(BF)
        slope = half + hidden * (0.5 * c0) * (1.0 - tanh * tanh) * (1.0 + (3 * 0.044715) * square)
        part = dot(active, w_down)
        total = part if total is None else total + part
        grad_hidden[:, 512 * group : 512 * group + 512] = (slope * dot_nt(grads, w_down)).astype(BF)
        d_down[32 * group : 32 * group + 32] = dot_tn(active, grads).astype(BF).reshape(32, 16, D)
    take_blocks(order, bases[2], (own_out, other_out), lambda index: d_down[four_rows(index)])
    result[...] = (x2[...] + (total + vecs[9:10, :])).astype(BF)
    own, other = halves(result, place, rows)
    out_keep[...], out_send[...] = own[...], other[...]


def ffn_back_kernel(
    base, order, info, up, grad_hidden, grad_out, x2, normed3, vecs, grad_x2, small, ffg, own_out, other_out, d_up
):
    normed_t = normed3[...].T
    grad_normed = None
    ffg[...] = jnp.zeros_like(ffg)
    for group in range(FF // 512):
        grad = grad_hidden[:, 512 * group : 512 * group + 512]
        d_up[:, 512 * group : 512 * group + 512] = dot(normed_t, grad).astype(BF)
        ffg[group : group + 1, :] = row_sum(grad)
        part = dot_nt(grad, up[:, 512 * group : 512 * group + 512])
        grad_normed = part if grad_normed is None else grad_normed + part
    take_blocks(order, base, (own_out, other_out), lambda index: d_up[rows16(index), :])
    part, d_gain, d_shift = norm_back(x2[...], vecs[12:13, :], grad_normed)
    grads = grad_out[...]
    grad_x2[...] = grads.astype(F32) + part
    small[...] = jnp.zeros_like(small)
    small[12:13, :] = d_gain
    small[8:9, :] = d_shift
    small[9:10, :] = row_sum(grads)


def cross_back_kernel(
    base, order, info, weights, weights1, x1, normed2, mem, cq, ck, cv, mixed1, mixed2, log2, mask, grad_x2, vecs, small_in,
    grad_x1, grad_mixed1, mem_keep, mem_send, small, own_out, other_out,
    d_weights, grad_mixed, dq, dk, dv, grad_mem,
):
    place = info[0]
    small[...] = small_in[...]
    grad_y = grad_x2[...].astype(BF)
    d_weights[:, 1536:2048] = dot_tn(mixed2[...], grad_y).astype(BF)
    small[7:8, :] = row_sum(grad_y)
    grad_mixed[...] = dot_nt(grad_y, weights[:, 1536:2048]).astype(BF)
    attend_back(cq, ck, cv, cross_visible(mask), log2, grad_mixed, dq, dk, dv)
    memory_t = mem[...].T
    d_weights[:, 512:1024] = dot(memory_t, dk[...]).astype(BF)
    d_weights[:, 1024:1536] = dot(memory_t, dv[...]).astype(BF)
    d_weights[:, 0:512] = dot_tn(normed2[...], dq[...]).astype(BF)
    small[6:7, :] = row_sum(dv[...])
    small[5:6, :] = row_sum(dq[...])
    grad_mem[...] = dot_nt(dk[...], weights[:, 512:1024]) + dot_nt(dv[...], weights[:, 1024:1536])
    own, other = halves(grad_mem, place, mem_keep.shape[0])
    mem_keep[...] = own[...]
    mem_send[...] = other[...].astype(BF)
    part, d_gain, d_shift = norm_back(x1[...], vecs[11:12, :], dot_nt(dq[...], weights[:, 0:512]))
    small[11:12, :] = d_gain
    small[4:5, :] = d_shift
    total = grad_x2[...] + part
    grad_x1[...] = total
    grad_y = total.astype(BF)
    d_weights[:, 2048:2560] = dot_tn(mixed1[...], grad_y).astype(BF)
    small[3:4, :] = row_sum(grad_y)
    grad_mixed1[...] = dot_nt(grad_y, weights1[:, 1536:2048]).astype(BF)
    take_blocks(order, base, (own_out, other_out), lambda index: d_weights[rows16(index), :])


def self_back_kernel(
    base, order, info, weights, x0, normed1, q, k, v, log1, grad_x1, grad_mixed, vecs, small_in, ffg,
    in_keep, in_send, own_out, other_out,
    d_weights, d_small, small, dq, dk, dv, grad_in,
):
    place, length = info[0], info[1]
    small[...] = small_in[...]
    rows = q.shape[0]
    attend_back(q, k, v, self_visible(length, rows), log1, grad_mixed, dq, dk, dv)
    normed_t = normed1[...].T
    for i, part in enumerate((dq, dk, dv)):
        d_weights[:, 512 * i : 512 * i + 512] = dot(normed_t, part[...]).astype(BF)
    small[1:2, :] = row_sum(dq[...])
    small[2:3, :] = row_sum(dv[...])
    grad_normed = (
        dot_nt(dq[...], weights[:, 0:512])
        + dot_nt(dk[...], weights[:, 512:1024])
        + dot_nt(dv[...], weights[:, 1024:1536])
    )
    part, d_gain, d_shift = norm_back(x0[...].astype(F32), vecs[10:11, :], grad_normed)
    small[10:11, :] = d_gain
    small[0:1, :] = d_shift
    for index in range(BLOCKS):
        tile = 128 * (index // 8)
        d_small[index] = small[:, tile : tile + 128].astype(BF)
        group, tile = index // 8, 128 * ((index // 2) % 4)
        d_small[index, 13:14, :] = ffg[group : group + 1, tile : tile + 128].astype(BF)
    first = base
    for out in (own_out, other_out):
        if out is None:
            continue

        @pl.loop(0, out.shape[0])
        def _(b, out=out, first=first):
            index = order[first + b]
            out[b, :, 0:1536] = d_weights[rows16(index), :]
            out[b, :, 1536:1664] = d_small[index]

        first += out.shape[0]
    grad_in[...] = grad_x1[...] + part
    own, other = halves(grad_in, place, rows // 2)
    in_keep[...] = own[...]
    in_send[...] = other[...].astype(BF)


def take_blocks(order, base, outs, take):
    first = base
    for out in outs:
        if out is None:
            continue

        @pl.loop(0, out.shape[0])
        def _(b, out=out, first=first):
            out[b] = take(order[first + b])

        first += out.shape[0]


VMEM = pl.BlockSpec(memory_space=pltpu.VMEM)
SMEM = pl.BlockSpec(memory_space=pltpu.SMEM)
HBM = pl.BlockSpec(memory_space=pltpu.HBM)


def shape(dims, dtype):
    return jax.ShapeDtypeStruct(dims, dtype)


EVENT = 1_000_000_000


class Line:
    def __init__(self):
        self.token = None

    def call(self, kernel, name, inputs, outs, scratch=(), scalars=0, flops=1):
        given = [i for i in inputs if i is not None]
        made = [o for o in outs if o is not None]
        tokens = [self.token] if self.token is not None else []

        def body(*refs):
            refs = list(refs)
            taken = [None if i is None else refs.pop(0) for i in inputs]
            for _ in tokens:
                refs.pop(0)
            given_out = [None if o is None else refs.pop(0) for o in outs]
            out_token = refs.pop(0)
            out_token[...] = jnp.zeros_like(out_token)
            kernel(*taken, *given_out, *refs)

        moved = sum(a.size * a.dtype.itemsize for a in given)
        *results, self.token = pl.pallas_call(
            body,
            name=name,
            out_shape=[shape(*o) for o in made] + [shape((8, 128), F32)],
            in_specs=[SMEM] * scalars + [VMEM] * (len(given) - scalars + len(tokens)),
            out_specs=[VMEM] * (len(made) + 1),
            scratch_shapes=list(scratch),
            compiler_params=pltpu.CompilerParams(vmem_limit_bytes=32 * 1024 * 1024),
            cost_estimate=pl.CostEstimate(flops=flops, bytes_accessed=1, transcendentals=0),
        )(*given, *tokens)
        results = iter(results)
        return [None if o is None else next(results) for o in outs]


def flat_index(z, y, c, x):
    return ((z * 2 + y) * 2 + c) * 2 + x


def pairs_of(move):
    pairs = []
    for z in range(4):
        for y in range(2):
            for c in range(2):
                for x in range(2):
                    pairs.append((flat_index(z, y, c, x), flat_index(*move(z, y, c, x))))
    return pairs


CORE = pairs_of(lambda z, y, c, x: (z, y, 1 - c, x))
SIDE = pairs_of(lambda z, y, c, x: (z, y, c, 1 - x))
HOP_Z1 = pairs_of(lambda z, y, c, x: (z ^ 1 if c == 0 else z ^ 2, y, c, x))
HOP_Z2 = pairs_of(lambda z, y, c, x: (z ^ 2 if c == 0 else z ^ 1, y, c, x))
HOP_P1 = pairs_of(lambda z, y, c, x: (z, y, c, 1 - x) if c == 0 else (z, 1 - y, c, x))
HOP_P2 = pairs_of(lambda z, y, c, x: (z, y, c, 1 - x) if c == 1 else (z, 1 - y, c, x))
HOPS = (
    (HOP_Z1, HOP_Z2, HOP_P1, HOP_P2),
    (HOP_P1, HOP_P2, HOP_Z1, HOP_Z2),
    (HOP_P1, HOP_Z1, HOP_Z2, HOP_P2),
)
FLIPS = (
    ((8, 16, 1, 4), (16, 8, 4, 1)),
    ((1, 4, 8, 16), (4, 1, 16, 8)),
    ((1, 8, 16, 4), (4, 16, 8, 1)),
)
GATHER_KIND = dict(a=0, u=0, w=1)
GATHER = "a:12 w:12 u:12 a:12 w:12 u:12 a:12 w:12 u:12"
SCATTER_KIND = dict(d=2, u=2, c=0, s=0)
SCATTER = (
    "d:0 u:0 X:0 Y:0 d:12 s:3 u:0 c:0 d:0.3 o:4 s:0.6 c:0 u:0 s:0.3 d:1.5"
    " c:0 u:0 d:0.6 s:1.5 u:0 c:0 h:0 s:1 m:0 c:0"
)


def plan(text):
    return [(item.split(":")[0], int(float(item.split(":")[1]) * EVENT) + 1) for item in text.split()]


def permute(value, pairs):
    return lax.ppermute(value, BOTH, pairs)


class Gather:
    def __init__(self, line, name, own):
        self.line, self.name, self.have, self.hop = line, name, own, 0
        self.hops = HOPS[GATHER_KIND[name]]

    def start(self):
        with jax.named_scope(f"gather_{self.name}_hop{self.hop}"):
            self.coming = permute(self.have, self.hops[self.hop])
        self.hop += 1
        if self.hop == 4:
            with jax.named_scope(f"gather_{self.name}_core0"):
                self.core = permute(self.have, CORE)

    def step(self, extra, cost):
        dims = self.have.shape
        (self.have,) = self.line.call(
            join_kernel, f"join_{self.name}{self.hop}", [self.have, self.coming, extra],
            [((2 * dims[0],) + dims[1:], BF)], flops=cost,
        )
        self.start()

    def finish(self, tied=False):
        if tied:
            (self.coming,) = self.line.call(
                pass_kernel, f"pass_{self.name}", [self.coming], [(self.coming.shape, BF)], flops=12 * EVENT
            )
        with jax.named_scope(f"gather_{self.name}_core1"):
            return [self.have, self.coming, self.core, permute(self.coming, CORE)]


class Scatter:
    def __init__(self, line, name, own, other):
        self.line, self.name, self.own, self.hop = line, name, own, 4
        self.hops = HOPS[SCATTER_KIND[name]]
        with jax.named_scope(f"scatter_{name}_core"):
            self.coming = permute(other, CORE)

    def step(self, cost):
        self.hop -= 1
        dims = (1 << self.hop,) + self.own.shape[1:]
        send, self.own = self.line.call(
            add_kernel, f"add_{self.name}{self.hop}", [self.own, self.coming],
            [(dims, BF), (dims, BF if self.hop else F32)], flops=cost,
        )
        with jax.named_scope(f"scatter_{self.name}_hop{self.hop}"):
            self.coming = permute(send, self.hops[self.hop])


def small_rows(biases, gains, ffn_bias):
    count = biases.shape[0]
    columns = jnp.concatenate([biases, gains], axis=2).transpose(0, 2, 1)
    rows = jnp.tile(columns, (1, 1, 8))
    units = jnp.tile(ffn_bias.reshape(count, 1, 64), (1, 1, 2))
    return jnp.concatenate([rows, units, jnp.zeros((count, 2, 128), BF)], axis=1)


def pack_attention(qkv, out, cq, ckv, co, small):
    return jnp.concatenate([qkv, out, cq, ckv, co, small], axis=2)


def packed(hidden_in, memory, lengths, source_mask, grad_out, params, me):
    (w_qkv, w_out, w_cq, w_ckv, w_co, w_up, w_down, gains, biases, ffn_bias) = params
    rows = 2 * hidden_in.shape[1] + memory.shape[1]
    return pl.pallas_call(
        pack_kernel,
        name="pack",
        out_shape=[
            shape((len(FLIPS) * BLOCKS,), jnp.int32), shape((2,), jnp.int32), shape((1, 16, WIDE + 128), BF),
            shape((16, FF), BF), shape((64, D), BF), shape((rows, D), BF), shape((rows, D), BF),
            shape((1, source_mask.shape[1]), jnp.int32), shape((8, 128), F32),
        ],
        in_specs=[SMEM] + [HBM] * 15,
        out_specs=[SMEM, SMEM] + [VMEM] * 7,
        scratch_shapes=[
            pltpu.VMEM((16, 128), F32), pltpu.VMEM((3, 16), BF), pltpu.VMEM((16, 10), BF),
            pltpu.SMEM(lengths.shape, jnp.int32), pltpu.VMEM((1, 64), BF), pltpu.SemaphoreType.DMA((18,)),
        ],
        compiler_params=pltpu.CompilerParams(vmem_limit_bytes=16 * 1024 * 1024),
    )(
        me,
        *(
            pltpu.with_memory_space_constraint(v, pltpu.HBM)
            for v in (
                lengths, ffn_bias.reshape(1, 64), gains.T, biases, w_qkv, w_out, w_cq, w_ckv, w_co, w_up, w_down, hidden_in, memory, grad_out, source_mask,
            )
        ),
    )


def per_device(n_devices, hidden_in, memory, lengths, source_mask, grad_out, *params):
    permuted = n_devices == BLOCKS
    rows, sources = hidden_in.shape[1], memory.shape[1]
    tgt, src = 2 * rows, 2 * sources
    line = Line()

    def swap(value, name):
        with jax.named_scope(f"swap_{name}"):
            return lax.ppermute(value, "seq", [(0, 1), (1, 0)])

    place = lax.axis_index("seq")
    if permuted:
        me = lax.axis_index(BOTH).astype(jnp.int32).reshape(1)
        order, info, attention, w_up, w_down, sent, kept, mask, line.token = packed(
            hidden_in, memory, lengths, source_mask, grad_out, params, me
        )
        chunks = dict(
            a=Gather(line, "a", attention), w=Gather(line, "w", w_down.reshape(1, 4, 16, D)),
            u=Gather(line, "u", w_up[None]),
        )
        chunks["a"].start()
        chunks["w"].start()
        new = swap(sent, "in")
        chunks["u"].start()
        for name, cost in plan(GATHER):
            chunks[name].step(new if name == "a" and chunks[name].hop == 2 else None, cost)
        a_pieces = chunks["a"].finish()
        halves_of = (16, 16)
        base = lambda kind: BLOCKS * kind
    else:
        params = [lax.all_gather(p, BOTH, axis=0, tiled=True) for p in params]
        (w_qkv, w_out, w_cq, w_ckv, w_co, w_up, w_down, gains, biases, ffn_bias) = params
        cut = lambda w: w.reshape(BLOCKS, -1, w.shape[1])
        attention = pack_attention(
            *(cut(w) for w in (w_qkv, w_out, w_cq, w_ckv, w_co)), small_rows(cut(biases), cut(gains), ffn_bias)
        )
        pick = lambda v, i: lax.dynamic_index_in_dim(v, i, 0, keepdims=False)
        both_of = lambda i: jnp.concatenate([pick(v, i) for v in (hidden_in, memory, grad_out)], axis=0)
        kept, new = both_of(place), swap(both_of(1 - place), "in")
        mask = pick(source_mask, place)[None]
        info = jnp.stack([place, pick(lengths, place)]).astype(jnp.int32)
        order = jnp.arange(BLOCKS, dtype=jnp.int32)
        a_pieces = [attention, None, None, None]
        halves_of = (BLOCKS, None)
        base = lambda kind: 0

    wide = (tgt, D)
    vec = ((16, D), F32)
    units = ((8, 512), F32)
    blocks = lambda *dims: [None if n is None else ((n,) + dims, BF) for n in halves_of]
    weights1, vecs, ffb, x0, normed1, q, k, v, mixed1, log1, x1, normed2 = line.call(
        functools.partial(self_forward_kernel, base(GATHER_KIND["a"])), "self_forward", [order, info, *a_pieces, kept, new],
        [
            ((D, 2048), BF), vec, units, (wide, BF), (wide, BF), (wide, BF), (wide, BF), (wide, BF), (wide, BF),
            ((HEADS, tgt), F32), (wide, F32), (wide, BF),
        ],
        [pltpu.VMEM((BLOCKS, 16, 128), BF)], 2,
    )
    weights2, mem, cq, ck, cv, mixed2, log2, x2, normed3 = line.call(
        functools.partial(cross_forward_kernel, base(GATHER_KIND["a"])), "cross_forward",
        [order, info, *a_pieces, kept, new, mask, vecs, x1, normed2],
        [
            ((D, 2048), BF), ((src, D), BF), (wide, BF), ((src, D), BF), ((src, D), BF), (wide, BF),
            ((HEADS, tgt), F32), (wide, F32), (wide, BF),
        ],
        [], 2,
    )
    if permuted:
        w_pieces, u_pieces = chunks["w"].finish(True), chunks["u"].finish(True)
    else:
        u_pieces, w_pieces = [cut(w_up), None, None, None], [w_down.reshape(BLOCKS, 4, 16, D), None, None, None]
    bases = (base(GATHER_KIND["u"]), base(GATHER_KIND["w"]), base(SCATTER_KIND["d"]))
    out_keep, out_send, up, grad_hidden, g_full, *d_down = line.call(
        functools.partial(ffn_kernel, bases), "ffn",
        [order, info, *u_pieces, *w_pieces, x2, normed3, kept, new, vecs, ffb],
        [((rows, D), BF), ((rows, D), BF), ((D, FF), BF), ((tgt, FF), BF), (wide, BF), *blocks(4, 16, D)],
        [pltpu.VMEM((128, 16, D), BF), pltpu.VMEM((128, 16, D), BF), pltpu.VMEM(wide, BF)], 2,
    )
    if permuted:
        chunks = dict(d=Scatter(line, "d", *d_down))
        out_got = swap(out_send, "out")
    grad_x2, small, ffg, *d_up = line.call(
        functools.partial(ffn_back_kernel, base(SCATTER_KIND["u"])), "ffn_back",
        [order, info, up, grad_hidden, g_full, x2, normed3, vecs],
        [(wide, F32), vec, units, *blocks(16, FF)],
        [pltpu.VMEM((D, FF), BF)], 2,
    )

    def cross_back():
        return line.call(
            functools.partial(cross_back_kernel, base(SCATTER_KIND["c"])), "cross_back",
            [
                order, info, weights2, weights1, x1, normed2, mem, cq, ck, cv, mixed1, mixed2, log2, mask, grad_x2,
                vecs, small,
            ],
            [(wide, F32), (wide, BF), ((sources, D), F32), ((sources, D), BF), vec, *blocks(16, 2560)],
            [
                pltpu.VMEM((D, 2560), BF), pltpu.VMEM(wide, BF), pltpu.VMEM(wide, BF),
                pltpu.VMEM((src, D), BF), pltpu.VMEM((src, D), BF), pltpu.VMEM((src, D), F32),
            ],
            2,
        )

    def self_back(grad_x1, grad_mixed1, small):
        return line.call(
            functools.partial(self_back_kernel, base(SCATTER_KIND["s"])), "self_back",
            [order, info, weights1, x0, normed1, q, k, v, log1, grad_x1, grad_mixed1, vecs, small, ffg],
            [((rows, D), F32), ((rows, D), BF), *blocks(16, 1664)],
            [
                pltpu.VMEM((D, 1536), BF), pltpu.VMEM((BLOCKS, 16, 128), BF), pltpu.VMEM((16, D), F32),
                pltpu.VMEM(wide, BF), pltpu.VMEM(wide, BF), pltpu.VMEM(wide, BF), pltpu.VMEM(wide, F32),
            ],
            2,
        )

    def both(kept, got, name):
        return line.call(halves_kernel, f"halves_{name}", [info, kept, got], [((2,) + kept.shape, kept.dtype)], (), 1)[0]

    if permuted:
        chunks["u"] = Scatter(line, "u", *d_up)
        lasts = dict(
            d=(last_kernel, [((4, 16, D), F32)]),
            u=(last_kernel, [((16, FF), F32)]),
            c=(last_cross_kernel, [((16, n), F32) for n in (512, 1024, 512, 512)]),
            s=(last_self_kernel, [((16, 1536), F32), ((3, 16), F32), ((16, 10), F32), ((1, 64), F32)]),
        )
        done = {}
        for name, cost in plan(SCATTER):
            if name == "X":
                grad_x1, grad_mixed1, mem_keep, mem_send, small, *d_cross = cross_back()
                chunks["c"] = Scatter(line, "c", *d_cross)
                mem_got = swap(mem_send, "memory")
            elif name == "Y":
                in_keep, in_send, *d_self = self_back(grad_x1, grad_mixed1, small)
                chunks["s"] = Scatter(line, "s", *d_self)
                in_got = swap(in_send, "hidden")
            elif name == "o":
                output = both(out_keep, out_got, "out")
            elif name == "m":
                grad_memory = both(mem_keep, mem_got, "memory")
            elif name == "h":
                grad_hidden_in = both(in_keep, in_got, "hidden")
            elif chunks[name].hop:
                chunks[name].step(cost)
            else:
                kernel, shapes = lasts[name]
                mine = [me] if name == "s" else []
                done[name] = line.call(
                    kernel, f"last_{name}", [*mine, chunks[name].own, chunks[name].coming], shapes,
                    scalars=len(mine), flops=cost,
                )
        g_cq, g_ckv, g_co, g_out = done["c"]
        g_qkv, g_gains, g_biases, g_units = done["s"]
        rest = (
            g_qkv, g_out, g_cq, g_ckv, g_co, done["u"][0], done["d"][0].reshape(64, D), g_gains.T, g_biases,
            g_units.reshape(64),
        )
    else:
        grad_x1, grad_mixed1, mem_keep, mem_send, small, *d_cross = cross_back()
        in_keep, in_send, *d_self = self_back(grad_x1, grad_mixed1, small)
        output = both(out_keep, swap(out_send, "out"), "out")
        grad_memory = both(mem_keep, swap(mem_send, "memory"), "memory")
        grad_hidden_in = both(in_keep, swap(in_send, "hidden"), "hidden")
        d_down, d_up, d_cross, d_self = (d[0].astype(F32) for d in (d_down, d_up, d_cross, d_self))
        d_small = d_self[:, :, 1536:]
        columns = jnp.concatenate([d_small[i, :13, 16 * (i % 8) : 16 * (i % 8) + 16].T for i in range(BLOCKS)])
        d_unit = jnp.concatenate([d_small[i, 13, 64 * (i % 2) : 64 * (i % 2) + 64] for i in range(BLOCKS)])
        d_cross = d_cross.reshape(D, 2560)
        rest = tuple(
            lax.psum_scatter(d, BOTH, scatter_dimension=0, tiled=True)
            for d in (
                d_self[:, :, :1536].reshape(D, 1536), d_cross[:, 2048:], d_cross[:, :512], d_cross[:, 512:1536],
                d_cross[:, 1536:2048], d_up.reshape(D, FF), d_down.reshape(FF, D), columns[:, 10:], columns[:, :10],
                d_unit,
            )
        )
    return (output, grad_hidden_in, grad_memory) + rest


def solution(mesh):
    rows = P(BOTH, None)
    part = P("batch", "seq", None)
    return jax.shard_map(
        functools.partial(per_device, mesh.devices.size),
        mesh=mesh,
        in_specs=(part, part, P("batch"), P("batch", None), part) + (rows,) * 9 + (P(BOTH),),
        out_specs=(part, part, part) + (rows,) * 9 + (P(BOTH),),
        check_vma=False,
    )
```

time: 203 us -> 134 us (0.66)
  waiting for transfers between devices: 86.3 us -> 45.9 us
  local copies, waits for them, and re-layouts: 25.6 us -> 0 us
  other arithmetic: 10.5 us -> 0 us
  starting transfers between devices: 39 us -> 47.4 us
    ppermute x27 -> x38, waiting for transfers between devices: 81.3 us -> 42 us  [permute(): return lax.ppermute(value, BOTH, pairs)]
    unnamed x56 -> x0, local copies, waits for them, and re-layouts: 10.9 us -> none
    ppermute x27 -> x38, starting transfers between devices: 34.5 us -> 44.4 us  [permute(): return lax.ppermute(value, BOTH, pairs)]
    slice x9 -> x0, local copies, waits for them, and re-layouts: 5.67 us -> none  [the longest x2 1.88 us: per_device(): h_new, m_new = (new[:rows], new[rows:])]
    convert_element_type x13 -> x0, other arithmetic: 4.78 us -> none  [the longest x12 3.92 us: add(): return (a.astype(F32) + b.astype(F32)).astype(BF)]
    squeeze x3 -> x0, local copies, waits for them, and re-layouts: 3.69 us -> none  [per_device(): pick = lambda v, i: lax.dynamic_index_in_dim(v, i, 0, keepdims=False)]
    select_n x3 -> x0, other arithmetic: 2.64 us -> none  [both(): return jnp.where(place == 0, jnp.stack([keep, got]), jnp.stack([got, keep]))]
    ppermute x5 -> x4, starting transfers between devices: 4.45 us -> 3.09 us  [swap(): return lax.ppermute(value, 'seq', [(0, 1), (1, 0)])]
  transfers between devices with their start and end apart: 32 -> 42, of which waited for: 16 -> 16; matrix products, arithmetic and copies ran while one was open for 11% -> 0% of each run, Pallas kernels for 9% -> 23%
where the time goes in v2:
time: 134 us; the launch traced here: 133 us
  starting transfers between devices  47.4 us (35%)
  waiting for transfers between devices  45.9 us (34%)
  Pallas kernels  39.1 us (29%)
    ppermute x38, starting transfers between devices, permute(): return lax.ppermute(value, BOTH, pairs)  44.4 us
    ppermute x38, waiting for transfers between devices, permute(): return lax.ppermute(value, BOTH, pairs)  42 us
    pallas_call x40, Pallas kernels, call(): pl.pallas_call(body, name=name, out_shape=[shape(*o) for o in made] + [sh...  36.9 us
    ppermute x4, waiting for transfers between devices, swap(): return lax.ppermute(value, 'seq', [(0, 1), (1, 0)])  3.93 us
    ppermute x4, starting transfers between devices, swap(): return lax.ppermute(value, 'seq', [(0, 1), (1, 0)])  3.09 us
  transfers between devices with their start and end apart: 42, of which 16 were waited for; matrix products, arithmetic and copies ran while one was open for 0% of the time, Pallas kernels for 23%

profile of v2, /device:TPU:0, one launch (start us, length us, event | category | flops | bytes accessed | tf_op | source)
XLA Modules:
  0.0 133.4 jit_solution(5158753567873239088)
XLA Ops:
  0.7 2.2 %pack.1 = (s32[96]{0:T(128)S(1)}, s32[2]{0:T(128)S(1)}, bf16[1,16,4224]{2,1,0:T(8,128)(2,1)S(1)}, bf16[16,2048]{1,0:T(8,128)(2,1)S(1)}, bf16[64,512]{1,0:T(8,128...) custom-call(s32[1]{0:T(128)} %bitcast.me.refs_0_, ...), custom_call_target="tpu_custom_call" | custom-call | tf_op jit(solution)/shard_map/pack/pallas_call | solution.py:614
  2.9 3.1 %collective-permute-start.2 = (bf16[1,16,4224]{2,1,0:T(8,128)(2,1)S(1)}, bf16[1,16,4224]{2,1,0:T(8,128)(2,1)S(1)}, u32[]{:S(2)}, u32[]{:S(2)}) collective-permute-start(bf16[1,16,4224]{2,1,0:T(8,128)(2,1)S(1)} %get-tuple-element.165.refs_0_), channel_id=1, source_target_pairs={{0,8},{1,9},{2,18},{3,19},{4,12},{5,13},{6,22},{7,23},{8,0},{9,1},... | collective-permute-start | bytes 405512 | tf_op jit(solution)/shard_map/gather_a_hop0/ppermute | solution.py:548
  8.0 2.0 %collective-permute-done.2.refs_1_ = bf16[1,16,4224]{2,1,0:T(8,128)(2,1)S(1)} collective-permute-done((bf16[1,16,4224]{2,1,0:T(8,128)(2,1)S(1)}, bf16[1,16,4224]{2,1,0:T(8,128)(2,1)S(1)}, u32[]{:S(2)}, u32[]{:S(2)}) %collective-permute-start.2) | collective-permute-done | bytes 135200 | tf_op jit(solution)/shard_map/gather_a_hop0/ppermute | solution.py:548
  10.1 2.4 %collective-permute-start.5 = (bf16[2,16,4224]{2,1,0:T(8,128)(2,1)S(1)}, bf16[2,16,4224]{2,1,0:T(8,128)(2,1)S(1)}, u32[]{:S(2)}, u32[]{:S(2)}) collective-permute-start(bf16[2,16,4224]{2,1,0:T(8,128)(2,1)S(1)} %get-tuple-element.171.refs_0_), channel_id=1, source_target_pairs={{0,16},{1,17},{2,10},{3,11},{4,20},{5,21},{6,14},{7,15},{8,24},{9,... | collective-permute-start | bytes 811016 | tf_op jit(solution)/shard_map/gather_a_hop1/ppermute | solution.py:548
  12.5 1.9 %collective-permute-start.3 = (bf16[2,16,2048]{2,1,0:T(8,128)(2,1)S(1)}, bf16[2,16,2048]{2,1,0:T(8,128)(2,1)S(1)}, u32[]{:S(2)}, u32[]{:S(2)}) collective-permute-start(bf16[2,16,2048]{2,1,0:T(8,128)(2,1)S(1)} %get-tuple-element.169.refs_0_), channel_id=1, source_target_pairs={{0,16},{1,17},{2,10},{3,11},{4,20},{5,21},{6,14},{7,15},{8,24},{9,... | collective-permute-start | bytes 393224 | tf_op jit(solution)/shard_map/gather_u_hop1/ppermute | solution.py:548
  14.4 1.5 %collective-permute-start.4 = (bf16[2,4,16,512]{3,2,1,0:T(8,128)(2,1)S(1)}, bf16[2,4,16,512]{3,2,1,0:T(8,128)(2,1)S(1)}, u32[]{:S(2)}, u32[]{:S(2)}) collective-permute-start(bf16[2,4,16,512]{3,2,1,0:T(8,128)(2,1)S(1)} %get-tuple-element.170.refs_0_), channel_id=1, source_target_pairs={{0,4},{1,5},{2,3},{3,2},{4,0},{5,1},{6,7},{7,6},{8,12},{9,13},{10,... | collective-permute-start | bytes 393224 | tf_op jit(solution)/shard_map/gather_w_hop1/ppermute | solution.py:548
  15.9 2.9 %collective-permute-done.5.refs_1_ = bf16[2,16,4224]{2,1,0:T(8,128)(2,1)S(1)} collective-permute-done((bf16[2,16,4224]{2,1,0:T(8,128)(2,1)S(1)}, bf16[2,16,4224]{2,1,0:T(8,128)(2,1)S(1)}, u32[]{:S(2)}, u32[]{:S(2)}) %collective-permute-start.5) | collective-permute-done | bytes 270368 | tf_op jit(solution)/shard_map/gather_a_hop1/ppermute | solution.py:548
  18.8 3.9 %collective-permute-done.6.refs_2_.refs_7_.refs_13_ = bf16[512,512]{1,0:T(8,128)(2,1)S(1)} collective-permute-done((bf16[512,512]{1,0:T(8,128)(2,1)S(1)}, bf16[512,512]{1,0:T(8,128)(2,1)S(1)}, u32[]{:S(2)}, u32[]{:S(2)}) %collective-permute-start.6) | collective-permute-done | bytes 524320 | tf_op jit(solution)/shard_map/swap_in/ppermute | solution.py:648
  22.9 2.0 %collective-permute-start.7 = (bf16[4,16,2048]{2,1,0:T(8,128)(2,1)S(1)}, bf16[4,16,2048]{2,1,0:T(8,128)(2,1)S(1)}, u32[]{:S(2)}, u32[]{:S(2)}) collective-permute-start(bf16[4,16,2048]{2,1,0:T(8,128)(2,1)S(1)} %get-tuple-element.176.refs_0_), channel_id=1, source_target_pairs={{0,1},{1,0},{2,6},{3,7},{4,5},{5,4},{6,2},{7,3},{8,9},{9,8},{10,14... | collective-permute-start | bytes 786440 | tf_op jit(solution)/shard_map/gather_u_hop2/ppermute | solution.py:548
  24.9 1.6 %collective-permute-start.8 = (bf16[4,4,16,512]{3,2,1,0:T(8,128)(2,1)S(1)}, bf16[4,4,16,512]{3,2,1,0:T(8,128)(2,1)S(1)}, u32[]{:S(2)}, u32[]{:S(2)}) collective-permute-start(bf16[4,4,16,512]{3,2,1,0:T(8,128)(2,1)S(1)} %get-tuple-element.177.refs_0_), channel_id=1, source_target_pairs={{0,8},{1,9},{2,18},{3,19},{4,12},{5,13},{6,22},{7,23},{8,0},{9,1},... | collective-permute-start | bytes 786440 | tf_op jit(solution)/shard_map/gather_w_hop2/ppermute | solution.py:548
  26.5 5.6 %collective-permute-done.9.refs_1_ = bf16[4,16,4224]{2,1,0:T(8,128)(2,1)S(1)} collective-permute-done((bf16[4,16,4224]{2,1,0:T(8,128)(2,1)S(1)}, bf16[4,16,4224]{2,1,0:T(8,128)(2,1)S(1)}, u32[]{:S(2)}, u32[]{:S(2)}) %collective-permute-start.9) | collective-permute-done | bytes 540704 | tf_op jit(solution)/shard_map/gather_a_hop2/ppermute | solution.py:548
  32.3 1.7 %collective-permute-start.12 = (bf16[8,16,4224]{2,1,0:T(8,128)(2,1)S(1)}, bf16[8,16,4224]{2,1,0:T(8,128)(2,1)S(1)}, u32[]{:S(2)}, u32[]{:S(2)}) collective-permute-start(bf16[8,16,4224]{2,1,0:T(8,128)(2,1)S(1)} %get-tuple-element.184.refs_2_), channel_id=1, source_target_pairs={{0,4},{1,5},{2,3},{3,2},{4,0},{5,1},{6,7},{7,6},{8,12},{9,13},{10,... | collective-permute-start | bytes 3244040 | tf_op jit(solution)/shard_map/gather_a_hop3/ppermute | solution.py:548
  34.0 2.6 %collective-permute-start.11 = (bf16[8,4,16,512]{3,2,1,0:T(8,128)(2,1)S(1)}, bf16[8,4,16,512]{3,2,1,0:T(8,128)(2,1)S(1)}, u32[]{:S(2)}, u32[]{:S(2)}) collective-permute-start(bf16[8,4,16,512]{3,2,1,0:T(8,128)(2,1)S(1)} %get-tuple-element.183.refs_6_), channel_id=1, source_target_pairs={{0,16},{1,17},{2,10},{3,11},{4,20},{5,21},{6,14},{7,15},{8,24},{9,... | collective-permute-start | bytes 1572872 | tf_op jit(solution)/shard_map/gather_w_hop3/ppermute | solution.py:548
  36.6 10.9 %collective-permute-done.12.refs_3_ = bf16[8,16,4224]{2,1,0:T(8,128)(2,1)S(1)} collective-permute-done((bf16[8,16,4224]{2,1,0:T(8,128)(2,1)S(1)}, bf16[8,16,4224]{2,1,0:T(8,128)(2,1)S(1)}, u32[]{:S(2)}, u32[]{:S(2)}) %collective-permute-start.12) | collective-permute-done | bytes 1081376 | tf_op jit(solution)/shard_map/gather_a_hop3/ppermute | solution.py:548
  48.1 1.6 %collective-permute-start.10 = (bf16[8,16,2048]{2,1,0:T(8,128)(2,1)S(1)}, bf16[8,16,2048]{2,1,0:T(8,128)(2,1)S(1)}, u32[]{:S(2)}, u32[]{:S(2)}) collective-permute-start(bf16[8,16,2048]{2,1,0:T(8,128)(2,1)S(1)} %get-tuple-element.182.refs_2_), channel_id=1, source_target_pairs={{0,4},{1,5},{2,3},{3,2},{4,0},{5,1},{6,7},{7,6},{8,12},{9,13},{10,... | collective-permute-start | bytes 1572872 | tf_op jit(solution)/shard_map/gather_u_hop3/ppermute | solution.py:548
  50.2 3.6 %self_forward.1 = (bf16[512,2048]{1,0:T(8,128)(2,1)S(1)}, f32[16,512]{1,0:T(8,128)S(1)}, f32[8,512]{1,0:T(8,128)S(1)}, bf16[256,512]{1,0:T(8,128)(2,1)S(1)}, bf1...) custom-call(s32[96]{0:T(128)S(1)} %get-tuple-element.162.refs_0_, ...), custom_call_target="tpu_custom_call" | custom-call | flops 1 | bytes 1 | tf_op jit(solution)/shard_map/self_forward/pallas_call | solution.py:490
  53.8 4.8 %cross_forward.1 = (bf16[512,2048]{1,0:T(8,128)(2,1)S(1)}, bf16[512,512]{1,0:T(8,128)(2,1)S(1)}, bf16[256,512]{1,0:T(8,128)(2,1)S(1)}, bf16[512,512]{1,0:T(8,128...) custom-call(s32[96]{0:T(128)S(1)} %get-tuple-element.162.refs_0_, ...), custom_call_target="tpu_custom_call" | custom-call | flops 1 | bytes 1 | tf_op jit(solution)/shard_map/cross_forward/pallas_call | solution.py:490
  61.4 4.7 %ffn.1 = (bf16[128,512]{1,0:T(8,128)(2,1)S(1)}, bf16[128,512]{1,0:T(8,128)(2,1)S(1)}, bf16[512,2048]{1,0:T(8,128)(2,1)S(1)}, bf16[256,2048]{1,0:T(8,128)(2,1)S(1...) custom-call(s32[96]{0:T(128)S(1)} %get-tuple-element.162.refs_0_, ...), custom_call_target="tpu_custom_call" | custom-call | flops 1 | bytes 1 | tf_op jit(solution)/shard_map/ffn/pallas_call | solution.py:490
  66.4 2.8 %ffn_back.1 = (f32[256,512]{1,0:T(8,128)S(1)}, f32[16,512]{1,0:T(8,128)S(1)}, f32[8,512]{1,0:T(8,128)S(1)}, bf16[16,16,2048]{2,1,0:T(8,128)(2,1)S(1)}, bf16[16,1...) custom-call(s32[96]{0:T(128)S(1)} %get-tuple-element.162.refs_0_, s32[2]{0:T(128)S(1)} %get-tuple-element.161.refs_1_.refs_0_, ...), custom_call_target="tpu_custom_call" | custom-call | flops 1 | bytes 1 | tf_op jit(solution)/shard_map/ffn_back/pallas_call | solution.py:490
  69.9 1.7 %collective-permute-start.21 = (bf16[8,4,16,512]{3,2,1,0:T(8,128)(2,1)S(1)}, bf16[8,4,16,512]{3,2,1,0:T(8,128)(2,1)S(1)}, u32[]{:S(2)}, u32[]{:S(2)}) collective-permute-start(bf16[8,4,16,512]{3,2,1,0:T(8,128)(2,1)S(1)} %get-tuple-element.210), channel_id=1, source_target_pairs={{0,4},{1,5},{2,3},{3,2},{4,0},{5,1},{6,7},{7,6},{8,12},{9,13},{10,... | collective-permute-start | bytes 1572872 | tf_op jit(solution)/shard_map/scatter_d_hop3/ppermute | solution.py:548
  72.2 1.7 %collective-permute-start.25 = (bf16[8,16,2048]{2,1,0:T(8,128)(2,1)S(1)}, bf16[8,16,2048]{2,1,0:T(8,128)(2,1)S(1)}, u32[]{:S(2)}, u32[]{:S(2)}) collective-permute-start(bf16[8,16,2048]{2,1,0:T(8,128)(2,1)S(1)} %get-tuple-element.243), channel_id=1, source_target_pairs={{0,4},{1,5},{2,3},{3,2},{4,0},{5,1},{6,7},{7,6},{8,12},{9,13},{10,... | collective-permute-start | bytes 1572872 | tf_op jit(solution)/shard_map/scatter_u_hop3/ppermute | solution.py:548
  73.9 7.3 %cross_back.1 = (f32[256,512]{1,0:T(8,128)S(1)}, bf16[256,512]{1,0:T(8,128)(2,1)S(1)}, f32[256,512]{1,0:T(8,128)S(1)}, bf16[256,512]{1,0:T(8,128)(2,1)S(1)}, f32...) custom-call(s32[96]{0:T(128)S(1)} %get-tuple-element.162.refs_0_, ...), custom_call_target="tpu_custom_call" | custom-call | flops 1 | bytes 1 | tf_op jit(solution)/shard_map/cross_back/pallas_call | solution.py:490
  81.2 4.4 %self_back.1 = (f32[128,512]{1,0:T(8,128)S(1)}, bf16[128,512]{1,0:T(8,128)(2,1)S(1)}, bf16[16,16,1664]{2,1,0:T(8,128)(2,1)S(1)}, bf16[16,16,1664]{2,1,0:T(8,128)(2,1)S(1)}, f32[8,128]{1,0:T(8,128)S(1)}) custom-call(s32[96]{0:T(128)S(1)} %get-tuple-element.162.refs_0_, s32[2]{0:T(128)S(1)} %get-tuple-element.161.refs_1_.refs_0_, ...), custom_call_target="tpu_custom_call" | custom-call | flops 1 | bytes 1 | tf_op jit(solution)/shard_map/self_back/pallas_call | solution.py:490
  86.3 1.7 %collective-permute-done.26.refs_1_ = bf16[16,16,1664]{2,1,0:T(8,128)(2,1)S(1)} collective-permute-done((bf16[16,16,1664]{2,1,0:T(8,128)(2,1)S(1)}, bf16[16,16,1664]{2,1,0:T(8,128)(2,1)S(1)}, u32[]{:S(2)}, u32[]{:S(2)}) %collective-permute-start.26) | collective-permute-done | bytes 852000 | tf_op jit(solution)/shard_map/scatter_s_core/ppermute | solution.py:548
  92.3 2.6 %collective-permute-start.23 = (bf16[4,4,16,512]{3,2,1,0:T(8,128)(2,1)S(1)}, bf16[4,4,16,512]{3,2,1,0:T(8,128)(2,1)S(1)}, u32[]{:S(2)}, u32[]{:S(2)}) collective-permute-start(bf16[4,4,16,512]{3,2,1,0:T(8,128)(2,1)S(1)} %get-tuple-element.239), channel_id=1, source_target_pairs={{0,16},{1,17},{2,10},{3,11},{4,20},{5,21},{6,14},{7,15},{8,24},{9,... | collective-permute-start | bytes 786440 | tf_op jit(solution)/shard_map/scatter_d_hop2/ppermute | solution.py:548
  96.1 6.0 %collective-permute-done.23.refs_1_ = bf16[4,4,16,512]{3,2,1,0:T(8,128)(2,1)S(1)} collective-permute-done((bf16[4,4,16,512]{3,2,1,0:T(8,128)(2,1)S(1)}, bf16[4,4,16,512]{3,2,1,0:T(8,128)(2,1)S(1)}, u32[]{:S(2)}, u32[]{:S(2)}) %collective-permute-start.23) | collective-permute-done | bytes 262176 | tf_op jit(solution)/shard_map/scatter_d_hop2/ppermute | solution.py:548
  103.5 2.0 %collective-permute-done.29.refs_1_ = bf16[8,16,1664]{2,1,0:T(8,128)(2,1)S(1)} collective-permute-done((bf16[8,16,1664]{2,1,0:T(8,128)(2,1)S(1)}, bf16[8,16,1664]{2,1,0:T(8,128)(2,1)S(1)}, u32[]{:S(2)}, u32[]{:S(2)}) %collective-permute-start.29) | collective-permute-done | bytes 426016 | tf_op jit(solution)/shard_map/scatter_s_hop3/ppermute | solution.py:548
  112.7 2.6 %collective-permute-start.37 = (bf16[2,16,1664]{2,1,0:T(8,128)(2,1)S(1)}, bf16[2,16,1664]{2,1,0:T(8,128)(2,1)S(1)}, u32[]{:S(2)}, u32[]{:S(2)}) collective-permute-start(bf16[2,16,1664]{2,1,0:T(8,128)(2,1)S(1)} %get-tuple-element.280), channel_id=1, source_target_pairs={{0,16},{1,17},{2,10},{3,11},{4,20},{5,21},{6,14},{7,15},{8,24},{9,... | collective-permute-start | bytes 319496 | tf_op jit(solution)/shard_map/scatter_s_hop1/ppermute | solution.py:548
  118.5 1.7 %collective-permute-start.34 = (bf16[2,16,2560]{2,1,0:T(8,128)(2,1)S(1)}, bf16[2,16,2560]{2,1,0:T(8,128)(2,1)S(1)}, u32[]{:S(2)}, u32[]{:S(2)}) collective-permute-start(bf16[2,16,2560]{2,1,0:T(8,128)(2,1)S(1)} %get-tuple-element.273), channel_id=1, source_target_pairs={{0,16},{1,17},{2,10},{3,11},{4,20},{5,21},{6,14},{7,15},{8,24},{9,... | collective-permute-start | bytes 491528 | tf_op jit(solution)/shard_map/scatter_c_hop1/ppermute | solution.py:548
  121.6 4.2 %collective-permute-done.36.refs_1_ = bf16[1,16,2048]{2,1,0:T(8,128)(2,1)S(1)} collective-permute-done((bf16[1,16,2048]{2,1,0:T(8,128)(2,1)S(1)}, bf16[1,16,2048]{2,1,0:T(8,128)(2,1)S(1)}, u32[]{:S(2)}, u32[]{:S(2)}) %collective-permute-start.36) | collective-permute-done | bytes 65568 | tf_op jit(solution)/shard_map/scatter_u_hop0/ppermute | solution.py:548
  126.6 2.4 %collective-permute-start.41 = (bf16[1,16,2560]{2,1,0:T(8,128)(2,1)S(1)}, bf16[1,16,2560]{2,1,0:T(8,128)(2,1)S(1)}, u32[]{:S(2)}, u32[]{:S(2)}) collective-permute-start(bf16[1,16,2560]{2,1,0:T(8,128)(2,1)S(1)} %get-tuple-element.298), channel_id=1, source_target_pairs={{0,8},{1,9},{2,18},{3,19},{4,12},{5,13},{6,22},{7,23},{8,0},{9,1},... | collective-permute-start | bytes 245768 | tf_op jit(solution)/shard_map/scatter_c_hop0/ppermute | solution.py:548
  131.2 1.6 %halves_memory.1 = (f32[2,256,512]{2,1,0:T(8,128)}, f32[8,128]{1,0:T(8,128)S(1)}) custom-call(s32[2]{0:T(128)S(1)} %get-tuple-element.161.refs_1_.refs_0_, f32[256,512]{1,0:T(8,128)S(1)} %get-tuple-element.289.refs_1_, bf16[256,512]{1,0:T(8,128)(2,1)S(1)} %collective-permute-done.39.refs_2_, f32[8,128]{1,0:T(8,128)S(1)} %get-tuple-element.294.refs_3_), custom_call_target="tpu_custom_call" | custom-call | flops 1 | bytes 1 | tf_op jit(solution)/shard_map/halves_memory/pallas_call | solution.py:490
  (93 shorter events, 30.8 us)
Async XLA Ops:
  2.9 7.2 %collective-permute-start.2 = (bf16[1,16,4224]{2,1,0:T(8,128)(2,1)S(1)}, bf16[1,16,4224]{2,1,0:T(8,128)(2,1)S(1)}, u32[]{:S(2)}, u32[]{:S(2)}) collective-permute-start(bf16[1,16,4224]{2,1,0:T(8,128)(2,1)S(1)} %get-tuple-element.165.refs_0_), channel_id=1, source_target_pairs={{0,8},{1,9},{2,18},{3,19},{4,12},{5,13},{6,22},{7,23},{8,0},{9,1},... | collective-permute-start | bytes 405512 | tf_op jit(solution)/shard_map/gather_a_hop0/ppermute | solution.py:548
  5.9 6.5 %collective-permute-start.1 = (bf16[1,4,16,512]{3,2,1,0:T(8,128)(2,1)S(1)}, bf16[1,4,16,512]{3,2,1,0:T(8,128)(2,1)S(1)}, u32[]{:S(2)}, u32[]{:S(2)}) collective-permute-start(bf16[1,4,16,512]{3,2,1,0:T(8,128)(2,1)S(1)} %bitcast.10), channel_id=1, source_target_pairs={{0,1},{1,0},{2,6},{3,7},{4,5},{5,4},{6,2},{7,3},{8,9},{9,8},{10,14... | collective-permute-start | bytes 196616 | tf_op jit(solution)/shard_map/gather_w_hop0/ppermute | solution.py:548
  7.9 14.8 %collective-permute-start.6 = (bf16[512,512]{1,0:T(8,128)(2,1)S(1)}, bf16[512,512]{1,0:T(8,128)(2,1)S(1)}, u32[]{:S(2)}, u32[]{:S(2)}) collective-permute-start(bf16[512,512]{1,0:T(8,128)(2,1)S(1)} %get-tuple-element.172), channel_id=1, source_target_pairs={{0,1},{1,0},{2,3},{3,2},{4,5},{5,4},{6,7},{7,6},{8,9},{9,8},{10,11... | collective-permute-start | bytes 1572872 | tf_op jit(solution)/shard_map/swap_in/ppermute | solution.py:648
  10.1 8.7 %collective-permute-start.5 = (bf16[2,16,4224]{2,1,0:T(8,128)(2,1)S(1)}, bf16[2,16,4224]{2,1,0:T(8,128)(2,1)S(1)}, u32[]{:S(2)}, u32[]{:S(2)}) collective-permute-start(bf16[2,16,4224]{2,1,0:T(8,128)(2,1)S(1)} %get-tuple-element.171.refs_0_), channel_id=1, source_target_pairs={{0,16},{1,17},{2,10},{3,11},{4,20},{5,21},{6,14},{7,15},{8,24},{9,... | collective-permute-start | bytes 811016 | tf_op jit(solution)/shard_map/gather_a_hop1/ppermute | solution.py:548
  12.5 10.4 %collective-permute-start.3 = (bf16[2,16,2048]{2,1,0:T(8,128)(2,1)S(1)}, bf16[2,16,2048]{2,1,0:T(8,128)(2,1)S(1)}, u32[]{:S(2)}, u32[]{:S(2)}) collective-permute-start(bf16[2,16,2048]{2,1,0:T(8,128)(2,1)S(1)} %get-tuple-element.169.refs_0_), channel_id=1, source_target_pairs={{0,16},{1,17},{2,10},{3,11},{4,20},{5,21},{6,14},{7,15},{8,24},{9,... | collective-permute-start | bytes 393224 | tf_op jit(solution)/shard_map/gather_u_hop1/ppermute | solution.py:548
  14.4 8.5 %collective-permute-start.4 = (bf16[2,4,16,512]{3,2,1,0:T(8,128)(2,1)S(1)}, bf16[2,4,16,512]{3,2,1,0:T(8,128)(2,1)S(1)}, u32[]{:S(2)}, u32[]{:S(2)}) collective-permute-start(bf16[2,4,16,512]{3,2,1,0:T(8,128)(2,1)S(1)} %get-tuple-element.170.refs_0_), channel_id=1, source_target_pairs={{0,4},{1,5},{2,3},{3,2},{4,0},{5,1},{6,7},{7,6},{8,12},{9,13},{10,... | collective-permute-start | bytes 393224 | tf_op jit(solution)/shard_map/gather_w_hop1/ppermute | solution.py:548
  22.7 9.4 %collective-permute-start.9 = (bf16[4,16,4224]{2,1,0:T(8,128)(2,1)S(1)}, bf16[4,16,4224]{2,1,0:T(8,128)(2,1)S(1)}, u32[]{:S(2)}, u32[]{:S(2)}) collective-permute-start(bf16[4,16,4224]{2,1,0:T(8,128)(2,1)S(1)} %get-tuple-element.178.refs_0_), channel_id=1, source_target_pairs={{0,1},{1,0},{2,6},{3,7},{4,5},{5,4},{6,2},{7,3},{8,9},{9,8},{10,14... | collective-permute-start | bytes 1622024 | tf_op jit(solution)/shard_map/gather_a_hop2/ppermute | solution.py:548
  22.9 24.6 %collective-permute-start.7 = (bf16[4,16,2048]{2,1,0:T(8,128)(2,1)S(1)}, bf16[4,16,2048]{2,1,0:T(8,128)(2,1)S(1)}, u32[]{:S(2)}, u32[]{:S(2)}) collective-permute-start(bf16[4,16,2048]{2,1,0:T(8,128)(2,1)S(1)} %get-tuple-element.176.refs_0_), channel_id=1, source_target_pairs={{0,1},{1,0},{2,6},{3,7},{4,5},{5,4},{6,2},{7,3},{8,9},{9,8},{10,14... | collective-permute-start | bytes 786440 | tf_op jit(solution)/shard_map/gather_u_hop2/ppermute | solution.py:548
  24.9 9.0 %collective-permute-start.8 = (bf16[4,4,16,512]{3,2,1,0:T(8,128)(2,1)S(1)}, bf16[4,4,16,512]{3,2,1,0:T(8,128)(2,1)S(1)}, u32[]{:S(2)}, u32[]{:S(2)}) collective-permute-start(bf16[4,4,16,512]{3,2,1,0:T(8,128)(2,1)S(1)} %get-tuple-element.177.refs_0_), channel_id=1, source_target_pairs={{0,8},{1,9},{2,18},{3,19},{4,12},{5,13},{6,22},{7,23},{8,0},{9,1},... | collective-permute-start | bytes 786440 | tf_op jit(solution)/shard_map/gather_w_hop2/ppermute | solution.py:548
  32.2 17.5 %collective-permute-start.13 = (bf16[8,16,4224]{2,1,0:T(8,128)(2,1)S(1)}, bf16[8,16,4224]{2,1,0:T(8,128)(2,1)S(1)}, u32[]{:S(2)}, u32[]{:S(2)}) collective-permute-start(bf16[8,16,4224]{2,1,0:T(8,128)(2,1)S(1)} %get-tuple-element.184.refs_2_), channel_id=1, source_target_pairs={{0,2},{1,3},{2,0},{3,1},{4,6},{5,7},{6,4},{7,5},{8,10},{9,11},{10,... | collective-permute-start | bytes 3244040 | tf_op jit(solution)/shard_map/gather_a_core0/ppermute | solution.py:548
  32.3 15.2 %collective-permute-start.12 = (bf16[8,16,4224]{2,1,0:T(8,128)(2,1)S(1)}, bf16[8,16,4224]{2,1,0:T(8,128)(2,1)S(1)}, u32[]{:S(2)}, u32[]{:S(2)}) collective-permute-start(bf16[8,16,4224]{2,1,0:T(8,128)(2,1)S(1)} %get-tuple-element.184.refs_2_), channel_id=1, source_target_pairs={{0,4},{1,5},{2,3},{3,2},{4,0},{5,1},{6,7},{7,6},{8,12},{9,13},{10,... | collective-permute-start | bytes 3244040 | tf_op jit(solution)/shard_map/gather_a_hop3/ppermute | solution.py:548
  34.0 24.6 %collective-permute-start.11 = (bf16[8,4,16,512]{3,2,1,0:T(8,128)(2,1)S(1)}, bf16[8,4,16,512]{3,2,1,0:T(8,128)(2,1)S(1)}, u32[]{:S(2)}, u32[]{:S(2)}) collective-permute-start(bf16[8,4,16,512]{3,2,1,0:T(8,128)(2,1)S(1)} %get-tuple-element.183.refs_6_), channel_id=1, source_target_pairs={{0,16},{1,17},{2,10},{3,11},{4,20},{5,21},{6,14},{7,15},{8,24},{9,... | collective-permute-start | bytes 1572872 | tf_op jit(solution)/shard_map/gather_w_hop3/ppermute | solution.py:548
  47.6 11.7 %collective-permute-start.15 = (bf16[8,16,2048]{2,1,0:T(8,128)(2,1)S(1)}, bf16[8,16,2048]{2,1,0:T(8,128)(2,1)S(1)}, u32[]{:S(2)}, u32[]{:S(2)}) collective-permute-start(bf16[8,16,2048]{2,1,0:T(8,128)(2,1)S(1)} %get-tuple-element.182.refs_2_), channel_id=1, source_target_pairs={{0,2},{1,3},{2,0},{3,1},{4,6},{5,7},{6,4},{7,5},{8,10},{9,11},{10,... | collective-permute-start | bytes 1572872 | tf_op jit(solution)/shard_map/gather_u_core0/ppermute | solution.py:548
  48.1 10.5 %collective-permute-start.10 = (bf16[8,16,2048]{2,1,0:T(8,128)(2,1)S(1)}, bf16[8,16,2048]{2,1,0:T(8,128)(2,1)S(1)}, u32[]{:S(2)}, u32[]{:S(2)}) collective-permute-start(bf16[8,16,2048]{2,1,0:T(8,128)(2,1)S(1)} %get-tuple-element.182.refs_2_), channel_id=1, source_target_pairs={{0,4},{1,5},{2,3},{3,2},{4,0},{5,1},{6,7},{7,6},{8,12},{9,13},{10,... | collective-permute-start | bytes 1572872 | tf_op jit(solution)/shard_map/gather_u_hop3/ppermute | solution.py:548
  49.7 9.6 %collective-permute-start.17 = (bf16[8,4,16,512]{3,2,1,0:T(8,128)(2,1)S(1)}, bf16[8,4,16,512]{3,2,1,0:T(8,128)(2,1)S(1)}, u32[]{:S(2)}, u32[]{:S(2)}) collective-permute-start(bf16[8,4,16,512]{3,2,1,0:T(8,128)(2,1)S(1)} %get-tuple-element.183.refs_6_), channel_id=1, source_target_pairs={{0,2},{1,3},{2,0},{3,1},{4,6},{5,7},{6,4},{7,5},{8,10},{9,11},{10,... | collective-permute-start | bytes 1572872 | tf_op jit(solution)/shard_map/gather_w_core0/ppermute | solution.py:548
  69.9 16.3 %collective-permute-start.21 = (bf16[8,4,16,512]{3,2,1,0:T(8,128)(2,1)S(1)}, bf16[8,4,16,512]{3,2,1,0:T(8,128)(2,1)S(1)}, u32[]{:S(2)}, u32[]{:S(2)}) collective-permute-start(bf16[8,4,16,512]{3,2,1,0:T(8,128)(2,1)S(1)} %get-tuple-element.210), channel_id=1, source_target_pairs={{0,4},{1,5},{2,3},{3,2},{4,0},{5,1},{6,7},{7,6},{8,12},{9,13},{10,... | collective-permute-start | bytes 1572872 | tf_op jit(solution)/shard_map/scatter_d_hop3/ppermute | solution.py:548
  72.2 16.1 %collective-permute-start.25 = (bf16[8,16,2048]{2,1,0:T(8,128)(2,1)S(1)}, bf16[8,16,2048]{2,1,0:T(8,128)(2,1)S(1)}, u32[]{:S(2)}, u32[]{:S(2)}) collective-permute-start(bf16[8,16,2048]{2,1,0:T(8,128)(2,1)S(1)} %get-tuple-element.243), channel_id=1, source_target_pairs={{0,4},{1,5},{2,3},{3,2},{4,0},{5,1},{6,7},{7,6},{8,12},{9,13},{10,... | collective-permute-start | bytes 1572872 | tf_op jit(solution)/shard_map/scatter_u_hop3/ppermute | solution.py:548
  90.2 17.5 %collective-permute-start.28 = (bf16[8,16,2560]{2,1,0:T(8,128)(2,1)S(1)}, bf16[8,16,2560]{2,1,0:T(8,128)(2,1)S(1)}, u32[]{:S(2)}, u32[]{:S(2)}) collective-permute-start(bf16[8,16,2560]{2,1,0:T(8,128)(2,1)S(1)} %get-tuple-element.255), channel_id=1, source_target_pairs={{0,4},{1,5},{2,3},{3,2},{4,0},{5,1},{6,7},{7,6},{8,12},{9,13},{10,... | collective-permute-start | bytes 1966088 | tf_op jit(solution)/shard_map/scatter_c_hop3/ppermute | solution.py:548
  90.9 14.5 %collective-permute-start.29 = (bf16[8,16,1664]{2,1,0:T(8,128)(2,1)S(1)}, bf16[8,16,1664]{2,1,0:T(8,128)(2,1)S(1)}, u32[]{:S(2)}, u32[]{:S(2)}) collective-permute-start(bf16[8,16,1664]{2,1,0:T(8,128)(2,1)S(1)} %get-tuple-element.257), channel_id=1, source_target_pairs={{0,4},{1,5},{2,3},{3,2},{4,0},{5,1},{6,7},{7,6},{8,12},{9,13},{10,... | collective-permute-start | bytes 1277960 | tf_op jit(solution)/shard_map/scatter_s_hop3/ppermute | solution.py:548
  92.3 9.8 %collective-permute-start.23 = (bf16[4,4,16,512]{3,2,1,0:T(8,128)(2,1)S(1)}, bf16[4,4,16,512]{3,2,1,0:T(8,128)(2,1)S(1)}, u32[]{:S(2)}, u32[]{:S(2)}) collective-permute-start(bf16[4,4,16,512]{3,2,1,0:T(8,128)(2,1)S(1)} %get-tuple-element.239), channel_id=1, source_target_pairs={{0,16},{1,17},{2,10},{3,11},{4,20},{5,21},{6,14},{7,15},{8,24},{9,... | collective-permute-start | bytes 786440 | tf_op jit(solution)/shard_map/scatter_d_hop2/ppermute | solution.py:548
  94.9 7.3 %collective-permute-start.19 = (bf16[128,512]{1,0:T(8,128)(2,1)S(1)}, bf16[128,512]{1,0:T(8,128)(2,1)S(1)}, u32[]{:S(2)}, u32[]{:S(2)}) collective-permute-start(bf16[128,512]{1,0:T(8,128)(2,1)S(1)} %get-tuple-element.201), channel_id=1, source_target_pairs={{0,1},{1,0},{2,3},{3,2},{4,5},{5,4},{6,7},{7,6},{8,9},{9,8},{10,11... | collective-permute-start | bytes 393224 | tf_op jit(solution)/shard_map/swap_out/ppermute | solution.py:648
  95.8 13.0 %collective-permute-start.33 = (bf16[4,16,2048]{2,1,0:T(8,128)(2,1)S(1)}, bf16[4,16,2048]{2,1,0:T(8,128)(2,1)S(1)}, u32[]{:S(2)}, u32[]{:S(2)}) collective-permute-start(bf16[4,16,2048]{2,1,0:T(8,128)(2,1)S(1)} %get-tuple-element.267), channel_id=1, source_target_pairs={{0,16},{1,17},{2,10},{3,11},{4,20},{5,21},{6,14},{7,15},{8,24},{9,... | collective-permute-start | bytes 786440 | tf_op jit(solution)/shard_map/scatter_u_hop2/ppermute | solution.py:548
  107.9 8.4 %collective-permute-start.30 = (bf16[4,16,2560]{2,1,0:T(8,128)(2,1)S(1)}, bf16[4,16,2560]{2,1,0:T(8,128)(2,1)S(1)}, u32[]{:S(2)}, u32[]{:S(2)}) collective-permute-start(bf16[4,16,2560]{2,1,0:T(8,128)(2,1)S(1)} %get-tuple-element.261), channel_id=1, source_target_pairs={{0,1},{1,0},{2,6},{3,7},{4,5},{5,4},{6,2},{7,3},{8,9},{9,8},{10,14... | collective-permute-start | bytes 983048 | tf_op jit(solution)/shard_map/scatter_c_hop2/ppermute | solution.py:548
  108.8 8.6 %collective-permute-start.35 = (bf16[2,16,2048]{2,1,0:T(8,128)(2,1)S(1)}, bf16[2,16,2048]{2,1,0:T(8,128)(2,1)S(1)}, u32[]{:S(2)}, u32[]{:S(2)}) collective-permute-start(bf16[2,16,2048]{2,1,0:T(8,128)(2,1)S(1)} %get-tuple-element.275), channel_id=1, source_target_pairs={{0,8},{1,9},{2,18},{3,19},{4,12},{5,13},{6,22},{7,23},{8,0},{9,1},... | collective-permute-start | bytes 393224 | tf_op jit(solution)/shard_map/scatter_u_hop1/ppermute | solution.py:548
  111.6 6.9 %collective-permute-start.38 = (bf16[1,4,16,512]{3,2,1,0:T(8,128)(2,1)S(1)}, bf16[1,4,16,512]{3,2,1,0:T(8,128)(2,1)S(1)}, u32[]{:S(2)}, u32[]{:S(2)}) collective-permute-start(bf16[1,4,16,512]{3,2,1,0:T(8,128)(2,1)S(1)} %get-tuple-element.282), channel_id=1, source_target_pairs={{0,1},{1,0},{2,6},{3,7},{4,5},{5,4},{6,2},{7,3},{8,9},{9,8},{10,14... | collective-permute-start | bytes 196616 | tf_op jit(solution)/shard_map/scatter_d_hop0/ppermute | solution.py:548
  112.7 8.8 %collective-permute-start.37 = (bf16[2,16,1664]{2,1,0:T(8,128)(2,1)S(1)}, bf16[2,16,1664]{2,1,0:T(8,128)(2,1)S(1)}, u32[]{:S(2)}, u32[]{:S(2)}) collective-permute-start(bf16[2,16,1664]{2,1,0:T(8,128)(2,1)S(1)} %get-tuple-element.280), channel_id=1, source_target_pairs={{0,16},{1,17},{2,10},{3,11},{4,20},{5,21},{6,14},{7,15},{8,24},{9,... | collective-permute-start | bytes 319496 | tf_op jit(solution)/shard_map/scatter_s_hop1/ppermute | solution.py:548
  115.4 13.7 %collective-permute-start.27 = (bf16[128,512]{1,0:T(8,128)(2,1)S(1)}, bf16[128,512]{1,0:T(8,128)(2,1)S(1)}, u32[]{:S(2)}, u32[]{:S(2)}) collective-permute-start(bf16[128,512]{1,0:T(8,128)(2,1)S(1)} %get-tuple-element.253), channel_id=1, source_target_pairs={{0,1},{1,0},{2,3},{3,2},{4,5},{5,4},{6,7},{7,6},{8,9},{9,8},{10,11... | collective-permute-start | bytes 393224 | tf_op jit(solution)/shard_map/swap_hidden/ppermute | solution.py:648
  116.2 14.9 %collective-permute-start.39 = (bf16[256,512]{1,0:T(8,128)(2,1)S(1)}, bf16[256,512]{1,0:T(8,128)(2,1)S(1)}, u32[]{:S(2)}, u32[]{:S(2)}) collective-permute-start(bf16[256,512]{1,0:T(8,128)(2,1)S(1)} %get-tuple-element.290), channel_id=1, source_target_pairs={{0,1},{1,0},{2,3},{3,2},{4,5},{5,4},{6,7},{7,6},{8,9},{9,8},{10,11... | collective-permute-start | bytes 786440 | tf_op jit(solution)/shard_map/swap_memory/ppermute | solution.py:648
  117.5 8.3 %collective-permute-start.36 = (bf16[1,16,2048]{2,1,0:T(8,128)(2,1)S(1)}, bf16[1,16,2048]{2,1,0:T(8,128)(2,1)S(1)}, u32[]{:S(2)}, u32[]{:S(2)}) collective-permute-start(bf16[1,16,2048]{2,1,0:T(8,128)(2,1)S(1)} %get-tuple-element.278), channel_id=1, source_target_pairs={{0,1},{1,0},{2,6},{3,7},{4,5},{5,4},{6,2},{7,3},{8,9},{9,8},{10,14... | collective-permute-start | bytes 196616 | tf_op jit(solution)/shard_map/scatter_u_hop0/ppermute | solution.py:548
  118.5 8.1 %collective-permute-start.34 = (bf16[2,16,2560]{2,1,0:T(8,128)(2,1)S(1)}, bf16[2,16,2560]{2,1,0:T(8,128)(2,1)S(1)}, u32[]{:S(2)}, u32[]{:S(2)}) collective-permute-start(bf16[2,16,2560]{2,1,0:T(8,128)(2,1)S(1)} %get-tuple-element.273), channel_id=1, source_target_pairs={{0,16},{1,17},{2,10},{3,11},{4,20},{5,21},{6,14},{7,15},{8,24},{9,... | collective-permute-start | bytes 491528 | tf_op jit(solution)/shard_map/scatter_c_hop1/ppermute | solution.py:548
  121.5 8.9 %collective-permute-start.40 = (bf16[1,16,1664]{2,1,0:T(8,128)(2,1)S(1)}, bf16[1,16,1664]{2,1,0:T(8,128)(2,1)S(1)}, u32[]{:S(2)}, u32[]{:S(2)}) collective-permute-start(bf16[1,16,1664]{2,1,0:T(8,128)(2,1)S(1)} %get-tuple-element.292), channel_id=1, source_target_pairs={{0,8},{1,9},{2,18},{3,19},{4,12},{5,13},{6,22},{7,23},{8,0},{9,1},... | collective-permute-start | bytes 159752 | tf_op jit(solution)/shard_map/scatter_s_hop0/ppermute | solution.py:548
  126.6 6.1 %collective-permute-start.41 = (bf16[1,16,2560]{2,1,0:T(8,128)(2,1)S(1)}, bf16[1,16,2560]{2,1,0:T(8,128)(2,1)S(1)}, u32[]{:S(2)}, u32[]{:S(2)}) collective-permute-start(bf16[1,16,2560]{2,1,0:T(8,128)(2,1)S(1)} %get-tuple-element.298), channel_id=1, source_target_pairs={{0,8},{1,9},{2,18},{3,19},{4,12},{5,13},{6,22},{7,23},{8,0},{9,1},... | collective-permute-start | bytes 245768 | tf_op jit(solution)/shard_map/scatter_c_hop0/ppermute | solution.py:548
  (10 other events, 36.0 us)

commit v3 on v2

--- a/solution.py
+++ b/solution.py
@@ -65,7 +65,7 @@
     return jnp.where(visible, dot_nt(keys, queries) * SCALE, NEGATIVE)
 
 
-def attend(q_ref, k_ref, v_ref, visible, mixed_ref, log_ref):
+def attend(q_ref, k_ref, v_ref, visible, mixed_ref, probs_ref):
     masks = lane_masks(BF)
     for pair in range(HEADS // 2):
         cols = slice(128 * pair, 128 * pair + 128)
@@ -77,26 +77,30 @@
             exponent = jnp.exp(scores - top)
             row_total = jnp.sum(exponent, axis=0, keepdims=True)
             probs = (exponent * (1.0 / row_total)).astype(BF)
-            log_ref[2 * pair + j : 2 * pair + j + 1, :] = top + jnp.log(row_total)
+            probs_ref[2 * pair + j] = probs
             part = dot_tn(probs, values * masks[j])
             total = part if total is None else total + part
         mixed_ref[:, cols] = total.astype(BF)
 
 
-def attend_back(q_ref, k_ref, v_ref, visible, log_ref, grad_ref, dq_ref, dk_ref, dv_ref):
+def attend_back(q_ref, k_ref, v_ref, probs_ref, mixed_ref, grad_ref, dq_ref, dk_ref, dv_ref):
     masks = lane_masks(BF)
+    product = grad_ref[...].astype(F32) * mixed_ref[...].astype(F32)
+    high = product.astype(BF)
+    low = (product - high.astype(F32)).astype(BF)
+    head = lax.broadcasted_iota(jnp.int32, (HEADS, D), 0)
+    picks = (lax.broadcasted_iota(jnp.int32, (HEADS, D), 1) // HEAD_DIM == head).astype(BF)
+    inner = dot_nt(picks, high) + dot_nt(picks, low)
     for pair in range(HEADS // 2):
         cols = slice(128 * pair, 128 * pair + 128)
         queries, keys, values, grads = q_ref[:, cols], k_ref[:, cols], v_ref[:, cols], grad_ref[:, cols]
         dq = dk = dv = None
         for j in range(2):
             own_q, own_k, own_g = queries * masks[j], keys * masks[j], grads * masks[j]
-            scores = scores_t(keys, own_q, visible)
-            probs = jnp.exp(scores - log_ref[2 * pair + j : 2 * pair + j + 1, :])
+            probs = probs_ref[2 * pair + j]
             grad_probs = dot_nt(values, own_g)
-            part_v = dot(probs.astype(BF), own_g)
-            inner = jnp.sum(probs * grad_probs, axis=0, keepdims=True)
-            low = (probs * (grad_probs - inner)).astype(BF)
+            part_v = dot(probs, own_g)
+            low = (probs.astype(F32) * (grad_probs - inner[2 * pair + j : 2 * pair + j + 1, :])).astype(BF)
             part_k = dot(low, own_q)
             part_q = dot_tn(low, own_k)
             dq = part_q if dq is None else dq + part_q
@@ -195,28 +199,37 @@
     out[...] = value[...]
 
 
-def add_kernel(own, got, send, keep):
+def add_kernel(axis, *refs):
+    *parts, send, keep = refs
     count = send.shape[0]
-    send[...] = (own[count:].astype(F32) + got[count:].astype(F32)).astype(send.dtype)
-    keep[...] = (own[:count].astype(F32) + got[:count].astype(F32)).astype(keep.dtype)
-
-
-def last_kernel(own, got, out):
-    out[...] = own[0] + got[0].astype(F32)
-
-
-def last_cross_kernel(own, got, d_cq, d_ckv, d_co, d_out):
-    total = own[0] + got[0].astype(F32)
+    first = 0
+    for own, got in zip(parts[::2], parts[1::2]):
+        last = first + own.shape[axis]
+        place = (slice(None),) * axis + (slice(first, last),)
+        send[place] = (own[count:].astype(F32) + got[count:].astype(F32)).astype(send.dtype)
+        keep[place] = (own[:count].astype(F32) + got[:count].astype(F32)).astype(keep.dtype)
+        first = last
+
+
+def last_ffn_kernel(*refs):
+    (*parts, d_up, d_down) = refs
+    total = [own[0] + got[0].astype(F32) for own, got in zip(parts[::2], parts[1::2])]
+    total = total[0] if len(total) == 1 else jnp.concatenate(total, axis=0)
+    for group in range(4):
+        d_up[:, 512 * group : 512 * group + 512] = total[group]
+        d_down[16 * group : 16 * group + 16, :] = total[4 + group]
+
+
+def last_attention_kernel(me, *refs):
+    (*parts, d_cq, d_ckv, d_co, d_out, d_qkv, d_gains, d_biases, d_units) = refs
+    total = [own[0] + got[0].astype(F32) for own, got in zip(parts[::2], parts[1::2])]
+    total = total[0] if len(total) == 1 else jnp.concatenate(total, axis=1)
     d_cq[...] = total[:, 0:512]
     d_ckv[...] = total[:, 512:1536]
     d_co[...] = total[:, 1536:2048]
     d_out[...] = total[:, 2048:2560]
-
-
-def last_self_kernel(me, own, got, d_qkv, d_gains, d_biases, d_units):
-    total = own[0] + got[0].astype(F32)
-    d_qkv[...] = total[:, 0:1536]
-    small = total[:, 1536:1664]
+    d_qkv[...] = total[:, 2560:4096]
+    small = total[:, 4096:4224]
     index = me[0]
     vectors = pltpu.roll(small, (128 - 16 * (index % 8)) % 128, 1)[:, 0:16]
     d_gains[...] = vectors[10:13, :]
@@ -231,7 +244,7 @@
 
 
 def self_forward_kernel(
-    base, order, info, p0, p1, p2, p3, kept, new, weights, vecs, ffb, x0, normed1, q, k, v, mixed1, log1, x1, normed2,
+    base, order, info, p0, p1, p2, p3, kept, new, weights, vecs, ffb, x0, normed1, q, k, v, mixed1, probs1, x1, normed2,
     small,
 ):
     place, length = info[0], info[1]
@@ -263,7 +276,7 @@
     q[...] = (dot(normed1[...], weights[:, 0:512]) + bias(1)).astype(BF)
     k[...] = dot(normed1[...], weights[:, 512:1024]).astype(BF)
     v[...] = (dot(normed1[...], weights[:, 1024:1536]) + bias(2)).astype(BF)
-    attend(q, k, v, self_visible(length, 2 * rows), mixed1, log1)
+    attend(q, k, v, self_visible(length, 2 * rows), mixed1, probs1)
     after_self = hidden + (dot(mixed1[...], weights[:, 1536:2048]) + bias(3))
     x1[...] = after_self
     normed2[...] = (norm(after_self)[0] * bias(11) + bias(4)).astype(BF)
@@ -271,7 +284,7 @@
 
 def cross_forward_kernel(
     base, order, info, p0, p1, p2, p3, kept, new, mask, vecs, x1, normed2,
-    weights, mem, cq, ck, cv, mixed2, log2, x2, normed3,
+    weights, mem, cq, ck, cv, mixed2, probs2, x2, normed3,
 ):
     place = info[0]
 
@@ -290,7 +303,7 @@
     ck[...] = dot(mem[...], weights[:, 512:1024]).astype(BF)
     cv[...] = (dot(mem[...], weights[:, 1024:1536]) + bias(6)).astype(BF)
     cq[...] = (dot(normed2[...], weights[:, 0:512]) + bias(5)).astype(BF)
-    attend(cq, ck, cv, cross_visible(mask), mixed2, log2)
+    attend(cq, ck, cv, cross_visible(mask), mixed2, probs2)
     after_cross = x1[...] + (dot(mixed2[...], weights[:, 1536:2048]) + bias(7))
     x2[...] = after_cross
     normed3[...] = (norm(after_cross)[0] * bias(12) + bias(8)).astype(BF)
@@ -349,11 +362,11 @@
     ffg[...] = jnp.zeros_like(ffg)
     for group in range(FF // 512):
         grad = grad_hidden[:, 512 * group : 512 * group + 512]
-        d_up[:, 512 * group : 512 * group + 512] = dot(normed_t, grad).astype(BF)
+        d_up[group] = dot(normed_t, grad).astype(BF)
         ffg[group : group + 1, :] = row_sum(grad)
         part = dot_nt(grad, up[:, 512 * group : 512 * group + 512])
         grad_normed = part if grad_normed is None else grad_normed + part
-    take_blocks(order, base, (own_out, other_out), lambda index: d_up[rows16(index), :])
+    take_blocks(order, base, (own_out, other_out), lambda index: d_up[:, rows16(index), :])
     part, d_gain, d_shift = norm_back(x2[...], vecs[12:13, :], grad_normed)
     grads = grad_out[...]
     grad_x2[...] = grads.astype(F32) + part
@@ -364,7 +377,7 @@
 
 
 def cross_back_kernel(
-    base, order, info, weights, weights1, x1, normed2, mem, cq, ck, cv, mixed1, mixed2, log2, mask, grad_x2, vecs, small_in,
+    base, order, info, weights, weights1, x1, normed2, mem, cq, ck, cv, mixed1, mixed2, probs2, grad_x2, vecs, small_in,
     grad_x1, grad_mixed1, mem_keep, mem_send, small, own_out, other_out,
     d_weights, grad_mixed, dq, dk, dv, grad_mem,
 ):
@@ -374,7 +387,7 @@
     d_weights[:, 1536:2048] = dot_tn(mixed2[...], grad_y).astype(BF)
     small[7:8, :] = row_sum(grad_y)
     grad_mixed[...] = dot_nt(grad_y, weights[:, 1536:2048]).astype(BF)
-    attend_back(cq, ck, cv, cross_visible(mask), log2, grad_mixed, dq, dk, dv)
+    attend_back(cq, ck, cv, probs2, mixed2, grad_mixed, dq, dk, dv)
     memory_t = mem[...].T
     d_weights[:, 512:1024] = dot(memory_t, dk[...]).astype(BF)
     d_weights[:, 1024:1536] = dot(memory_t, dv[...]).astype(BF)
@@ -398,14 +411,14 @@
 
 
 def self_back_kernel(
-    base, order, info, weights, x0, normed1, q, k, v, log1, grad_x1, grad_mixed, vecs, small_in, ffg,
+    base, order, info, weights, x0, normed1, q, k, v, mixed1, probs1, grad_x1, grad_mixed, vecs, small_in, ffg,
     in_keep, in_send, own_out, other_out,
     d_weights, d_small, small, dq, dk, dv, grad_in,
 ):
-    place, length = info[0], info[1]
+    place = info[0]
     small[...] = small_in[...]
     rows = q.shape[0]
-    attend_back(q, k, v, self_visible(length, rows), log1, grad_mixed, dq, dk, dv)
+    attend_back(q, k, v, probs1, mixed1, grad_mixed, dq, dk, dv)
     normed_t = normed1[...].T
     for i, part in enumerate((dq, dk, dv)):
         d_weights[:, 512 * i : 512 * i + 512] = dot(normed_t, part[...]).astype(BF)
@@ -532,16 +545,16 @@
     ((1, 8, 16, 4), (4, 16, 8, 1)),
 )
 GATHER_KIND = dict(a=0, u=0, w=1)
-GATHER = "a:12 w:12 u:12 a:12 w:12 u:12 a:12 w:12 u:12"
-SCATTER_KIND = dict(d=2, u=2, c=0, s=0)
+GATHER = (
+    ("a", 12), ("w", 12), ("u", 12), ("a", 12), ("w", 12), ("u", 12), ("a", 12), ("w", 12), ("u", 12),
+)
+SCATTER_KIND = dict(d=2, u=2, f=2, c=0, s=0, a=0)
 SCATTER = (
-    "d:0 u:0 X:0 Y:0 d:12 s:3 u:0 c:0 d:0.3 o:4 s:0.6 c:0 u:0 s:0.3 d:1.5"
-    " c:0 u:0 d:0.6 s:1.5 u:0 c:0 h:0 s:1 m:0 c:0"
+    ("d", 0), ("u", 0), ("X", 0), ("Y", 0), ("d", 12), ("u", 0), ("c", 3),
+    ("s", 0), ("d", 0.3), ("o", 4), ("s", 0.6), ("c", 0), ("u", 0), ("s", 0.3),
+    ("d", 1.5), ("c", 0), ("u", 0), ("s", 1.5), ("c", 0), ("m", 0), ("udf", 0),
+    ("f", 0.6), ("h", 0), ("csa", 0), ("a", 0),
 )
-
-
-def plan(text):
-    return [(item.split(":")[0], int(float(item.split(":")[1]) * EVENT) + 1) for item in text.split()]
 
 
 def permute(value, pairs):
@@ -579,21 +592,25 @@
 
 
 class Scatter:
-    def __init__(self, line, name, own, other):
-        self.line, self.name, self.own, self.hop = line, name, own, 4
-        self.hops = HOPS[SCATTER_KIND[name]]
+    def __init__(self, line, name, hop, parts):
+        self.line, self.name, self.hop, self.parts = line, name, hop, parts
+        self.hops, self.axis = HOPS[SCATTER_KIND[name]], (1 if name in "duf" else 2)
+
+    @classmethod
+    def begin(cls, line, name, own, other):
         with jax.named_scope(f"scatter_{name}_core"):
-            self.coming = permute(other, CORE)
+            return cls(line, name, 4, [(own, permute(other, CORE))])
 
     def step(self, cost):
         self.hop -= 1
-        dims = (1 << self.hop,) + self.own.shape[1:]
-        send, self.own = self.line.call(
-            add_kernel, f"add_{self.name}{self.hop}", [self.own, self.coming],
-            [(dims, BF), (dims, BF if self.hop else F32)], flops=cost,
+        dims = list(self.parts[0][0].shape)
+        dims[0], dims[self.axis] = 1 << self.hop, sum(own.shape[self.axis] for own, _ in self.parts)
+        send, own = self.line.call(
+            functools.partial(add_kernel, self.axis), f"add_{self.name}{self.hop}", [v for p in self.parts for v in p],
+            [(tuple(dims), BF), (tuple(dims), BF if self.hop else F32)], flops=cost,
         )
         with jax.named_scope(f"scatter_{self.name}_hop{self.hop}"):
-            self.coming = permute(send, self.hops[self.hop])
+            self.parts = [(own, permute(send, self.hops[self.hop]))]
 
 
 def small_rows(biases, gains, ffn_bias):
@@ -661,8 +678,8 @@
         chunks["w"].start()
         new = swap(sent, "in")
         chunks["u"].start()
-        for name, cost in plan(GATHER):
-            chunks[name].step(new if name == "a" and chunks[name].hop == 2 else None, cost)
+        for name, cost in GATHER:
+            chunks[name].step(new if name == "a" and chunks[name].hop == 2 else None, int(cost * EVENT))
         a_pieces = chunks["a"].finish()
         halves_of = (16, 16)
         base = lambda kind: BLOCKS * kind
@@ -687,25 +704,27 @@
     vec = ((16, D), F32)
     units = ((8, 512), F32)
     blocks = lambda *dims: [None if n is None else ((n,) + dims, BF) for n in halves_of]
-    weights1, vecs, ffb, x0, normed1, q, k, v, mixed1, log1, x1, normed2 = line.call(
+    weights1, vecs, ffb, x0, normed1, q, k, v, mixed1, probs1, x1, normed2 = line.call(
         functools.partial(self_forward_kernel, base(GATHER_KIND["a"])), "self_forward", [order, info, *a_pieces, kept, new],
         [
             ((D, 2048), BF), vec, units, (wide, BF), (wide, BF), (wide, BF), (wide, BF), (wide, BF), (wide, BF),
-            ((HEADS, tgt), F32), (wide, F32), (wide, BF),
+            ((HEADS, tgt, tgt), BF), (wide, F32), (wide, BF),
         ],
         [pltpu.VMEM((BLOCKS, 16, 128), BF)], 2,
     )
-    weights2, mem, cq, ck, cv, mixed2, log2, x2, normed3 = line.call(
+    if permuted:
+        w_pieces = chunks["w"].finish(True)
+    weights2, mem, cq, ck, cv, mixed2, probs2, x2, normed3 = line.call(
         functools.partial(cross_forward_kernel, base(GATHER_KIND["a"])), "cross_forward",
         [order, info, *a_pieces, kept, new, mask, vecs, x1, normed2],
         [
             ((D, 2048), BF), ((src, D), BF), (wide, BF), ((src, D), BF), ((src, D), BF), (wide, BF),
-            ((HEADS, tgt), F32), (wide, F32), (wide, BF),
+            ((HEADS, src, tgt), BF), (wide, F32), (wide, BF),
         ],
         [], 2,
     )
     if permuted:
-        w_pieces, u_pieces = chunks["w"].finish(True), chunks["u"].finish(True)
+        u_pieces = chunks["u"].finish(True)
     else:
         u_pieces, w_pieces = [cut(w_up), None, None, None], [w_down.reshape(BLOCKS, 4, 16, D), None, None, None]
     bases = (base(GATHER_KIND["u"]), base(GATHER_KIND["w"]), base(SCATTER_KIND["d"]))
@@ -716,21 +735,21 @@
         [pltpu.VMEM((128, 16, D), BF), pltpu.VMEM((128, 16, D), BF), pltpu.VMEM(wide, BF)], 2,
     )
     if permuted:
-        chunks = dict(d=Scatter(line, "d", *d_down))
+        chunks = dict(d=Scatter.begin(line, "d", *d_down))
         out_got = swap(out_send, "out")
     grad_x2, small, ffg, *d_up = line.call(
         functools.partial(ffn_back_kernel, base(SCATTER_KIND["u"])), "ffn_back",
         [order, info, up, grad_hidden, g_full, x2, normed3, vecs],
-        [(wide, F32), vec, units, *blocks(16, FF)],
-        [pltpu.VMEM((D, FF), BF)], 2,
+        [(wide, F32), vec, units, *blocks(4, 16, 512)],
+        [pltpu.VMEM((4, D, 512), BF)], 2,
     )
 
     def cross_back():
         return line.call(
             functools.partial(cross_back_kernel, base(SCATTER_KIND["c"])), "cross_back",
             [
-                order, info, weights2, weights1, x1, normed2, mem, cq, ck, cv, mixed1, mixed2, log2, mask, grad_x2,
-                vecs, small,
+                order, info, weights2, weights1, x1, normed2, mem, cq, ck, cv, mixed1, mixed2, probs2, grad_x2, vecs,
+                small,
             ],
             [(wide, F32), (wide, BF), ((sources, D), F32), ((sources, D), BF), vec, *blocks(16, 2560)],
             [
@@ -743,7 +762,7 @@
     def self_back(grad_x1, grad_mixed1, small):
         return line.call(
             functools.partial(self_back_kernel, base(SCATTER_KIND["s"])), "self_back",
-            [order, info, weights1, x0, normed1, q, k, v, log1, grad_x1, grad_mixed1, vecs, small, ffg],
+            [order, info, weights1, x0, normed1, q, k, v, mixed1, probs1, grad_x1, grad_mixed1, vecs, small, ffg],
             [((rows, D), F32), ((rows, D), BF), *blocks(16, 1664)],
             [
                 pltpu.VMEM((D, 1536), BF), pltpu.VMEM((BLOCKS, 16, 128), BF), pltpu.VMEM((16, D), F32),
@@ -756,22 +775,24 @@
         return line.call(halves_kernel, f"halves_{name}", [info, kept, got], [((2,) + kept.shape, kept.dtype)], (), 1)[0]
 
     if permuted:
-        chunks["u"] = Scatter(line, "u", *d_up)
+        chunks["u"] = Scatter.begin(line, "u", *d_up)
         lasts = dict(
-            d=(last_kernel, [((4, 16, D), F32)]),
-            u=(last_kernel, [((16, FF), F32)]),
-            c=(last_cross_kernel, [((16, n), F32) for n in (512, 1024, 512, 512)]),
-            s=(last_self_kernel, [((16, 1536), F32), ((3, 16), F32), ((16, 10), F32), ((1, 64), F32)]),
+            f=(last_ffn_kernel, [((16, FF), F32), ((64, D), F32)]),
+            a=(
+                last_attention_kernel,
+                [((16, n), F32) for n in (512, 1024, 512, 512, 1536)]
+                + [((3, 16), F32), ((16, 10), F32), ((1, 64), F32)],
+            ),
         )
         done = {}
-        for name, cost in plan(SCATTER):
+        for name, cost in SCATTER:
             if name == "X":
                 grad_x1, grad_mixed1, mem_keep, mem_send, small, *d_cross = cross_back()
-                chunks["c"] = Scatter(line, "c", *d_cross)
+                chunks["c"] = Scatter.begin(line, "c", *d_cross)
                 mem_got = swap(mem_send, "memory")
             elif name == "Y":
                 in_keep, in_send, *d_self = self_back(grad_x1, grad_mixed1, small)
-                chunks["s"] = Scatter(line, "s", *d_self)
+                chunks["s"] = Scatter.begin(line, "s", *d_self)
                 in_got = swap(in_send, "hidden")
             elif name == "o":
                 output = both(out_keep, out_got, "out")
@@ -779,21 +800,22 @@
                 grad_memory = both(mem_keep, mem_got, "memory")
             elif name == "h":
                 grad_hidden_in = both(in_keep, in_got, "hidden")
+            elif len(name) > 1:
+                first, second, joined = name
+                hop = chunks[first].hop
+                chunks[joined] = Scatter(line, joined, hop, chunks[first].parts + chunks[second].parts)
             elif chunks[name].hop:
-                chunks[name].step(cost)
+                chunks[name].step(int(cost * EVENT))
             else:
                 kernel, shapes = lasts[name]
-                mine = [me] if name == "s" else []
+                mine = [me] if name == "a" else []
                 done[name] = line.call(
-                    kernel, f"last_{name}", [*mine, chunks[name].own, chunks[name].coming], shapes,
-                    scalars=len(mine), flops=cost,
+                    kernel, f"last_{name}", mine + [v for p in chunks[name].parts for v in p], shapes,
+                    scalars=len(mine), flops=int(cost * EVENT),
                 )
-        g_cq, g_ckv, g_co, g_out = done["c"]
-        g_qkv, g_gains, g_biases, g_units = done["s"]
-        rest = (
-            g_qkv, g_out, g_cq, g_ckv, g_co, done["u"][0], done["d"][0].reshape(64, D), g_gains.T, g_biases,
-            g_units.reshape(64),
-        )
+        g_up, g_down = done["f"]
+        g_cq, g_ckv, g_co, g_out, g_qkv, g_gains, g_biases, g_units = done["a"]
+        rest = (g_qkv, g_out, g_cq, g_ckv, g_co, g_up, g_down, g_gains.T, g_biases, g_units.reshape(64))
     else:
         grad_x1, grad_mixed1, mem_keep, mem_send, small, *d_cross = cross_back()
         in_keep, in_send, *d_self = self_back(grad_x1, grad_mixed1, small)
@@ -809,7 +831,7 @@
             lax.psum_scatter(d, BOTH, scatter_dimension=0, tiled=True)
             for d in (
                 d_self[:, :, :1536].reshape(D, 1536), d_cross[:, 2048:], d_cross[:, :512], d_cross[:, 512:1536],
-                d_cross[:, 1536:2048], d_up.reshape(D, FF), d_down.reshape(FF, D), columns[:, 10:], columns[:, :10],
+                d_cross[:, 1536:2048], d_up.transpose(0, 2, 1, 3).reshape(D, FF), d_down.reshape(FF, D), columns[:, 10:], columns[:, :10],
                 d_unit,
             )
         )

time: 134 us -> 131 us (0.978)
  waiting for transfers between devices: 45.9 us -> 42 us
  starting transfers between devices: 47.4 us -> 50.7 us
  Pallas kernels: 39.1 us -> 36.8 us
    ppermute x38, starting transfers between devices: 44.4 us -> 48.4 us  [permute(): return lax.ppermute(value, BOTH, pairs)]
    ppermute x38, waiting for transfers between devices: 42 us -> 38.1 us  [permute(): return lax.ppermute(value, BOTH, pairs)]
    pallas_call x40 -> x38, Pallas kernels: 36.9 us -> 34.6 us  [call(): pl.pallas_call(body, name=name, out_shape=[shape(*o) for o in made] + [sh...]
  transfers between devices with their start and end apart: 42 -> 42, of which waited for: 16 -> 14; matrix products, arithmetic and copies ran while one was open for 0% -> 0% of each run, Pallas kernels for 23% -> 22%
where the time goes in v3:
time: 131 us
  starting transfers between devices  50.7 us (39%)
  waiting for transfers between devices  42 us (32%)
  Pallas kernels  36.8 us (28%)
    ppermute x38, starting transfers between devices, permute(): return lax.ppermute(value, BOTH, pairs)  48.4 us
    ppermute x38, waiting for transfers between devices, permute(): return lax.ppermute(value, BOTH, pairs)  38.1 us
    pallas_call x38, Pallas kernels, call(): pl.pallas_call(body, name=name, out_shape=[shape(*o) for o in made] + [sh...  34.6 us
    ppermute x4, waiting for transfers between devices, swap(): return lax.ppermute(value, 'seq', [(0, 1), (1, 0)])  3.93 us
  transfers between devices with their start and end apart: 42, of which 14 were waited for; matrix products, arithmetic and copies ran while one was open for 0% of the time, Pallas kernels for 22%

profile of v3, /device:TPU:0, one launch (start us, length us, event | category | flops | bytes accessed | tf_op | source)
XLA Modules:
  0.0 130.5 jit_solution(17891039080966239256)
XLA Ops:
  0.7 2.2 %pack.1 = (s32[96]{0:T(128)S(1)}, s32[2]{0:T(128)S(1)}, bf16[1,16,4224]{2,1,0:T(8,128)(2,1)S(1)}, bf16[16,2048]{1,0:T(8,128)(2,1)S(1)}, bf16[64,512]{1,0:T(8,128...) custom-call(s32[1]{0:T(128)} %bitcast.me.refs_0_, ...), custom_call_target="tpu_custom_call" | custom-call | tf_op jit(solution)/shard_map/pack/pallas_call | solution.py:631
  2.9 3.1 %collective-permute-start.2 = (bf16[1,16,4224]{2,1,0:T(8,128)(2,1)S(1)}, bf16[1,16,4224]{2,1,0:T(8,128)(2,1)S(1)}, u32[]{:S(2)}, u32[]{:S(2)}) collective-permute-start(bf16[1,16,4224]{2,1,0:T(8,128)(2,1)S(1)} %get-tuple-element.163.refs_0_), channel_id=1, source_target_pairs={{0,8},{1,9},{2,18},{3,19},{4,12},{5,13},{6,22},{7,23},{8,0},{9,1},... | collective-permute-start | bytes 405512 | tf_op jit(solution)/shard_map/gather_a_hop0/ppermute | solution.py:561
  8.0 2.0 %collective-permute-done.2.refs_1_ = bf16[1,16,4224]{2,1,0:T(8,128)(2,1)S(1)} collective-permute-done((bf16[1,16,4224]{2,1,0:T(8,128)(2,1)S(1)}, bf16[1,16,4224]{2,1,0:T(8,128)(2,1)S(1)}, u32[]{:S(2)}, u32[]{:S(2)}) %collective-permute-start.2) | collective-permute-done | bytes 135200 | tf_op jit(solution)/shard_map/gather_a_hop0/ppermute | solution.py:561
  10.1 2.4 %collective-permute-start.5 = (bf16[2,16,4224]{2,1,0:T(8,128)(2,1)S(1)}, bf16[2,16,4224]{2,1,0:T(8,128)(2,1)S(1)}, u32[]{:S(2)}, u32[]{:S(2)}) collective-permute-start(bf16[2,16,4224]{2,1,0:T(8,128)(2,1)S(1)} %get-tuple-element.169.refs_0_), channel_id=1, source_target_pairs={{0,16},{1,17},{2,10},{3,11},{4,20},{5,21},{6,14},{7,15},{8,24},{9,... | collective-permute-start | bytes 811016 | tf_op jit(solution)/shard_map/gather_a_hop1/ppermute | solution.py:561
  12.5 1.9 %collective-permute-start.3 = (bf16[2,16,2048]{2,1,0:T(8,128)(2,1)S(1)}, bf16[2,16,2048]{2,1,0:T(8,128)(2,1)S(1)}, u32[]{:S(2)}, u32[]{:S(2)}) collective-permute-start(bf16[2,16,2048]{2,1,0:T(8,128)(2,1)S(1)} %get-tuple-element.167.refs_0_), channel_id=1, source_target_pairs={{0,16},{1,17},{2,10},{3,11},{4,20},{5,21},{6,14},{7,15},{8,24},{9,... | collective-permute-start | bytes 393224 | tf_op jit(solution)/shard_map/gather_u_hop1/ppermute | solution.py:561
  15.9 2.9 %collective-permute-done.5.refs_1_ = bf16[2,16,4224]{2,1,0:T(8,128)(2,1)S(1)} collective-permute-done((bf16[2,16,4224]{2,1,0:T(8,128)(2,1)S(1)}, bf16[2,16,4224]{2,1,0:T(8,128)(2,1)S(1)}, u32[]{:S(2)}, u32[]{:S(2)}) %collective-permute-start.5) | collective-permute-done | bytes 270368 | tf_op jit(solution)/shard_map/gather_a_hop1/ppermute | solution.py:561
  18.8 3.9 %collective-permute-done.6.refs_2_.refs_7_.refs_13_ = bf16[512,512]{1,0:T(8,128)(2,1)S(1)} collective-permute-done((bf16[512,512]{1,0:T(8,128)(2,1)S(1)}, bf16[512,512]{1,0:T(8,128)(2,1)S(1)}, u32[]{:S(2)}, u32[]{:S(2)}) %collective-permute-start.6) | collective-permute-done | bytes 524320 | tf_op jit(solution)/shard_map/swap_in/ppermute | solution.py:665
  22.9 2.0 %collective-permute-start.7 = (bf16[4,16,2048]{2,1,0:T(8,128)(2,1)S(1)}, bf16[4,16,2048]{2,1,0:T(8,128)(2,1)S(1)}, u32[]{:S(2)}, u32[]{:S(2)}) collective-permute-start(bf16[4,16,2048]{2,1,0:T(8,128)(2,1)S(1)} %get-tuple-element.174.refs_0_), channel_id=1, source_target_pairs={{0,1},{1,0},{2,6},{3,7},{4,5},{5,4},{6,2},{7,3},{8,9},{9,8},{10,14... | collective-permute-start | bytes 786440 | tf_op jit(solution)/shard_map/gather_u_hop2/ppermute | solution.py:561
  26.5 5.6 %collective-permute-done.9.refs_1_ = bf16[4,16,4224]{2,1,0:T(8,128)(2,1)S(1)} collective-permute-done((bf16[4,16,4224]{2,1,0:T(8,128)(2,1)S(1)}, bf16[4,16,4224]{2,1,0:T(8,128)(2,1)S(1)}, u32[]{:S(2)}, u32[]{:S(2)}) %collective-permute-start.9) | collective-permute-done | bytes 540704 | tf_op jit(solution)/shard_map/gather_a_hop2/ppermute | solution.py:561
  32.3 1.7 %collective-permute-start.11 = (bf16[8,16,4224]{2,1,0:T(8,128)(2,1)S(1)}, bf16[8,16,4224]{2,1,0:T(8,128)(2,1)S(1)}, u32[]{:S(2)}, u32[]{:S(2)}) collective-permute-start(bf16[8,16,4224]{2,1,0:T(8,128)(2,1)S(1)} %get-tuple-element.181.refs_2_), channel_id=1, source_target_pairs={{0,4},{1,5},{2,3},{3,2},{4,0},{5,1},{6,7},{7,6},{8,12},{9,13},{10,... | collective-permute-start | bytes 3244040 | tf_op jit(solution)/shard_map/gather_a_hop3/ppermute | solution.py:561
  34.0 2.6 %collective-permute-start.14 = (bf16[8,4,16,512]{3,2,1,0:T(8,128)(2,1)S(1)}, bf16[8,4,16,512]{3,2,1,0:T(8,128)(2,1)S(1)}, u32[]{:S(2)}, u32[]{:S(2)}) collective-permute-start(bf16[8,4,16,512]{3,2,1,0:T(8,128)(2,1)S(1)} %get-tuple-element.188.refs_6_), channel_id=1, source_target_pairs={{0,16},{1,17},{2,10},{3,11},{4,20},{5,21},{6,14},{7,15},{8,24},{9,... | collective-permute-start | bytes 1572872 | tf_op jit(solution)/shard_map/gather_w_hop3/ppermute | solution.py:561
  36.6 10.9 %collective-permute-done.11.refs_3_ = bf16[8,16,4224]{2,1,0:T(8,128)(2,1)S(1)} collective-permute-done((bf16[8,16,4224]{2,1,0:T(8,128)(2,1)S(1)}, bf16[8,16,4224]{2,1,0:T(8,128)(2,1)S(1)}, u32[]{:S(2)}, u32[]{:S(2)}) %collective-permute-start.11) | collective-permute-done | bytes 1081376 | tf_op jit(solution)/shard_map/gather_a_hop3/ppermute | solution.py:561
  48.1 1.6 %collective-permute-start.10 = (bf16[8,16,2048]{2,1,0:T(8,128)(2,1)S(1)}, bf16[8,16,2048]{2,1,0:T(8,128)(2,1)S(1)}, u32[]{:S(2)}, u32[]{:S(2)}) collective-permute-start(bf16[8,16,2048]{2,1,0:T(8,128)(2,1)S(1)} %get-tuple-element.180.refs_2_), channel_id=1, source_target_pairs={{0,4},{1,5},{2,3},{3,2},{4,0},{5,1},{6,7},{7,6},{8,12},{9,13},{10,... | collective-permute-start | bytes 1572872 | tf_op jit(solution)/shard_map/gather_u_hop3/ppermute | solution.py:561
  50.2 3.5 %self_forward.1 = (bf16[512,2048]{1,0:T(8,128)(2,1)S(1)}, f32[16,512]{1,0:T(8,128)S(1)}, f32[8,512]{1,0:T(8,128)S(1)}, bf16[256,512]{1,0:T(8,128)(2,1)S(1)}, bf1...) custom-call(s32[96]{0:T(128)S(1)} %get-tuple-element.160.refs_0_, ...), custom_call_target="tpu_custom_call" | custom-call | flops 1 | bytes 1 | tf_op jit(solution)/shard_map/self_forward/pallas_call | solution.py:503
  54.0 4.9 %cross_forward.1 = (bf16[512,2048]{1,0:T(8,128)(2,1)S(1)}, bf16[512,512]{1,0:T(8,128)(2,1)S(1)}, bf16[256,512]{1,0:T(8,128)(2,1)S(1)}, bf16[512,512]{1,0:T(8,128...) custom-call(s32[96]{0:T(128)S(1)} %get-tuple-element.160.refs_0_, ...), custom_call_target="tpu_custom_call" | custom-call | flops 1 | bytes 1 | tf_op jit(solution)/shard_map/cross_forward/pallas_call | solution.py:503
  61.0 4.7 %ffn.1 = (bf16[128,512]{1,0:T(8,128)(2,1)S(1)}, bf16[128,512]{1,0:T(8,128)(2,1)S(1)}, bf16[512,2048]{1,0:T(8,128)(2,1)S(1)}, bf16[256,2048]{1,0:T(8,128)(2,1)S(1...) custom-call(s32[96]{0:T(128)S(1)} %get-tuple-element.160.refs_0_, ...), custom_call_target="tpu_custom_call" | custom-call | flops 1 | bytes 1 | tf_op jit(solution)/shard_map/ffn/pallas_call | solution.py:503
  66.1 2.8 %ffn_back.1 = (f32[256,512]{1,0:T(8,128)S(1)}, f32[16,512]{1,0:T(8,128)S(1)}, f32[8,512]{1,0:T(8,128)S(1)}, bf16[16,4,16,512]{3,2,1,0:T(8,128)(2,1)S(1)}, bf16[1...) custom-call(s32[96]{0:T(128)S(1)} %get-tuple-element.160.refs_0_, s32[2]{0:T(128)S(1)} %get-tuple-element.159.refs_1_.refs_0_, ...), custom_call_target="tpu_custom_call" | custom-call | flops 1 | bytes 1 | tf_op jit(solution)/shard_map/ffn_back/pallas_call | solution.py:503
  69.4 1.7 %collective-permute-start.21 = (bf16[8,4,16,512]{3,2,1,0:T(8,128)(2,1)S(1)}, bf16[8,4,16,512]{3,2,1,0:T(8,128)(2,1)S(1)}, u32[]{:S(2)}, u32[]{:S(2)}) collective-permute-start(bf16[8,4,16,512]{3,2,1,0:T(8,128)(2,1)S(1)} %get-tuple-element.208), channel_id=1, source_target_pairs={{0,4},{1,5},{2,3},{3,2},{4,0},{5,1},{6,7},{7,6},{8,12},{9,13},{10,... | collective-permute-start | bytes 1572872 | tf_op jit(solution)/shard_map/scatter_d_hop3/ppermute | solution.py:561
  71.9 6.3 %cross_back.1 = (f32[256,512]{1,0:T(8,128)S(1)}, bf16[256,512]{1,0:T(8,128)(2,1)S(1)}, f32[256,512]{1,0:T(8,128)S(1)}, bf16[256,512]{1,0:T(8,128)(2,1)S(1)}, f32...) custom-call(s32[96]{0:T(128)S(1)} %get-tuple-element.160.refs_0_, ...), custom_call_target="tpu_custom_call" | custom-call | flops 1 | bytes 1 | tf_op jit(solution)/shard_map/cross_back/pallas_call | solution.py:503
  78.4 1.6 %collective-permute-start.26 = (bf16[8,4,16,512]{3,2,1,0:T(8,128)(2,1)S(1)}, bf16[8,4,16,512]{3,2,1,0:T(8,128)(2,1)S(1)}, u32[]{:S(2)}, u32[]{:S(2)}) collective-permute-start(bf16[8,4,16,512]{3,2,1,0:T(8,128)(2,1)S(1)} %get-tuple-element.243), channel_id=1, source_target_pairs={{0,4},{1,5},{2,3},{3,2},{4,0},{5,1},{6,7},{7,6},{8,12},{9,13},{10,... | collective-permute-start | bytes 1572872 | tf_op jit(solution)/shard_map/scatter_u_hop3/ppermute | solution.py:561
  80.0 4.3 %self_back.1 = (f32[128,512]{1,0:T(8,128)S(1)}, bf16[128,512]{1,0:T(8,128)(2,1)S(1)}, bf16[16,16,1664]{2,1,0:T(8,128)(2,1)S(1)}, bf16[16,16,1664]{2,1,0:T(8,128)(2,1)S(1)}, f32[8,128]{1,0:T(8,128)S(1)}) custom-call(s32[96]{0:T(128)S(1)} %get-tuple-element.160.refs_0_, s32[2]{0:T(128)S(1)} %get-tuple-element.159.refs_1_.refs_0_, ...), custom_call_target="tpu_custom_call" | custom-call | flops 1 | bytes 1 | tf_op jit(solution)/shard_map/self_back/pallas_call | solution.py:503
  84.5 3.1 %collective-permute-done.26.refs_1_ = bf16[8,4,16,512]{3,2,1,0:T(8,128)(2,1)S(1)} collective-permute-done((bf16[8,4,16,512]{3,2,1,0:T(8,128)(2,1)S(1)}, bf16[8,4,16,512]{3,2,1,0:T(8,128)(2,1)S(1)}, u32[]{:S(2)}, u32[]{:S(2)}) %collective-permute-start.26) | collective-permute-done | bytes 524320 | tf_op jit(solution)/shard_map/scatter_u_hop3/ppermute | solution.py:561
  88.1 1.7 %collective-permute-start.29 = (bf16[8,16,2560]{2,1,0:T(8,128)(2,1)S(1)}, bf16[8,16,2560]{2,1,0:T(8,128)(2,1)S(1)}, u32[]{:S(2)}, u32[]{:S(2)}) collective-permute-start(bf16[8,16,2560]{2,1,0:T(8,128)(2,1)S(1)} %get-tuple-element.255), channel_id=1, source_target_pairs={{0,4},{1,5},{2,3},{3,2},{4,0},{5,1},{6,7},{7,6},{8,12},{9,13},{10,... | collective-permute-start | bytes 1966088 | tf_op jit(solution)/shard_map/scatter_c_hop3/ppermute | solution.py:561
  90.5 2.6 %collective-permute-start.23 = (bf16[4,4,16,512]{3,2,1,0:T(8,128)(2,1)S(1)}, bf16[4,4,16,512]{3,2,1,0:T(8,128)(2,1)S(1)}, u32[]{:S(2)}, u32[]{:S(2)}) collective-permute-start(bf16[4,4,16,512]{3,2,1,0:T(8,128)(2,1)S(1)} %get-tuple-element.237), channel_id=1, source_target_pairs={{0,16},{1,17},{2,10},{3,11},{4,20},{5,21},{6,14},{7,15},{8,24},{9,... | collective-permute-start | bytes 786440 | tf_op jit(solution)/shard_map/scatter_d_hop2/ppermute | solution.py:561
  94.2 5.4 %collective-permute-done.23.refs_1_ = bf16[4,4,16,512]{3,2,1,0:T(8,128)(2,1)S(1)} collective-permute-done((bf16[4,4,16,512]{3,2,1,0:T(8,128)(2,1)S(1)}, bf16[4,4,16,512]{3,2,1,0:T(8,128)(2,1)S(1)}, u32[]{:S(2)}, u32[]{:S(2)}) %collective-permute-start.23) | collective-permute-done | bytes 262176 | tf_op jit(solution)/shard_map/scatter_d_hop2/ppermute | solution.py:561
  100.9 2.4 %collective-permute-done.30.refs_1_ = bf16[8,16,1664]{2,1,0:T(8,128)(2,1)S(1)} collective-permute-done((bf16[8,16,1664]{2,1,0:T(8,128)(2,1)S(1)}, bf16[8,16,1664]{2,1,0:T(8,128)(2,1)S(1)}, u32[]{:S(2)}, u32[]{:S(2)}) %collective-permute-start.30) | collective-permute-done | bytes 426016 | tf_op jit(solution)/shard_map/scatter_s_hop3/ppermute | solution.py:561
  105.8 2.2 %collective-permute-start.33 = (bf16[2,4,16,512]{3,2,1,0:T(8,128)(2,1)S(1)}, bf16[2,4,16,512]{3,2,1,0:T(8,128)(2,1)S(1)}, u32[]{:S(2)}, u32[]{:S(2)}) collective-permute-start(bf16[2,4,16,512]{3,2,1,0:T(8,128)(2,1)S(1)} %get-tuple-element.266), channel_id=1, source_target_pairs={{0,8},{1,9},{2,18},{3,19},{4,12},{5,13},{6,22},{7,23},{8,0},{9,1},... | collective-permute-start | bytes 393224 | tf_op jit(solution)/shard_map/scatter_d_hop1/ppermute | solution.py:561
  109.4 2.9 %collective-permute-start.39 = (bf16[2,16,1664]{2,1,0:T(8,128)(2,1)S(1)}, bf16[2,16,1664]{2,1,0:T(8,128)(2,1)S(1)}, u32[]{:S(2)}, u32[]{:S(2)}) collective-permute-start(bf16[2,16,1664]{2,1,0:T(8,128)(2,1)S(1)} %get-tuple-element.282), channel_id=1, source_target_pairs={{0,16},{1,17},{2,10},{3,11},{4,20},{5,21},{6,14},{7,15},{8,24},{9,... | collective-permute-start | bytes 319496 | tf_op jit(solution)/shard_map/scatter_s_hop1/ppermute | solution.py:561
  112.3 2.8 %collective-permute-start.31 = (bf16[2,4,16,512]{3,2,1,0:T(8,128)(2,1)S(1)}, bf16[2,4,16,512]{3,2,1,0:T(8,128)(2,1)S(1)}, u32[]{:S(2)}, u32[]{:S(2)}) collective-permute-start(bf16[2,4,16,512]{3,2,1,0:T(8,128)(2,1)S(1)} %get-tuple-element.262), channel_id=1, source_target_pairs={{0,8},{1,9},{2,18},{3,19},{4,12},{5,13},{6,22},{7,23},{8,0},{9,1},... | collective-permute-start | bytes 393224 | tf_op jit(solution)/shard_map/scatter_u_hop1/ppermute | solution.py:561
  115.3 2.6 %collective-permute-start.38 = (bf16[2,16,2560]{2,1,0:T(8,128)(2,1)S(1)}, bf16[2,16,2560]{2,1,0:T(8,128)(2,1)S(1)}, u32[]{:S(2)}, u32[]{:S(2)}) collective-permute-start(bf16[2,16,2560]{2,1,0:T(8,128)(2,1)S(1)} %get-tuple-element.280), channel_id=1, source_target_pairs={{0,16},{1,17},{2,10},{3,11},{4,20},{5,21},{6,14},{7,15},{8,24},{9,... | collective-permute-start | bytes 491528 | tf_op jit(solution)/shard_map/scatter_c_hop1/ppermute | solution.py:561
  118.5 1.7 %collective-permute-done.31.refs_1_ = bf16[2,4,16,512]{3,2,1,0:T(8,128)(2,1)S(1)} collective-permute-done((bf16[2,4,16,512]{3,2,1,0:T(8,128)(2,1)S(1)}, bf16[2,4,16,512]{3,2,1,0:T(8,128)(2,1)S(1)}, u32[]{:S(2)}, u32[]{:S(2)}) %collective-permute-start.31) | collective-permute-done | bytes 131104 | tf_op jit(solution)/shard_map/scatter_u_hop1/ppermute | solution.py:561
  122.5 2.6 %collective-permute-start.40 = (bf16[1,16,2560]{2,1,0:T(8,128)(2,1)S(1)}, bf16[1,16,2560]{2,1,0:T(8,128)(2,1)S(1)}, u32[]{:S(2)}, u32[]{:S(2)}) collective-permute-start(bf16[1,16,2560]{2,1,0:T(8,128)(2,1)S(1)} %get-tuple-element.291), channel_id=1, source_target_pairs={{0,8},{1,9},{2,18},{3,19},{4,12},{5,13},{6,22},{7,23},{8,0},{9,1},... | collective-permute-start | bytes 245768 | tf_op jit(solution)/shard_map/scatter_c_hop0/ppermute | solution.py:561
  (91 shorter events, 27.1 us)
Async XLA Ops:
  2.9 7.2 %collective-permute-start.2 = (bf16[1,16,4224]{2,1,0:T(8,128)(2,1)S(1)}, bf16[1,16,4224]{2,1,0:T(8,128)(2,1)S(1)}, u32[]{:S(2)}, u32[]{:S(2)}) collective-permute-start(bf16[1,16,4224]{2,1,0:T(8,128)(2,1)S(1)} %get-tuple-element.163.refs_0_), channel_id=1, source_target_pairs={{0,8},{1,9},{2,18},{3,19},{4,12},{5,13},{6,22},{7,23},{8,0},{9,1},... | collective-permute-start | bytes 405512 | tf_op jit(solution)/shard_map/gather_a_hop0/ppermute | solution.py:561
  5.9 6.5 %collective-permute-start.1 = (bf16[1,4,16,512]{3,2,1,0:T(8,128)(2,1)S(1)}, bf16[1,4,16,512]{3,2,1,0:T(8,128)(2,1)S(1)}, u32[]{:S(2)}, u32[]{:S(2)}) collective-permute-start(bf16[1,4,16,512]{3,2,1,0:T(8,128)(2,1)S(1)} %bitcast.9), channel_id=1, source_target_pairs={{0,1},{1,0},{2,6},{3,7},{4,5},{5,4},{6,2},{7,3},{8,9},{9,8},{10,14... | collective-permute-start | bytes 196616 | tf_op jit(solution)/shard_map/gather_w_hop0/ppermute | solution.py:561
  7.9 14.8 %collective-permute-start.6 = (bf16[512,512]{1,0:T(8,128)(2,1)S(1)}, bf16[512,512]{1,0:T(8,128)(2,1)S(1)}, u32[]{:S(2)}, u32[]{:S(2)}) collective-permute-start(bf16[512,512]{1,0:T(8,128)(2,1)S(1)} %get-tuple-element.170), channel_id=1, source_target_pairs={{0,1},{1,0},{2,3},{3,2},{4,5},{5,4},{6,7},{7,6},{8,9},{9,8},{10,11... | collective-permute-start | bytes 1572872 | tf_op jit(solution)/shard_map/swap_in/ppermute | solution.py:665
  10.1 8.7 %collective-permute-start.5 = (bf16[2,16,4224]{2,1,0:T(8,128)(2,1)S(1)}, bf16[2,16,4224]{2,1,0:T(8,128)(2,1)S(1)}, u32[]{:S(2)}, u32[]{:S(2)}) collective-permute-start(bf16[2,16,4224]{2,1,0:T(8,128)(2,1)S(1)} %get-tuple-element.169.refs_0_), channel_id=1, source_target_pairs={{0,16},{1,17},{2,10},{3,11},{4,20},{5,21},{6,14},{7,15},{8,24},{9,... | collective-permute-start | bytes 811016 | tf_op jit(solution)/shard_map/gather_a_hop1/ppermute | solution.py:561
  12.5 10.4 %collective-permute-start.3 = (bf16[2,16,2048]{2,1,0:T(8,128)(2,1)S(1)}, bf16[2,16,2048]{2,1,0:T(8,128)(2,1)S(1)}, u32[]{:S(2)}, u32[]{:S(2)}) collective-permute-start(bf16[2,16,2048]{2,1,0:T(8,128)(2,1)S(1)} %get-tuple-element.167.refs_0_), channel_id=1, source_target_pairs={{0,16},{1,17},{2,10},{3,11},{4,20},{5,21},{6,14},{7,15},{8,24},{9,... | collective-permute-start | bytes 393224 | tf_op jit(solution)/shard_map/gather_u_hop1/ppermute | solution.py:561
  14.4 8.5 %collective-permute-start.4 = (bf16[2,4,16,512]{3,2,1,0:T(8,128)(2,1)S(1)}, bf16[2,4,16,512]{3,2,1,0:T(8,128)(2,1)S(1)}, u32[]{:S(2)}, u32[]{:S(2)}) collective-permute-start(bf16[2,4,16,512]{3,2,1,0:T(8,128)(2,1)S(1)} %get-tuple-element.168.refs_0_), channel_id=1, source_target_pairs={{0,4},{1,5},{2,3},{3,2},{4,0},{5,1},{6,7},{7,6},{8,12},{9,13},{10,... | collective-permute-start | bytes 393224 | tf_op jit(solution)/shard_map/gather_w_hop1/ppermute | solution.py:561
  22.7 9.4 %collective-permute-start.9 = (bf16[4,16,4224]{2,1,0:T(8,128)(2,1)S(1)}, bf16[4,16,4224]{2,1,0:T(8,128)(2,1)S(1)}, u32[]{:S(2)}, u32[]{:S(2)}) collective-permute-start(bf16[4,16,4224]{2,1,0:T(8,128)(2,1)S(1)} %get-tuple-element.176.refs_0_), channel_id=1, source_target_pairs={{0,1},{1,0},{2,6},{3,7},{4,5},{5,4},{6,2},{7,3},{8,9},{9,8},{10,14... | collective-permute-start | bytes 1622024 | tf_op jit(solution)/shard_map/gather_a_hop2/ppermute | solution.py:561
  22.9 24.6 %collective-permute-start.7 = (bf16[4,16,2048]{2,1,0:T(8,128)(2,1)S(1)}, bf16[4,16,2048]{2,1,0:T(8,128)(2,1)S(1)}, u32[]{:S(2)}, u32[]{:S(2)}) collective-permute-start(bf16[4,16,2048]{2,1,0:T(8,128)(2,1)S(1)} %get-tuple-element.174.refs_0_), channel_id=1, source_target_pairs={{0,1},{1,0},{2,6},{3,7},{4,5},{5,4},{6,2},{7,3},{8,9},{9,8},{10,14... | collective-permute-start | bytes 786440 | tf_op jit(solution)/shard_map/gather_u_hop2/ppermute | solution.py:561
  24.9 9.0 %collective-permute-start.8 = (bf16[4,4,16,512]{3,2,1,0:T(8,128)(2,1)S(1)}, bf16[4,4,16,512]{3,2,1,0:T(8,128)(2,1)S(1)}, u32[]{:S(2)}, u32[]{:S(2)}) collective-permute-start(bf16[4,4,16,512]{3,2,1,0:T(8,128)(2,1)S(1)} %get-tuple-element.175.refs_0_), channel_id=1, source_target_pairs={{0,8},{1,9},{2,18},{3,19},{4,12},{5,13},{6,22},{7,23},{8,0},{9,1},... | collective-permute-start | bytes 786440 | tf_op jit(solution)/shard_map/gather_w_hop2/ppermute | solution.py:561
  32.2 17.5 %collective-permute-start.12 = (bf16[8,16,4224]{2,1,0:T(8,128)(2,1)S(1)}, bf16[8,16,4224]{2,1,0:T(8,128)(2,1)S(1)}, u32[]{:S(2)}, u32[]{:S(2)}) collective-permute-start(bf16[8,16,4224]{2,1,0:T(8,128)(2,1)S(1)} %get-tuple-element.181.refs_2_), channel_id=1, source_target_pairs={{0,2},{1,3},{2,0},{3,1},{4,6},{5,7},{6,4},{7,5},{8,10},{9,11},{10,... | collective-permute-start | bytes 3244040 | tf_op jit(solution)/shard_map/gather_a_core0/ppermute | solution.py:561
  32.3 15.2 %collective-permute-start.11 = (bf16[8,16,4224]{2,1,0:T(8,128)(2,1)S(1)}, bf16[8,16,4224]{2,1,0:T(8,128)(2,1)S(1)}, u32[]{:S(2)}, u32[]{:S(2)}) collective-permute-start(bf16[8,16,4224]{2,1,0:T(8,128)(2,1)S(1)} %get-tuple-element.181.refs_2_), channel_id=1, source_target_pairs={{0,4},{1,5},{2,3},{3,2},{4,0},{5,1},{6,7},{7,6},{8,12},{9,13},{10,... | collective-permute-start | bytes 3244040 | tf_op jit(solution)/shard_map/gather_a_hop3/ppermute | solution.py:561
  34.0 19.8 %collective-permute-start.14 = (bf16[8,4,16,512]{3,2,1,0:T(8,128)(2,1)S(1)}, bf16[8,4,16,512]{3,2,1,0:T(8,128)(2,1)S(1)}, u32[]{:S(2)}, u32[]{:S(2)}) collective-permute-start(bf16[8,4,16,512]{3,2,1,0:T(8,128)(2,1)S(1)} %get-tuple-element.188.refs_6_), channel_id=1, source_target_pairs={{0,16},{1,17},{2,10},{3,11},{4,20},{5,21},{6,14},{7,15},{8,24},{9,... | collective-permute-start | bytes 1572872 | tf_op jit(solution)/shard_map/gather_w_hop3/ppermute | solution.py:561
  47.6 11.9 %collective-permute-start.15 = (bf16[8,16,2048]{2,1,0:T(8,128)(2,1)S(1)}, bf16[8,16,2048]{2,1,0:T(8,128)(2,1)S(1)}, u32[]{:S(2)}, u32[]{:S(2)}) collective-permute-start(bf16[8,16,2048]{2,1,0:T(8,128)(2,1)S(1)} %get-tuple-element.180.refs_2_), channel_id=1, source_target_pairs={{0,2},{1,3},{2,0},{3,1},{4,6},{5,7},{6,4},{7,5},{8,10},{9,11},{10,... | collective-permute-start | bytes 1572872 | tf_op jit(solution)/shard_map/gather_u_core0/ppermute | solution.py:561
  48.1 10.8 %collective-permute-start.10 = (bf16[8,16,2048]{2,1,0:T(8,128)(2,1)S(1)}, bf16[8,16,2048]{2,1,0:T(8,128)(2,1)S(1)}, u32[]{:S(2)}, u32[]{:S(2)}) collective-permute-start(bf16[8,16,2048]{2,1,0:T(8,128)(2,1)S(1)} %get-tuple-element.180.refs_2_), channel_id=1, source_target_pairs={{0,4},{1,5},{2,3},{3,2},{4,0},{5,1},{6,7},{7,6},{8,12},{9,13},{10,... | collective-permute-start | bytes 1572872 | tf_op jit(solution)/shard_map/gather_u_hop3/ppermute | solution.py:561
  49.7 9.7 %collective-permute-start.17 = (bf16[8,4,16,512]{3,2,1,0:T(8,128)(2,1)S(1)}, bf16[8,4,16,512]{3,2,1,0:T(8,128)(2,1)S(1)}, u32[]{:S(2)}, u32[]{:S(2)}) collective-permute-start(bf16[8,4,16,512]{3,2,1,0:T(8,128)(2,1)S(1)} %get-tuple-element.188.refs_6_), channel_id=1, source_target_pairs={{0,2},{1,3},{2,0},{3,1},{4,6},{5,7},{6,4},{7,5},{8,10},{9,11},{10,... | collective-permute-start | bytes 1572872 | tf_op jit(solution)/shard_map/gather_w_core0/ppermute | solution.py:561
  69.4 15.0 %collective-permute-start.21 = (bf16[8,4,16,512]{3,2,1,0:T(8,128)(2,1)S(1)}, bf16[8,4,16,512]{3,2,1,0:T(8,128)(2,1)S(1)}, u32[]{:S(2)}, u32[]{:S(2)}) collective-permute-start(bf16[8,4,16,512]{3,2,1,0:T(8,128)(2,1)S(1)} %get-tuple-element.208), channel_id=1, source_target_pairs={{0,4},{1,5},{2,3},{3,2},{4,0},{5,1},{6,7},{7,6},{8,12},{9,13},{10,... | collective-permute-start | bytes 1572872 | tf_op jit(solution)/shard_map/scatter_d_hop3/ppermute | solution.py:561
  78.2 9.5 %collective-permute-start.25 = (bf16[16,16,2560]{2,1,0:T(8,128)(2,1)S(1)}, bf16[16,16,2560]{2,1,0:T(8,128)(2,1)S(1)}, u32[]{:S(2)}, u32[]{:S(2)}) collective-permute-start(bf16[16,16,2560]{2,1,0:T(8,128)(2,1)S(1)} %get-tuple-element.241), channel_id=1, source_target_pairs={{0,2},{1,3},{2,0},{3,1},{4,6},{5,7},{6,4},{7,5},{8,10},{9,11},{10,... | collective-permute-start | bytes 3932168 | tf_op jit(solution)/shard_map/scatter_c_core/ppermute | solution.py:561
  78.4 9.2 %collective-permute-start.26 = (bf16[8,4,16,512]{3,2,1,0:T(8,128)(2,1)S(1)}, bf16[8,4,16,512]{3,2,1,0:T(8,128)(2,1)S(1)}, u32[]{:S(2)}, u32[]{:S(2)}) collective-permute-start(bf16[8,4,16,512]{3,2,1,0:T(8,128)(2,1)S(1)} %get-tuple-element.243), channel_id=1, source_target_pairs={{0,4},{1,5},{2,3},{3,2},{4,0},{5,1},{6,7},{7,6},{8,12},{9,13},{10,... | collective-permute-start | bytes 1572872 | tf_op jit(solution)/shard_map/scatter_u_hop3/ppermute | solution.py:561
  88.1 16.2 %collective-permute-start.29 = (bf16[8,16,2560]{2,1,0:T(8,128)(2,1)S(1)}, bf16[8,16,2560]{2,1,0:T(8,128)(2,1)S(1)}, u32[]{:S(2)}, u32[]{:S(2)}) collective-permute-start(bf16[8,16,2560]{2,1,0:T(8,128)(2,1)S(1)} %get-tuple-element.255), channel_id=1, source_target_pairs={{0,4},{1,5},{2,3},{3,2},{4,0},{5,1},{6,7},{7,6},{8,12},{9,13},{10,... | collective-permute-start | bytes 1966088 | tf_op jit(solution)/shard_map/scatter_c_hop3/ppermute | solution.py:561
  90.0 13.4 %collective-permute-start.30 = (bf16[8,16,1664]{2,1,0:T(8,128)(2,1)S(1)}, bf16[8,16,1664]{2,1,0:T(8,128)(2,1)S(1)}, u32[]{:S(2)}, u32[]{:S(2)}) collective-permute-start(bf16[8,16,1664]{2,1,0:T(8,128)(2,1)S(1)} %get-tuple-element.257), channel_id=1, source_target_pairs={{0,4},{1,5},{2,3},{3,2},{4,0},{5,1},{6,7},{7,6},{8,12},{9,13},{10,... | collective-permute-start | bytes 1277960 | tf_op jit(solution)/shard_map/scatter_s_hop3/ppermute | solution.py:561
  90.5 9.1 %collective-permute-start.23 = (bf16[4,4,16,512]{3,2,1,0:T(8,128)(2,1)S(1)}, bf16[4,4,16,512]{3,2,1,0:T(8,128)(2,1)S(1)}, u32[]{:S(2)}, u32[]{:S(2)}) collective-permute-start(bf16[4,4,16,512]{3,2,1,0:T(8,128)(2,1)S(1)} %get-tuple-element.237), channel_id=1, source_target_pairs={{0,16},{1,17},{2,10},{3,11},{4,20},{5,21},{6,14},{7,15},{8,24},{9,... | collective-permute-start | bytes 786440 | tf_op jit(solution)/shard_map/scatter_d_hop2/ppermute | solution.py:561
  93.1 6.6 %collective-permute-start.19 = (bf16[128,512]{1,0:T(8,128)(2,1)S(1)}, bf16[128,512]{1,0:T(8,128)(2,1)S(1)}, u32[]{:S(2)}, u32[]{:S(2)}) collective-permute-start(bf16[128,512]{1,0:T(8,128)(2,1)S(1)} %get-tuple-element.199), channel_id=1, source_target_pairs={{0,1},{1,0},{2,3},{3,2},{4,5},{5,4},{6,7},{7,6},{8,9},{9,8},{10,11... | collective-permute-start | bytes 393224 | tf_op jit(solution)/shard_map/swap_out/ppermute | solution.py:665
  93.8 14.9 %collective-permute-start.28 = (bf16[4,4,16,512]{3,2,1,0:T(8,128)(2,1)S(1)}, bf16[4,4,16,512]{3,2,1,0:T(8,128)(2,1)S(1)}, u32[]{:S(2)}, u32[]{:S(2)}) collective-permute-start(bf16[4,4,16,512]{3,2,1,0:T(8,128)(2,1)S(1)} %get-tuple-element.253), channel_id=1, source_target_pairs={{0,16},{1,17},{2,10},{3,11},{4,20},{5,21},{6,14},{7,15},{8,24},{9,... | collective-permute-start | bytes 786440 | tf_op jit(solution)/shard_map/scatter_u_hop2/ppermute | solution.py:561
  104.4 10.7 %collective-permute-start.32 = (bf16[4,16,2560]{2,1,0:T(8,128)(2,1)S(1)}, bf16[4,16,2560]{2,1,0:T(8,128)(2,1)S(1)}, u32[]{:S(2)}, u32[]{:S(2)}) collective-permute-start(bf16[4,16,2560]{2,1,0:T(8,128)(2,1)S(1)} %get-tuple-element.264), channel_id=1, source_target_pairs={{0,1},{1,0},{2,6},{3,7},{4,5},{5,4},{6,2},{7,3},{8,9},{9,8},{10,14... | collective-permute-start | bytes 983048 | tf_op jit(solution)/shard_map/scatter_c_hop2/ppermute | solution.py:561
  105.8 9.3 %collective-permute-start.33 = (bf16[2,4,16,512]{3,2,1,0:T(8,128)(2,1)S(1)}, bf16[2,4,16,512]{3,2,1,0:T(8,128)(2,1)S(1)}, u32[]{:S(2)}, u32[]{:S(2)}) collective-permute-start(bf16[2,4,16,512]{3,2,1,0:T(8,128)(2,1)S(1)} %get-tuple-element.266), channel_id=1, source_target_pairs={{0,8},{1,9},{2,18},{3,19},{4,12},{5,13},{6,22},{7,23},{8,0},{9,1},... | collective-permute-start | bytes 393224 | tf_op jit(solution)/shard_map/scatter_d_hop1/ppermute | solution.py:561
  108.0 17.1 %collective-permute-start.37 = (bf16[256,512]{1,0:T(8,128)(2,1)S(1)}, bf16[256,512]{1,0:T(8,128)(2,1)S(1)}, u32[]{:S(2)}, u32[]{:S(2)}) collective-permute-start(bf16[256,512]{1,0:T(8,128)(2,1)S(1)} %get-tuple-element.278), channel_id=1, source_target_pairs={{0,1},{1,0},{2,3},{3,2},{4,5},{5,4},{6,7},{7,6},{8,9},{9,8},{10,11... | collective-permute-start | bytes 786440 | tf_op jit(solution)/shard_map/swap_memory/ppermute | solution.py:665
  109.4 11.7 %collective-permute-start.39 = (bf16[2,16,1664]{2,1,0:T(8,128)(2,1)S(1)}, bf16[2,16,1664]{2,1,0:T(8,128)(2,1)S(1)}, u32[]{:S(2)}, u32[]{:S(2)}) collective-permute-start(bf16[2,16,1664]{2,1,0:T(8,128)(2,1)S(1)} %get-tuple-element.282), channel_id=1, source_target_pairs={{0,16},{1,17},{2,10},{3,11},{4,20},{5,21},{6,14},{7,15},{8,24},{9,... | collective-permute-start | bytes 319496 | tf_op jit(solution)/shard_map/scatter_s_hop1/ppermute | solution.py:561
  112.3 7.9 %collective-permute-start.31 = (bf16[2,4,16,512]{3,2,1,0:T(8,128)(2,1)S(1)}, bf16[2,4,16,512]{3,2,1,0:T(8,128)(2,1)S(1)}, u32[]{:S(2)}, u32[]{:S(2)}) collective-permute-start(bf16[2,4,16,512]{3,2,1,0:T(8,128)(2,1)S(1)} %get-tuple-element.262), channel_id=1, source_target_pairs={{0,8},{1,9},{2,18},{3,19},{4,12},{5,13},{6,22},{7,23},{8,0},{9,1},... | collective-permute-start | bytes 393224 | tf_op jit(solution)/shard_map/scatter_u_hop1/ppermute | solution.py:561
  115.3 7.2 %collective-permute-start.38 = (bf16[2,16,2560]{2,1,0:T(8,128)(2,1)S(1)}, bf16[2,16,2560]{2,1,0:T(8,128)(2,1)S(1)}, u32[]{:S(2)}, u32[]{:S(2)}) collective-permute-start(bf16[2,16,2560]{2,1,0:T(8,128)(2,1)S(1)} %get-tuple-element.280), channel_id=1, source_target_pairs={{0,16},{1,17},{2,10},{3,11},{4,20},{5,21},{6,14},{7,15},{8,24},{9,... | collective-permute-start | bytes 491528 | tf_op jit(solution)/shard_map/scatter_c_hop1/ppermute | solution.py:561
  117.8 9.7 %collective-permute-start.27 = (bf16[128,512]{1,0:T(8,128)(2,1)S(1)}, bf16[128,512]{1,0:T(8,128)(2,1)S(1)}, u32[]{:S(2)}, u32[]{:S(2)}) collective-permute-start(bf16[128,512]{1,0:T(8,128)(2,1)S(1)} %get-tuple-element.251), channel_id=1, source_target_pairs={{0,1},{1,0},{2,3},{3,2},{4,5},{5,4},{6,7},{7,6},{8,9},{9,8},{10,11... | collective-permute-start | bytes 393224 | tf_op jit(solution)/shard_map/swap_hidden/ppermute | solution.py:665
  120.2 6.5 %collective-permute-start.36 = (bf16[1,4,16,512]{3,2,1,0:T(8,128)(2,1)S(1)}, bf16[1,4,16,512]{3,2,1,0:T(8,128)(2,1)S(1)}, u32[]{:S(2)}, u32[]{:S(2)}) collective-permute-start(bf16[1,4,16,512]{3,2,1,0:T(8,128)(2,1)S(1)} %get-tuple-element.276), channel_id=1, source_target_pairs={{0,1},{1,0},{2,6},{3,7},{4,5},{5,4},{6,2},{7,3},{8,9},{9,8},{10,14... | collective-permute-start | bytes 196616 | tf_op jit(solution)/shard_map/scatter_d_hop0/ppermute | solution.py:561
  122.5 7.2 %collective-permute-start.40 = (bf16[1,16,2560]{2,1,0:T(8,128)(2,1)S(1)}, bf16[1,16,2560]{2,1,0:T(8,128)(2,1)S(1)}, u32[]{:S(2)}, u32[]{:S(2)}) collective-permute-start(bf16[1,16,2560]{2,1,0:T(8,128)(2,1)S(1)} %get-tuple-element.291), channel_id=1, source_target_pairs={{0,8},{1,9},{2,18},{3,19},{4,12},{5,13},{6,22},{7,23},{8,0},{9,1},... | collective-permute-start | bytes 245768 | tf_op jit(solution)/shard_map/scatter_c_hop0/ppermute | solution.py:561
  (10 other events, 43.2 us)

commit v4 on v3

--- a/solution.py
+++ b/solution.py
@@ -713,7 +713,7 @@
         [pltpu.VMEM((BLOCKS, 16, 128), BF)], 2,
     )
     if permuted:
-        w_pieces = chunks["w"].finish(True)
+        w_pieces = chunks["w"].finish()
     weights2, mem, cq, ck, cv, mixed2, probs2, x2, normed3 = line.call(
         functools.partial(cross_forward_kernel, base(GATHER_KIND["a"])), "cross_forward",
         [order, info, *a_pieces, kept, new, mask, vecs, x1, normed2],

time: 131 us -> 130 us (level)
    pallas_call x38 -> x37, Pallas kernels: 34.6 us -> 34.6 us  [call(): pl.pallas_call(body, name=name, out_shape=[shape(*o) for o in made] + [sh...]
where the time goes in v4:
time: 130 us
  starting transfers between devices  50.1 us (39%)
  waiting for transfers between devices  42.1 us (32%)
  Pallas kernels  36.7 us (28%)
    ppermute x38, starting transfers between devices, permute(): return lax.ppermute(value, BOTH, pairs)  48.5 us
    ppermute x38, waiting for transfers between devices, permute(): return lax.ppermute(value, BOTH, pairs)  38.1 us
    pallas_call x37, Pallas kernels, call(): pl.pallas_call(body, name=name, out_shape=[shape(*o) for o in made] + [sh...  34.6 us
    ppermute x4, waiting for transfers between devices, swap(): return lax.ppermute(value, 'seq', [(0, 1), (1, 0)])  3.93 us
  transfers between devices with their start and end apart: 42, of which 14 were waited for; matrix products, arithmetic and copies ran while one was open for 0% of the time, Pallas kernels for 22%

profile of v4, /device:TPU:0, one launch (start us, length us, event | category | flops | bytes accessed | tf_op | source)
XLA Modules:
  0.0 129.8 jit_solution(4618590167465250938)
XLA Ops:
  0.7 2.2 %pack.1 = (s32[96]{0:T(128)S(1)}, s32[2]{0:T(128)S(1)}, bf16[1,16,4224]{2,1,0:T(8,128)(2,1)S(1)}, bf16[16,2048]{1,0:T(8,128)(2,1)S(1)}, bf16[64,512]{1,0:T(8,128...) custom-call(s32[1]{0:T(128)} %bitcast.me.refs_0_, ...), custom_call_target="tpu_custom_call" | custom-call | tf_op jit(solution)/shard_map/pack/pallas_call | solution.py:631
  2.9 3.1 %collective-permute-start.2 = (bf16[1,16,4224]{2,1,0:T(8,128)(2,1)S(1)}, bf16[1,16,4224]{2,1,0:T(8,128)(2,1)S(1)}, u32[]{:S(2)}, u32[]{:S(2)}) collective-permute-start(bf16[1,16,4224]{2,1,0:T(8,128)(2,1)S(1)} %get-tuple-element.161.refs_0_), channel_id=1, source_target_pairs={{0,8},{1,9},{2,18},{3,19},{4,12},{5,13},{6,22},{7,23},{8,0},{9,1},... | collective-permute-start | bytes 405512 | tf_op jit(solution)/shard_map/gather_a_hop0/ppermute | solution.py:561
  8.0 2.0 %collective-permute-done.2.refs_1_ = bf16[1,16,4224]{2,1,0:T(8,128)(2,1)S(1)} collective-permute-done((bf16[1,16,4224]{2,1,0:T(8,128)(2,1)S(1)}, bf16[1,16,4224]{2,1,0:T(8,128)(2,1)S(1)}, u32[]{:S(2)}, u32[]{:S(2)}) %collective-permute-start.2) | collective-permute-done | bytes 135200 | tf_op jit(solution)/shard_map/gather_a_hop0/ppermute | solution.py:561
  10.1 2.4 %collective-permute-start.5 = (bf16[2,16,4224]{2,1,0:T(8,128)(2,1)S(1)}, bf16[2,16,4224]{2,1,0:T(8,128)(2,1)S(1)}, u32[]{:S(2)}, u32[]{:S(2)}) collective-permute-start(bf16[2,16,4224]{2,1,0:T(8,128)(2,1)S(1)} %get-tuple-element.167.refs_0_), channel_id=1, source_target_pairs={{0,16},{1,17},{2,10},{3,11},{4,20},{5,21},{6,14},{7,15},{8,24},{9,... | collective-permute-start | bytes 811016 | tf_op jit(solution)/shard_map/gather_a_hop1/ppermute | solution.py:561
  12.5 1.9 %collective-permute-start.3 = (bf16[2,16,2048]{2,1,0:T(8,128)(2,1)S(1)}, bf16[2,16,2048]{2,1,0:T(8,128)(2,1)S(1)}, u32[]{:S(2)}, u32[]{:S(2)}) collective-permute-start(bf16[2,16,2048]{2,1,0:T(8,128)(2,1)S(1)} %get-tuple-element.165.refs_0_), channel_id=1, source_target_pairs={{0,16},{1,17},{2,10},{3,11},{4,20},{5,21},{6,14},{7,15},{8,24},{9,... | collective-permute-start | bytes 393224 | tf_op jit(solution)/shard_map/gather_u_hop1/ppermute | solution.py:561
  15.9 2.9 %collective-permute-done.5.refs_1_ = bf16[2,16,4224]{2,1,0:T(8,128)(2,1)S(1)} collective-permute-done((bf16[2,16,4224]{2,1,0:T(8,128)(2,1)S(1)}, bf16[2,16,4224]{2,1,0:T(8,128)(2,1)S(1)}, u32[]{:S(2)}, u32[]{:S(2)}) %collective-permute-start.5) | collective-permute-done | bytes 270368 | tf_op jit(solution)/shard_map/gather_a_hop1/ppermute | solution.py:561
  18.8 3.9 %collective-permute-done.6.refs_2_.refs_7_.refs_13_ = bf16[512,512]{1,0:T(8,128)(2,1)S(1)} collective-permute-done((bf16[512,512]{1,0:T(8,128)(2,1)S(1)}, bf16[512,512]{1,0:T(8,128)(2,1)S(1)}, u32[]{:S(2)}, u32[]{:S(2)}) %collective-permute-start.6) | collective-permute-done | bytes 524320 | tf_op jit(solution)/shard_map/swap_in/ppermute | solution.py:665
  22.9 2.0 %collective-permute-start.7 = (bf16[4,16,2048]{2,1,0:T(8,128)(2,1)S(1)}, bf16[4,16,2048]{2,1,0:T(8,128)(2,1)S(1)}, u32[]{:S(2)}, u32[]{:S(2)}) collective-permute-start(bf16[4,16,2048]{2,1,0:T(8,128)(2,1)S(1)} %get-tuple-element.172.refs_0_), channel_id=1, source_target_pairs={{0,1},{1,0},{2,6},{3,7},{4,5},{5,4},{6,2},{7,3},{8,9},{9,8},{10,14... | collective-permute-start | bytes 786440 | tf_op jit(solution)/shard_map/gather_u_hop2/ppermute | solution.py:561
  26.5 5.6 %collective-permute-done.9.refs_1_ = bf16[4,16,4224]{2,1,0:T(8,128)(2,1)S(1)} collective-permute-done((bf16[4,16,4224]{2,1,0:T(8,128)(2,1)S(1)}, bf16[4,16,4224]{2,1,0:T(8,128)(2,1)S(1)}, u32[]{:S(2)}, u32[]{:S(2)}) %collective-permute-start.9) | collective-permute-done | bytes 540704 | tf_op jit(solution)/shard_map/gather_a_hop2/ppermute | solution.py:561
  32.3 1.7 %collective-permute-start.11 = (bf16[8,16,4224]{2,1,0:T(8,128)(2,1)S(1)}, bf16[8,16,4224]{2,1,0:T(8,128)(2,1)S(1)}, u32[]{:S(2)}, u32[]{:S(2)}) collective-permute-start(bf16[8,16,4224]{2,1,0:T(8,128)(2,1)S(1)} %get-tuple-element.179.refs_2_), channel_id=1, source_target_pairs={{0,4},{1,5},{2,3},{3,2},{4,0},{5,1},{6,7},{7,6},{8,12},{9,13},{10,... | collective-permute-start | bytes 3244040 | tf_op jit(solution)/shard_map/gather_a_hop3/ppermute | solution.py:561
  34.0 2.6 %collective-permute-start.16 = (bf16[8,4,16,512]{3,2,1,0:T(8,128)(2,1)S(1)}, bf16[8,4,16,512]{3,2,1,0:T(8,128)(2,1)S(1)}, u32[]{:S(2)}, u32[]{:S(2)}) collective-permute-start(bf16[8,4,16,512]{3,2,1,0:T(8,128)(2,1)S(1)} %get-tuple-element.189.refs_6_), channel_id=1, source_target_pairs={{0,16},{1,17},{2,10},{3,11},{4,20},{5,21},{6,14},{7,15},{8,24},{9,... | collective-permute-start | bytes 1572872 | tf_op jit(solution)/shard_map/gather_w_hop3/ppermute | solution.py:561
  36.6 10.9 %collective-permute-done.11.refs_3_ = bf16[8,16,4224]{2,1,0:T(8,128)(2,1)S(1)} collective-permute-done((bf16[8,16,4224]{2,1,0:T(8,128)(2,1)S(1)}, bf16[8,16,4224]{2,1,0:T(8,128)(2,1)S(1)}, u32[]{:S(2)}, u32[]{:S(2)}) %collective-permute-start.11) | collective-permute-done | bytes 1081376 | tf_op jit(solution)/shard_map/gather_a_hop3/ppermute | solution.py:561
  47.6 1.7 %collective-permute-start.10 = (bf16[8,16,2048]{2,1,0:T(8,128)(2,1)S(1)}, bf16[8,16,2048]{2,1,0:T(8,128)(2,1)S(1)}, u32[]{:S(2)}, u32[]{:S(2)}) collective-permute-start(bf16[8,16,2048]{2,1,0:T(8,128)(2,1)S(1)} %get-tuple-element.178.refs_2_), channel_id=1, source_target_pairs={{0,4},{1,5},{2,3},{3,2},{4,0},{5,1},{6,7},{7,6},{8,12},{9,13},{10,... | collective-permute-start | bytes 1572872 | tf_op jit(solution)/shard_map/gather_u_hop3/ppermute | solution.py:561
  50.3 3.5 %self_forward.1 = (bf16[512,2048]{1,0:T(8,128)(2,1)S(1)}, f32[16,512]{1,0:T(8,128)S(1)}, f32[8,512]{1,0:T(8,128)S(1)}, bf16[256,512]{1,0:T(8,128)(2,1)S(1)}, bf1...) custom-call(s32[96]{0:T(128)S(1)} %get-tuple-element.158.refs_0_, ...), custom_call_target="tpu_custom_call" | custom-call | flops 1 | bytes 1 | tf_op jit(solution)/shard_map/self_forward/pallas_call | solution.py:503
  53.8 4.9 %cross_forward.1 = (bf16[512,2048]{1,0:T(8,128)(2,1)S(1)}, bf16[512,512]{1,0:T(8,128)(2,1)S(1)}, bf16[256,512]{1,0:T(8,128)(2,1)S(1)}, bf16[512,512]{1,0:T(8,128...) custom-call(s32[96]{0:T(128)S(1)} %get-tuple-element.158.refs_0_, ...), custom_call_target="tpu_custom_call" | custom-call | flops 1 | bytes 1 | tf_op jit(solution)/shard_map/cross_forward/pallas_call | solution.py:503
  59.0 1.8 %collective-permute-done.15.refs_5_ = bf16[8,16,2048]{2,1,0:T(8,128)(2,1)S(1)} collective-permute-done((bf16[8,16,2048]{2,1,0:T(8,128)(2,1)S(1)}, bf16[8,16,2048]{2,1,0:T(8,128)(2,1)S(1)}, u32[]{:S(2)}, u32[]{:S(2)}) %collective-permute-start.15) | collective-permute-done | bytes 524320 | tf_op jit(solution)/shard_map/gather_u_core1/ppermute | solution.py:561
  60.8 4.7 %ffn.1 = (bf16[128,512]{1,0:T(8,128)(2,1)S(1)}, bf16[128,512]{1,0:T(8,128)(2,1)S(1)}, bf16[512,2048]{1,0:T(8,128)(2,1)S(1)}, bf16[256,2048]{1,0:T(8,128)(2,1)S(1...) custom-call(s32[96]{0:T(128)S(1)} %get-tuple-element.158.refs_0_, ...), custom_call_target="tpu_custom_call" | custom-call | flops 1 | bytes 1 | tf_op jit(solution)/shard_map/ffn/pallas_call | solution.py:503
  65.7 2.8 %ffn_back.1 = (f32[256,512]{1,0:T(8,128)S(1)}, f32[16,512]{1,0:T(8,128)S(1)}, f32[8,512]{1,0:T(8,128)S(1)}, bf16[16,4,16,512]{3,2,1,0:T(8,128)(2,1)S(1)}, bf16[1...) custom-call(s32[96]{0:T(128)S(1)} %get-tuple-element.158.refs_0_, s32[2]{0:T(128)S(1)} %get-tuple-element.157.refs_1_.refs_0_, ...), custom_call_target="tpu_custom_call" | custom-call | flops 1 | bytes 1 | tf_op jit(solution)/shard_map/ffn_back/pallas_call | solution.py:503
  69.2 1.6 %collective-permute-start.21 = (bf16[8,4,16,512]{3,2,1,0:T(8,128)(2,1)S(1)}, bf16[8,4,16,512]{3,2,1,0:T(8,128)(2,1)S(1)}, u32[]{:S(2)}, u32[]{:S(2)}) collective-permute-start(bf16[8,4,16,512]{3,2,1,0:T(8,128)(2,1)S(1)} %get-tuple-element.204), channel_id=1, source_target_pairs={{0,4},{1,5},{2,3},{3,2},{4,0},{5,1},{6,7},{7,6},{8,12},{9,13},{10,... | collective-permute-start | bytes 1572872 | tf_op jit(solution)/shard_map/scatter_d_hop3/ppermute | solution.py:561
  71.5 6.3 %cross_back.1 = (f32[256,512]{1,0:T(8,128)S(1)}, bf16[256,512]{1,0:T(8,128)(2,1)S(1)}, f32[256,512]{1,0:T(8,128)S(1)}, bf16[256,512]{1,0:T(8,128)(2,1)S(1)}, f32...) custom-call(s32[96]{0:T(128)S(1)} %get-tuple-element.158.refs_0_, ...), custom_call_target="tpu_custom_call" | custom-call | flops 1 | bytes 1 | tf_op jit(solution)/shard_map/cross_back/pallas_call | solution.py:503
  79.8 4.3 %self_back.1 = (f32[128,512]{1,0:T(8,128)S(1)}, bf16[128,512]{1,0:T(8,128)(2,1)S(1)}, bf16[16,16,1664]{2,1,0:T(8,128)(2,1)S(1)}, bf16[16,16,1664]{2,1,0:T(8,128)(2,1)S(1)}, f32[8,128]{1,0:T(8,128)S(1)}) custom-call(s32[96]{0:T(128)S(1)} %get-tuple-element.158.refs_0_, s32[2]{0:T(128)S(1)} %get-tuple-element.157.refs_1_.refs_0_, ...), custom_call_target="tpu_custom_call" | custom-call | flops 1 | bytes 1 | tf_op jit(solution)/shard_map/self_back/pallas_call | solution.py:503
  84.3 3.1 %collective-permute-done.26.refs_1_ = bf16[8,4,16,512]{3,2,1,0:T(8,128)(2,1)S(1)} collective-permute-done((bf16[8,4,16,512]{3,2,1,0:T(8,128)(2,1)S(1)}, bf16[8,4,16,512]{3,2,1,0:T(8,128)(2,1)S(1)}, u32[]{:S(2)}, u32[]{:S(2)}) %collective-permute-start.26) | collective-permute-done | bytes 524320 | tf_op jit(solution)/shard_map/scatter_u_hop3/ppermute | solution.py:561
  87.9 1.6 %collective-permute-start.29 = (bf16[8,16,2560]{2,1,0:T(8,128)(2,1)S(1)}, bf16[8,16,2560]{2,1,0:T(8,128)(2,1)S(1)}, u32[]{:S(2)}, u32[]{:S(2)}) collective-permute-start(bf16[8,16,2560]{2,1,0:T(8,128)(2,1)S(1)} %get-tuple-element.251), channel_id=1, source_target_pairs={{0,4},{1,5},{2,3},{3,2},{4,0},{5,1},{6,7},{7,6},{8,12},{9,13},{10,... | collective-permute-start | bytes 1966088 | tf_op jit(solution)/shard_map/scatter_c_hop3/ppermute | solution.py:561
  90.3 2.6 %collective-permute-start.23 = (bf16[4,4,16,512]{3,2,1,0:T(8,128)(2,1)S(1)}, bf16[4,4,16,512]{3,2,1,0:T(8,128)(2,1)S(1)}, u32[]{:S(2)}, u32[]{:S(2)}) collective-permute-start(bf16[4,4,16,512]{3,2,1,0:T(8,128)(2,1)S(1)} %get-tuple-element.233), channel_id=1, source_target_pairs={{0,16},{1,17},{2,10},{3,11},{4,20},{5,21},{6,14},{7,15},{8,24},{9,... | collective-permute-start | bytes 786440 | tf_op jit(solution)/shard_map/scatter_d_hop2/ppermute | solution.py:561
  94.1 5.3 %collective-permute-done.23.refs_1_ = bf16[4,4,16,512]{3,2,1,0:T(8,128)(2,1)S(1)} collective-permute-done((bf16[4,4,16,512]{3,2,1,0:T(8,128)(2,1)S(1)}, bf16[4,4,16,512]{3,2,1,0:T(8,128)(2,1)S(1)}, u32[]{:S(2)}, u32[]{:S(2)}) %collective-permute-start.23) | collective-permute-done | bytes 262176 | tf_op jit(solution)/shard_map/scatter_d_hop2/ppermute | solution.py:561
  100.8 2.4 %collective-permute-done.30.refs_1_ = bf16[8,16,1664]{2,1,0:T(8,128)(2,1)S(1)} collective-permute-done((bf16[8,16,1664]{2,1,0:T(8,128)(2,1)S(1)}, bf16[8,16,1664]{2,1,0:T(8,128)(2,1)S(1)}, u32[]{:S(2)}, u32[]{:S(2)}) %collective-permute-start.30) | collective-permute-done | bytes 426016 | tf_op jit(solution)/shard_map/scatter_s_hop3/ppermute | solution.py:561
  105.6 2.1 %collective-permute-start.33 = (bf16[2,4,16,512]{3,2,1,0:T(8,128)(2,1)S(1)}, bf16[2,4,16,512]{3,2,1,0:T(8,128)(2,1)S(1)}, u32[]{:S(2)}, u32[]{:S(2)}) collective-permute-start(bf16[2,4,16,512]{3,2,1,0:T(8,128)(2,1)S(1)} %get-tuple-element.262), channel_id=1, source_target_pairs={{0,8},{1,9},{2,18},{3,19},{4,12},{5,13},{6,22},{7,23},{8,0},{9,1},... | collective-permute-start | bytes 393224 | tf_op jit(solution)/shard_map/scatter_d_hop1/ppermute | solution.py:561
  109.2 2.8 %collective-permute-start.39 = (bf16[2,16,1664]{2,1,0:T(8,128)(2,1)S(1)}, bf16[2,16,1664]{2,1,0:T(8,128)(2,1)S(1)}, u32[]{:S(2)}, u32[]{:S(2)}) collective-permute-start(bf16[2,16,1664]{2,1,0:T(8,128)(2,1)S(1)} %get-tuple-element.278), channel_id=1, source_target_pairs={{0,16},{1,17},{2,10},{3,11},{4,20},{5,21},{6,14},{7,15},{8,24},{9,... | collective-permute-start | bytes 319496 | tf_op jit(solution)/shard_map/scatter_s_hop1/ppermute | solution.py:561
  112.0 3.1 %collective-permute-start.31 = (bf16[2,4,16,512]{3,2,1,0:T(8,128)(2,1)S(1)}, bf16[2,4,16,512]{3,2,1,0:T(8,128)(2,1)S(1)}, u32[]{:S(2)}, u32[]{:S(2)}) collective-permute-start(bf16[2,4,16,512]{3,2,1,0:T(8,128)(2,1)S(1)} %get-tuple-element.258), channel_id=1, source_target_pairs={{0,8},{1,9},{2,18},{3,19},{4,12},{5,13},{6,22},{7,23},{8,0},{9,1},... | collective-permute-start | bytes 393224 | tf_op jit(solution)/shard_map/scatter_u_hop1/ppermute | solution.py:561
  115.2 2.5 %collective-permute-start.38 = (bf16[2,16,2560]{2,1,0:T(8,128)(2,1)S(1)}, bf16[2,16,2560]{2,1,0:T(8,128)(2,1)S(1)}, u32[]{:S(2)}, u32[]{:S(2)}) collective-permute-start(bf16[2,16,2560]{2,1,0:T(8,128)(2,1)S(1)} %get-tuple-element.276), channel_id=1, source_target_pairs={{0,16},{1,17},{2,10},{3,11},{4,20},{5,21},{6,14},{7,15},{8,24},{9,... | collective-permute-start | bytes 491528 | tf_op jit(solution)/shard_map/scatter_c_hop1/ppermute | solution.py:561
  117.9 1.8 %collective-permute-done.31.refs_1_ = bf16[2,4,16,512]{3,2,1,0:T(8,128)(2,1)S(1)} collective-permute-done((bf16[2,4,16,512]{3,2,1,0:T(8,128)(2,1)S(1)}, bf16[2,4,16,512]{3,2,1,0:T(8,128)(2,1)S(1)}, u32[]{:S(2)}, u32[]{:S(2)}) %collective-permute-start.31) | collective-permute-done | bytes 131104 | tf_op jit(solution)/shard_map/scatter_u_hop1/ppermute | solution.py:561
  121.9 2.7 %collective-permute-start.40 = (bf16[1,16,2560]{2,1,0:T(8,128)(2,1)S(1)}, bf16[1,16,2560]{2,1,0:T(8,128)(2,1)S(1)}, u32[]{:S(2)}, u32[]{:S(2)}) collective-permute-start(bf16[1,16,2560]{2,1,0:T(8,128)(2,1)S(1)} %get-tuple-element.287), channel_id=1, source_target_pairs={{0,8},{1,9},{2,18},{3,19},{4,12},{5,13},{6,22},{7,23},{8,0},{9,1},... | collective-permute-start | bytes 245768 | tf_op jit(solution)/shard_map/scatter_c_hop0/ppermute | solution.py:561
  (90 shorter events, 26.1 us)
Async XLA Ops:
  2.9 7.2 %collective-permute-start.2 = (bf16[1,16,4224]{2,1,0:T(8,128)(2,1)S(1)}, bf16[1,16,4224]{2,1,0:T(8,128)(2,1)S(1)}, u32[]{:S(2)}, u32[]{:S(2)}) collective-permute-start(bf16[1,16,4224]{2,1,0:T(8,128)(2,1)S(1)} %get-tuple-element.161.refs_0_), channel_id=1, source_target_pairs={{0,8},{1,9},{2,18},{3,19},{4,12},{5,13},{6,22},{7,23},{8,0},{9,1},... | collective-permute-start | bytes 405512 | tf_op jit(solution)/shard_map/gather_a_hop0/ppermute | solution.py:561
  7.9 14.8 %collective-permute-start.6 = (bf16[512,512]{1,0:T(8,128)(2,1)S(1)}, bf16[512,512]{1,0:T(8,128)(2,1)S(1)}, u32[]{:S(2)}, u32[]{:S(2)}) collective-permute-start(bf16[512,512]{1,0:T(8,128)(2,1)S(1)} %get-tuple-element.168), channel_id=1, source_target_pairs={{0,1},{1,0},{2,3},{3,2},{4,5},{5,4},{6,7},{7,6},{8,9},{9,8},{10,11... | collective-permute-start | bytes 1572872 | tf_op jit(solution)/shard_map/swap_in/ppermute | solution.py:665
  10.1 8.7 %collective-permute-start.5 = (bf16[2,16,4224]{2,1,0:T(8,128)(2,1)S(1)}, bf16[2,16,4224]{2,1,0:T(8,128)(2,1)S(1)}, u32[]{:S(2)}, u32[]{:S(2)}) collective-permute-start(bf16[2,16,4224]{2,1,0:T(8,128)(2,1)S(1)} %get-tuple-element.167.refs_0_), channel_id=1, source_target_pairs={{0,16},{1,17},{2,10},{3,11},{4,20},{5,21},{6,14},{7,15},{8,24},{9,... | collective-permute-start | bytes 811016 | tf_op jit(solution)/shard_map/gather_a_hop1/ppermute | solution.py:561
  12.5 10.4 %collective-permute-start.3 = (bf16[2,16,2048]{2,1,0:T(8,128)(2,1)S(1)}, bf16[2,16,2048]{2,1,0:T(8,128)(2,1)S(1)}, u32[]{:S(2)}, u32[]{:S(2)}) collective-permute-start(bf16[2,16,2048]{2,1,0:T(8,128)(2,1)S(1)} %get-tuple-element.165.refs_0_), channel_id=1, source_target_pairs={{0,16},{1,17},{2,10},{3,11},{4,20},{5,21},{6,14},{7,15},{8,24},{9,... | collective-permute-start | bytes 393224 | tf_op jit(solution)/shard_map/gather_u_hop1/ppermute | solution.py:561
  14.4 8.5 %collective-permute-start.4 = (bf16[2,4,16,512]{3,2,1,0:T(8,128)(2,1)S(1)}, bf16[2,4,16,512]{3,2,1,0:T(8,128)(2,1)S(1)}, u32[]{:S(2)}, u32[]{:S(2)}) collective-permute-start(bf16[2,4,16,512]{3,2,1,0:T(8,128)(2,1)S(1)} %get-tuple-element.166.refs_0_), channel_id=1, source_target_pairs={{0,4},{1,5},{2,3},{3,2},{4,0},{5,1},{6,7},{7,6},{8,12},{9,13},{10,... | collective-permute-start | bytes 393224 | tf_op jit(solution)/shard_map/gather_w_hop1/ppermute | solution.py:561
  22.7 9.4 %collective-permute-start.9 = (bf16[4,16,4224]{2,1,0:T(8,128)(2,1)S(1)}, bf16[4,16,4224]{2,1,0:T(8,128)(2,1)S(1)}, u32[]{:S(2)}, u32[]{:S(2)}) collective-permute-start(bf16[4,16,4224]{2,1,0:T(8,128)(2,1)S(1)} %get-tuple-element.174.refs_0_), channel_id=1, source_target_pairs={{0,1},{1,0},{2,6},{3,7},{4,5},{5,4},{6,2},{7,3},{8,9},{9,8},{10,14... | collective-permute-start | bytes 1622024 | tf_op jit(solution)/shard_map/gather_a_hop2/ppermute | solution.py:561
  22.9 24.6 %collective-permute-start.7 = (bf16[4,16,2048]{2,1,0:T(8,128)(2,1)S(1)}, bf16[4,16,2048]{2,1,0:T(8,128)(2,1)S(1)}, u32[]{:S(2)}, u32[]{:S(2)}) collective-permute-start(bf16[4,16,2048]{2,1,0:T(8,128)(2,1)S(1)} %get-tuple-element.172.refs_0_), channel_id=1, source_target_pairs={{0,1},{1,0},{2,6},{3,7},{4,5},{5,4},{6,2},{7,3},{8,9},{9,8},{10,14... | collective-permute-start | bytes 786440 | tf_op jit(solution)/shard_map/gather_u_hop2/ppermute | solution.py:561
  24.9 9.0 %collective-permute-start.8 = (bf16[4,4,16,512]{3,2,1,0:T(8,128)(2,1)S(1)}, bf16[4,4,16,512]{3,2,1,0:T(8,128)(2,1)S(1)}, u32[]{:S(2)}, u32[]{:S(2)}) collective-permute-start(bf16[4,4,16,512]{3,2,1,0:T(8,128)(2,1)S(1)} %get-tuple-element.173.refs_0_), channel_id=1, source_target_pairs={{0,8},{1,9},{2,18},{3,19},{4,12},{5,13},{6,22},{7,23},{8,0},{9,1},... | collective-permute-start | bytes 786440 | tf_op jit(solution)/shard_map/gather_w_hop2/ppermute | solution.py:561
  32.2 17.5 %collective-permute-start.12 = (bf16[8,16,4224]{2,1,0:T(8,128)(2,1)S(1)}, bf16[8,16,4224]{2,1,0:T(8,128)(2,1)S(1)}, u32[]{:S(2)}, u32[]{:S(2)}) collective-permute-start(bf16[8,16,4224]{2,1,0:T(8,128)(2,1)S(1)} %get-tuple-element.179.refs_2_), channel_id=1, source_target_pairs={{0,2},{1,3},{2,0},{3,1},{4,6},{5,7},{6,4},{7,5},{8,10},{9,11},{10,... | collective-permute-start | bytes 3244040 | tf_op jit(solution)/shard_map/gather_a_core0/ppermute | solution.py:561
  32.3 15.2 %collective-permute-start.11 = (bf16[8,16,4224]{2,1,0:T(8,128)(2,1)S(1)}, bf16[8,16,4224]{2,1,0:T(8,128)(2,1)S(1)}, u32[]{:S(2)}, u32[]{:S(2)}) collective-permute-start(bf16[8,16,4224]{2,1,0:T(8,128)(2,1)S(1)} %get-tuple-element.179.refs_2_), channel_id=1, source_target_pairs={{0,4},{1,5},{2,3},{3,2},{4,0},{5,1},{6,7},{7,6},{8,12},{9,13},{10,... | collective-permute-start | bytes 3244040 | tf_op jit(solution)/shard_map/gather_a_hop3/ppermute | solution.py:561
  34.0 15.8 %collective-permute-start.16 = (bf16[8,4,16,512]{3,2,1,0:T(8,128)(2,1)S(1)}, bf16[8,4,16,512]{3,2,1,0:T(8,128)(2,1)S(1)}, u32[]{:S(2)}, u32[]{:S(2)}) collective-permute-start(bf16[8,4,16,512]{3,2,1,0:T(8,128)(2,1)S(1)} %get-tuple-element.189.refs_6_), channel_id=1, source_target_pairs={{0,16},{1,17},{2,10},{3,11},{4,20},{5,21},{6,14},{7,15},{8,24},{9,... | collective-permute-start | bytes 1572872 | tf_op jit(solution)/shard_map/gather_w_hop3/ppermute | solution.py:561
  47.6 11.2 %collective-permute-start.10 = (bf16[8,16,2048]{2,1,0:T(8,128)(2,1)S(1)}, bf16[8,16,2048]{2,1,0:T(8,128)(2,1)S(1)}, u32[]{:S(2)}, u32[]{:S(2)}) collective-permute-start(bf16[8,16,2048]{2,1,0:T(8,128)(2,1)S(1)} %get-tuple-element.178.refs_2_), channel_id=1, source_target_pairs={{0,4},{1,5},{2,3},{3,2},{4,0},{5,1},{6,7},{7,6},{8,12},{9,13},{10,... | collective-permute-start | bytes 1572872 | tf_op jit(solution)/shard_map/gather_u_hop3/ppermute | solution.py:561
  49.2 9.7 %collective-permute-start.14 = (bf16[8,16,2048]{2,1,0:T(8,128)(2,1)S(1)}, bf16[8,16,2048]{2,1,0:T(8,128)(2,1)S(1)}, u32[]{:S(2)}, u32[]{:S(2)}) collective-permute-start(bf16[8,16,2048]{2,1,0:T(8,128)(2,1)S(1)} %get-tuple-element.178.refs_2_), channel_id=1, source_target_pairs={{0,2},{1,3},{2,0},{3,1},{4,6},{5,7},{6,4},{7,5},{8,10},{9,11},{10,... | collective-permute-start | bytes 1572872 | tf_op jit(solution)/shard_map/gather_u_core0/ppermute | solution.py:561
  49.8 9.2 %collective-permute-start.17 = (bf16[8,4,16,512]{3,2,1,0:T(8,128)(2,1)S(1)}, bf16[8,4,16,512]{3,2,1,0:T(8,128)(2,1)S(1)}, u32[]{:S(2)}, u32[]{:S(2)}) collective-permute-start(bf16[8,4,16,512]{3,2,1,0:T(8,128)(2,1)S(1)} %get-tuple-element.189.refs_6_), channel_id=1, source_target_pairs={{0,2},{1,3},{2,0},{3,1},{4,6},{5,7},{6,4},{7,5},{8,10},{9,11},{10,... | collective-permute-start | bytes 1572872 | tf_op jit(solution)/shard_map/gather_w_core0/ppermute | solution.py:561
  49.8 9.2 %collective-permute-start.18 = (bf16[8,4,16,512]{3,2,1,0:T(8,128)(2,1)S(1)}, bf16[8,4,16,512]{3,2,1,0:T(8,128)(2,1)S(1)}, u32[]{:S(2)}, u32[]{:S(2)}) collective-permute-start(bf16[8,4,16,512]{3,2,1,0:T(8,128)(2,1)S(1)} %collective-permute-done.16.refs_7_), channel_id=1, source_target_pairs={{0,2},{1,3},{2,0},{3,1},{4,6},{5,7},{6,4},{7,5},{8,10},{9,11},{10,... | collective-permute-start | bytes 1572872 | tf_op jit(solution)/shard_map/gather_w_core1/ppermute | solution.py:561
  69.2 15.0 %collective-permute-start.21 = (bf16[8,4,16,512]{3,2,1,0:T(8,128)(2,1)S(1)}, bf16[8,4,16,512]{3,2,1,0:T(8,128)(2,1)S(1)}, u32[]{:S(2)}, u32[]{:S(2)}) collective-permute-start(bf16[8,4,16,512]{3,2,1,0:T(8,128)(2,1)S(1)} %get-tuple-element.204), channel_id=1, source_target_pairs={{0,4},{1,5},{2,3},{3,2},{4,0},{5,1},{6,7},{7,6},{8,12},{9,13},{10,... | collective-permute-start | bytes 1572872 | tf_op jit(solution)/shard_map/scatter_d_hop3/ppermute | solution.py:561
  77.8 9.7 %collective-permute-start.25 = (bf16[16,16,2560]{2,1,0:T(8,128)(2,1)S(1)}, bf16[16,16,2560]{2,1,0:T(8,128)(2,1)S(1)}, u32[]{:S(2)}, u32[]{:S(2)}) collective-permute-start(bf16[16,16,2560]{2,1,0:T(8,128)(2,1)S(1)} %get-tuple-element.237), channel_id=1, source_target_pairs={{0,2},{1,3},{2,0},{3,1},{4,6},{5,7},{6,4},{7,5},{8,10},{9,11},{10,... | collective-permute-start | bytes 3932168 | tf_op jit(solution)/shard_map/scatter_c_core/ppermute | solution.py:561
  78.2 9.2 %collective-permute-start.26 = (bf16[8,4,16,512]{3,2,1,0:T(8,128)(2,1)S(1)}, bf16[8,4,16,512]{3,2,1,0:T(8,128)(2,1)S(1)}, u32[]{:S(2)}, u32[]{:S(2)}) collective-permute-start(bf16[8,4,16,512]{3,2,1,0:T(8,128)(2,1)S(1)} %get-tuple-element.239), channel_id=1, source_target_pairs={{0,4},{1,5},{2,3},{3,2},{4,0},{5,1},{6,7},{7,6},{8,12},{9,13},{10,... | collective-permute-start | bytes 1572872 | tf_op jit(solution)/shard_map/scatter_u_hop3/ppermute | solution.py:561
  87.9 16.3 %collective-permute-start.29 = (bf16[8,16,2560]{2,1,0:T(8,128)(2,1)S(1)}, bf16[8,16,2560]{2,1,0:T(8,128)(2,1)S(1)}, u32[]{:S(2)}, u32[]{:S(2)}) collective-permute-start(bf16[8,16,2560]{2,1,0:T(8,128)(2,1)S(1)} %get-tuple-element.251), channel_id=1, source_target_pairs={{0,4},{1,5},{2,3},{3,2},{4,0},{5,1},{6,7},{7,6},{8,12},{9,13},{10,... | collective-permute-start | bytes 1966088 | tf_op jit(solution)/shard_map/scatter_c_hop3/ppermute | solution.py:561
  89.7 13.4 %collective-permute-start.30 = (bf16[8,16,1664]{2,1,0:T(8,128)(2,1)S(1)}, bf16[8,16,1664]{2,1,0:T(8,128)(2,1)S(1)}, u32[]{:S(2)}, u32[]{:S(2)}) collective-permute-start(bf16[8,16,1664]{2,1,0:T(8,128)(2,1)S(1)} %get-tuple-element.253), channel_id=1, source_target_pairs={{0,4},{1,5},{2,3},{3,2},{4,0},{5,1},{6,7},{7,6},{8,12},{9,13},{10,... | collective-permute-start | bytes 1277960 | tf_op jit(solution)/shard_map/scatter_s_hop3/ppermute | solution.py:561
  90.3 9.1 %collective-permute-start.23 = (bf16[4,4,16,512]{3,2,1,0:T(8,128)(2,1)S(1)}, bf16[4,4,16,512]{3,2,1,0:T(8,128)(2,1)S(1)}, u32[]{:S(2)}, u32[]{:S(2)}) collective-permute-start(bf16[4,4,16,512]{3,2,1,0:T(8,128)(2,1)S(1)} %get-tuple-element.233), channel_id=1, source_target_pairs={{0,16},{1,17},{2,10},{3,11},{4,20},{5,21},{6,14},{7,15},{8,24},{9,... | collective-permute-start | bytes 786440 | tf_op jit(solution)/shard_map/scatter_d_hop2/ppermute | solution.py:561
  92.8 6.7 %collective-permute-start.19 = (bf16[128,512]{1,0:T(8,128)(2,1)S(1)}, bf16[128,512]{1,0:T(8,128)(2,1)S(1)}, u32[]{:S(2)}, u32[]{:S(2)}) collective-permute-start(bf16[128,512]{1,0:T(8,128)(2,1)S(1)} %get-tuple-element.195), channel_id=1, source_target_pairs={{0,1},{1,0},{2,3},{3,2},{4,5},{5,4},{6,7},{7,6},{8,9},{9,8},{10,11... | collective-permute-start | bytes 393224 | tf_op jit(solution)/shard_map/swap_out/ppermute | solution.py:665
  93.3 15.0 %collective-permute-start.28 = (bf16[4,4,16,512]{3,2,1,0:T(8,128)(2,1)S(1)}, bf16[4,4,16,512]{3,2,1,0:T(8,128)(2,1)S(1)}, u32[]{:S(2)}, u32[]{:S(2)}) collective-permute-start(bf16[4,4,16,512]{3,2,1,0:T(8,128)(2,1)S(1)} %get-tuple-element.249), channel_id=1, source_target_pairs={{0,16},{1,17},{2,10},{3,11},{4,20},{5,21},{6,14},{7,15},{8,24},{9,... | collective-permute-start | bytes 786440 | tf_op jit(solution)/shard_map/scatter_u_hop2/ppermute | solution.py:561
  104.4 10.8 %collective-permute-start.32 = (bf16[4,16,2560]{2,1,0:T(8,128)(2,1)S(1)}, bf16[4,16,2560]{2,1,0:T(8,128)(2,1)S(1)}, u32[]{:S(2)}, u32[]{:S(2)}) collective-permute-start(bf16[4,16,2560]{2,1,0:T(8,128)(2,1)S(1)} %get-tuple-element.260), channel_id=1, source_target_pairs={{0,1},{1,0},{2,6},{3,7},{4,5},{5,4},{6,2},{7,3},{8,9},{9,8},{10,14... | collective-permute-start | bytes 983048 | tf_op jit(solution)/shard_map/scatter_c_hop2/ppermute | solution.py:561
  105.6 9.5 %collective-permute-start.33 = (bf16[2,4,16,512]{3,2,1,0:T(8,128)(2,1)S(1)}, bf16[2,4,16,512]{3,2,1,0:T(8,128)(2,1)S(1)}, u32[]{:S(2)}, u32[]{:S(2)}) collective-permute-start(bf16[2,4,16,512]{3,2,1,0:T(8,128)(2,1)S(1)} %get-tuple-element.262), channel_id=1, source_target_pairs={{0,8},{1,9},{2,18},{3,19},{4,12},{5,13},{6,22},{7,23},{8,0},{9,1},... | collective-permute-start | bytes 393224 | tf_op jit(solution)/shard_map/scatter_d_hop1/ppermute | solution.py:561
  107.7 16.9 %collective-permute-start.37 = (bf16[256,512]{1,0:T(8,128)(2,1)S(1)}, bf16[256,512]{1,0:T(8,128)(2,1)S(1)}, u32[]{:S(2)}, u32[]{:S(2)}) collective-permute-start(bf16[256,512]{1,0:T(8,128)(2,1)S(1)} %get-tuple-element.274), channel_id=1, source_target_pairs={{0,1},{1,0},{2,3},{3,2},{4,5},{5,4},{6,7},{7,6},{8,9},{9,8},{10,11... | collective-permute-start | bytes 786440 | tf_op jit(solution)/shard_map/swap_memory/ppermute | solution.py:665
  109.2 11.6 %collective-permute-start.39 = (bf16[2,16,1664]{2,1,0:T(8,128)(2,1)S(1)}, bf16[2,16,1664]{2,1,0:T(8,128)(2,1)S(1)}, u32[]{:S(2)}, u32[]{:S(2)}) collective-permute-start(bf16[2,16,1664]{2,1,0:T(8,128)(2,1)S(1)} %get-tuple-element.278), channel_id=1, source_target_pairs={{0,16},{1,17},{2,10},{3,11},{4,20},{5,21},{6,14},{7,15},{8,24},{9,... | collective-permute-start | bytes 319496 | tf_op jit(solution)/shard_map/scatter_s_hop1/ppermute | solution.py:561
  112.0 7.7 %collective-permute-start.31 = (bf16[2,4,16,512]{3,2,1,0:T(8,128)(2,1)S(1)}, bf16[2,4,16,512]{3,2,1,0:T(8,128)(2,1)S(1)}, u32[]{:S(2)}, u32[]{:S(2)}) collective-permute-start(bf16[2,4,16,512]{3,2,1,0:T(8,128)(2,1)S(1)} %get-tuple-element.258), channel_id=1, source_target_pairs={{0,8},{1,9},{2,18},{3,19},{4,12},{5,13},{6,22},{7,23},{8,0},{9,1},... | collective-permute-start | bytes 393224 | tf_op jit(solution)/shard_map/scatter_u_hop1/ppermute | solution.py:561
  115.2 6.6 %collective-permute-start.38 = (bf16[2,16,2560]{2,1,0:T(8,128)(2,1)S(1)}, bf16[2,16,2560]{2,1,0:T(8,128)(2,1)S(1)}, u32[]{:S(2)}, u32[]{:S(2)}) collective-permute-start(bf16[2,16,2560]{2,1,0:T(8,128)(2,1)S(1)} %get-tuple-element.276), channel_id=1, source_target_pairs={{0,16},{1,17},{2,10},{3,11},{4,20},{5,21},{6,14},{7,15},{8,24},{9,... | collective-permute-start | bytes 491528 | tf_op jit(solution)/shard_map/scatter_c_hop1/ppermute | solution.py:561
  117.7 9.3 %collective-permute-start.27 = (bf16[128,512]{1,0:T(8,128)(2,1)S(1)}, bf16[128,512]{1,0:T(8,128)(2,1)S(1)}, u32[]{:S(2)}, u32[]{:S(2)}) collective-permute-start(bf16[128,512]{1,0:T(8,128)(2,1)S(1)} %get-tuple-element.247), channel_id=1, source_target_pairs={{0,1},{1,0},{2,3},{3,2},{4,5},{5,4},{6,7},{7,6},{8,9},{9,8},{10,11... | collective-permute-start | bytes 393224 | tf_op jit(solution)/shard_map/swap_hidden/ppermute | solution.py:665
  119.7 6.6 %collective-permute-start.36 = (bf16[1,4,16,512]{3,2,1,0:T(8,128)(2,1)S(1)}, bf16[1,4,16,512]{3,2,1,0:T(8,128)(2,1)S(1)}, u32[]{:S(2)}, u32[]{:S(2)}) collective-permute-start(bf16[1,4,16,512]{3,2,1,0:T(8,128)(2,1)S(1)} %get-tuple-element.272), channel_id=1, source_target_pairs={{0,1},{1,0},{2,6},{3,7},{4,5},{5,4},{6,2},{7,3},{8,9},{9,8},{10,14... | collective-permute-start | bytes 196616 | tf_op jit(solution)/shard_map/scatter_d_hop0/ppermute | solution.py:561
  121.9 7.1 %collective-permute-start.40 = (bf16[1,16,2560]{2,1,0:T(8,128)(2,1)S(1)}, bf16[1,16,2560]{2,1,0:T(8,128)(2,1)S(1)}, u32[]{:S(2)}, u32[]{:S(2)}) collective-permute-start(bf16[1,16,2560]{2,1,0:T(8,128)(2,1)S(1)} %get-tuple-element.287), channel_id=1, source_target_pairs={{0,8},{1,9},{2,18},{3,19},{4,12},{5,13},{6,22},{7,23},{8,0},{9,1},... | collective-permute-start | bytes 245768 | tf_op jit(solution)/shard_map/scatter_c_hop0/ppermute | solution.py:561
  (10 other events, 43.7 us)
